TPU v7x, 32 devices: a whole 2x2x4 slice. The times are simulated.
32 devices in a mesh: dp: 4 (over y, core), fsdp: 8 (over z, x).
Axes of the slice: x: 2, y: 2, z: 4, core: 2. Of those that a mesh axis runs over, the one named last changes fastest.
Arguments:
- tokens: bfloat16 [33024, 1024], P(('dp', 'fsdp')), may hold values from -6 to 6
- frame_ids: int32 [33024], P(('dp', 'fsdp')), may hold values from 0 to 3, as said below
- pad_mask: int32 [33024], P(('dp', 'fsdp')), may hold values from 0 to 1, as said below
- episode_offsets: int32 [32, 3], P(('dp', 'fsdp')), may hold values from 0 to 4, as said below
- ln1_gain: bfloat16 [1024], P(('dp', 'fsdp')), may hold values from 0.5 to 1.5
- ln1_bias: bfloat16 [1024], P(('dp', 'fsdp')), may hold values from -4 to 4
- w_qkv: bfloat16 [1024, 3072], P(('dp', 'fsdp')), may hold values from -0.1875 to 0.1875
- b_qkv: bfloat16 [3, 1024], P(None, ('dp', 'fsdp')), may hold values from -4 to 4
- w_out: bfloat16 [1024, 1024], P(('dp', 'fsdp')), may hold values from -0.75 to 0.75
- b_out: bfloat16 [1024], P(('dp', 'fsdp')), may hold values from -4 to 4
- ln2_gain: bfloat16 [1024], P(('dp', 'fsdp')), may hold values from 0.5 to 1.5
- ln2_bias: bfloat16 [1024], P(('dp', 'fsdp')), may hold values from -4 to 4
- w_up: bfloat16 [1024, 4096], P(('dp', 'fsdp')), may hold values from -0.1875 to 0.1875
- b_up: bfloat16 [4096], P(('dp', 'fsdp')), may hold values from -4 to 4
- w_down: bfloat16 [4096, 1024], P(('dp', 'fsdp')), may hold values from -0.09375 to 0.09375
- b_down: bfloat16 [1024], P(('dp', 'fsdp')), may hold values from -4 to 4
- cotangent: bfloat16 [33024, 1024], P(('dp', 'fsdp')), may hold values from -6 to 6
Outputs:
- output: bfloat16 [33024, 1024], P(('dp', 'fsdp'))
- grad_tokens: float32 [33024, 1024], P(('dp', 'fsdp'))
- grad_ln1_gain: float32 [1024], P(('dp', 'fsdp'))
- grad_ln1_bias: float32 [1024], P(('dp', 'fsdp'))
- grad_w_qkv: float32 [1024, 3072], P(('dp', 'fsdp'))
- grad_b_qkv: float32 [3, 1024], P(None, ('dp', 'fsdp'))
- grad_w_out: float32 [1024, 1024], P(('dp', 'fsdp'))
- grad_b_out: float32 [1024], P(('dp', 'fsdp'))
- grad_ln2_gain: float32 [1024], P(('dp', 'fsdp'))
- grad_ln2_bias: float32 [1024], P(('dp', 'fsdp'))
- grad_w_up: float32 [1024, 4096], P(('dp', 'fsdp'))
- grad_b_up: float32 [4096], P(('dp', 'fsdp'))
- grad_w_down: float32 [4096, 1024], P(('dp', 'fsdp'))
- grad_b_down: float32 [1024], P(('dp', 'fsdp'))
Inputs may be any that keep to these rules, and one draw needn't show every extreme that they name: `episode_offsets`: row r holds 0, the frames of the first episode of device r (1 or more), and the frames used by its one or two episodes (at most 4); in every draw some device holds one episode of 4 frames; lengths are heavy-tailed toward short episodes. `frame_ids`: equal over the 258 rows of a frame; counts frames from the start of the frame's episode, and on padding frames from the end of the used ones. `pad_mask`: 1 exactly on the rows of the used frames given by episode_offsets.
All inputs are finite; a program needn't handle non-finite values.
Results may differ from a plain program's by a relative error of at most 0.0073.
Values may be sent and summed in bfloat16 or wider, within the bound.
No kernel may reach another device: no remote copies, remote signals or barrier semaphores. Data moves between devices by JAX's collectives and lax.ppermute only.
A program may use at most 384 MiB of HBM per device.

v0:
```python
import math

import jax
import jax.numpy as jnp
from jax import lax
from jax.sharding import PartitionSpec as P

HEAD = 64
GRID = 16
FRAME_ROWS = 258


eps_norm = 1e-06
part_sizes = (24, 20, 20)
masked_value = -1e30
inv_sqrt_two = 1.0 / math.sqrt(2.0)
inv_sqrt_tau = 1.0 / math.sqrt(2.0 * math.pi)


def rope_tables(frame_ids, rows_count):
    row_index = jnp.arange(rows_count, dtype=jnp.int32) % FRAME_ROWS
    patch_index = jnp.maximum(row_index - 2, 0)
    height = jnp.where(row_index >= 2, patch_index // GRID, 0)
    breadth = jnp.where(row_index >= 2, patch_index % GRID, 0)
    cosine_parts = []
    sine_parts = []
    for position, part_size in zip((frame_ids, height, breadth), part_sizes):
        half_size = part_size // 2
        frequency = 10000.0 ** (-jnp.arange(half_size).astype(jnp.float32) / half_size)
        angles = position.astype(jnp.float32)[:, None] * frequency[None, :]
        cosine_parts.append(jnp.cos(angles))
        sine_parts.append(jnp.sin(angles))
    return (
        jnp.concatenate(cosine_parts, 1)[:, None, :],
        jnp.concatenate(sine_parts, 1)[:, None, :],
    )


def rotate(vectors, cosine, sine_table):
    pieces = []
    offset_at = 0
    slot_at = 0
    for part_size in part_sizes:
        half_size = part_size // 2
        first_half = vectors[..., offset_at : offset_at + half_size]
        second_half = vectors[..., offset_at + half_size : offset_at + part_size]
        cosine_part = cosine[..., slot_at : slot_at + half_size]
        sine_part = sine_table[..., slot_at : slot_at + half_size]
        pieces.append(first_half * cosine_part - second_half * sine_part)
        pieces.append(second_half * cosine_part + first_half * sine_part)
        offset_at = offset_at + part_size
        slot_at = slot_at + half_size
    return jnp.concatenate(pieces, axis=-1)


def normalize(values, gain, bias_add):
    center = values - jnp.mean(values, axis=-1, keepdims=True)
    scale_inv = lax.rsqrt(jnp.mean(center * center, axis=-1, keepdims=True) + eps_norm)
    unit_rows = center * scale_inv
    return (unit_rows * gain + bias_add, unit_rows, scale_inv)


def norm_back(grad_out, unit_rows, scale_inv, gain):
    scaled = grad_out * gain
    mean_grad = jnp.mean(scaled, axis=-1, keepdims=True)
    mean_cross = jnp.mean(scaled * unit_rows, axis=-1, keepdims=True)
    return scale_inv * (scaled - mean_grad - unit_rows * mean_cross)


def visibility(frame_ids, pad_mask, offset_row, query_lo, query_hi, key_hi):
    frame_of = jnp.arange(key_hi, dtype=jnp.int32) // FRAME_ROWS
    episode = (frame_of >= offset_row[1]).astype(jnp.int32) + (frame_of >= offset_row[2]).astype(
        jnp.int32
    )
    same_episode = episode[query_lo:query_hi][:, None] == episode[None, :]
    earlier = frame_ids[None, :key_hi] <= frame_ids[query_lo:query_hi][:, None]
    rows_query = jnp.arange(query_lo, query_hi, dtype=jnp.int32)
    rows_key = jnp.arange(key_hi, dtype=jnp.int32)
    live = (pad_mask[None, :key_hi] > 0) | (rows_query[:, None] == rows_key[None, :])
    return same_episode & earlier & live


def gather_attention(ln1_gain, ln1_bias, w_qkv, b_qkv, w_out, b_out):
    fetched = (
        lax.all_gather(ln1_gain, ("dp", "fsdp"), axis=0, tiled=True),
        lax.all_gather(ln1_bias, ("dp", "fsdp"), axis=0, tiled=True),
        lax.all_gather(w_qkv, ("dp", "fsdp"), axis=0, tiled=True),
        lax.all_gather(b_qkv, ("dp", "fsdp"), axis=1, tiled=True),
        lax.all_gather(w_out, ("dp", "fsdp"), axis=0, tiled=True),
        lax.all_gather(b_out, ("dp", "fsdp"), axis=0, tiled=True),
    )
    return fetched


def gather_feed(ln2_gain, ln2_bias, w_up, b_up, w_down, b_down):
    fetched = (
        lax.all_gather(ln2_gain, ("dp", "fsdp"), axis=0, tiled=True),
        lax.all_gather(ln2_bias, ("dp", "fsdp"), axis=0, tiled=True),
        lax.all_gather(w_up, ("dp", "fsdp"), axis=0, tiled=True),
        lax.all_gather(b_up, ("dp", "fsdp"), axis=0, tiled=True),
        lax.all_gather(w_down, ("dp", "fsdp"), axis=0, tiled=True),
        lax.all_gather(b_down, ("dp", "fsdp"), axis=0, tiled=True),
    )
    return fetched


def reduce_attention(grad_gain, grad_bias, grad_matrix, grad_vector, grad_project, grad_shift):
    summed = (
        lax.psum_scatter(grad_gain, ("dp", "fsdp"), scatter_dimension=0, tiled=True),
        lax.psum_scatter(grad_bias, ("dp", "fsdp"), scatter_dimension=0, tiled=True),
        lax.psum_scatter(grad_matrix, ("dp", "fsdp"), scatter_dimension=0, tiled=True),
        lax.psum_scatter(grad_vector, ("dp", "fsdp"), scatter_dimension=1, tiled=True),
        lax.psum_scatter(grad_project, ("dp", "fsdp"), scatter_dimension=0, tiled=True),
        lax.psum_scatter(grad_shift, ("dp", "fsdp"), scatter_dimension=0, tiled=True),
    )
    return summed


def reduce_feed(grad_gain, grad_bias, grad_matrix, grad_vector, grad_project, grad_shift):
    summed = (
        lax.psum_scatter(grad_gain, ("dp", "fsdp"), scatter_dimension=0, tiled=True),
        lax.psum_scatter(grad_bias, ("dp", "fsdp"), scatter_dimension=0, tiled=True),
        lax.psum_scatter(grad_matrix, ("dp", "fsdp"), scatter_dimension=0, tiled=True),
        lax.psum_scatter(grad_vector, ("dp", "fsdp"), scatter_dimension=0, tiled=True),
        lax.psum_scatter(grad_project, ("dp", "fsdp"), scatter_dimension=0, tiled=True),
        lax.psum_scatter(grad_shift, ("dp", "fsdp"), scatter_dimension=0, tiled=True),
    )
    return summed


def body(
    tokens,
    frame_ids,
    pad_mask,
    episode_offsets,
    ln1_gain,
    ln1_bias,
    w_qkv,
    b_qkv,
    w_out,
    b_out,
    ln2_gain,
    ln2_bias,
    w_up,
    b_up,
    w_down,
    b_down,
    cotangent,
):
    rows_count, width = tokens.shape
    gain_one, bias_one, qkv_matrix, qkv_rows, out_matrix, out_bias = gather_attention(
        ln1_gain, ln1_bias, w_qkv, b_qkv, w_out, b_out
    )
    qkv_bias = qkv_rows.reshape(3 * width)
    heads_count = width // HEAD
    score_scale = 1.0 / math.sqrt(HEAD)
    gain_one_f = gain_one.astype(jnp.float32)
    values_in = tokens.astype(jnp.float32)
    normed_one, unit_one, inv_one = normalize(values_in, gain_one_f, bias_one.astype(jnp.float32))
    normed_one = normed_one.astype(jnp.bfloat16)
    mixed = jnp.dot(normed_one, qkv_matrix, preferred_element_type=jnp.float32) + qkv_bias.astype(
        jnp.float32
    )
    cosine, sine_table = rope_tables(frame_ids, rows_count)
    query = rotate(
        mixed[:, :width].reshape(rows_count, heads_count, HEAD), cosine, sine_table
    ).astype(jnp.bfloat16)
    key_rows = rotate(
        mixed[:, width : 2 * width].reshape(rows_count, heads_count, HEAD), cosine, sine_table
    ).astype(jnp.bfloat16)
    value_rows = mixed[:, 2 * width :].reshape(rows_count, heads_count, HEAD).astype(jnp.bfloat16)
    offset_row = episode_offsets[0]
    block_rows = 2 * FRAME_ROWS
    block_count = rows_count // block_rows
    attended_parts = []
    lse_parts = []
    for block_index in range(block_count):
        query_lo = block_index * block_rows
        query_hi = query_lo + block_rows
        allowed = visibility(frame_ids, pad_mask, offset_row, query_lo, query_hi, query_hi)
        scores = (
            jnp.einsum(
                "qhd,khd->hqk",
                query[query_lo:query_hi],
                key_rows[:query_hi],
                preferred_element_type=jnp.float32,
            )
            * score_scale
        )
        scores = jnp.where(allowed[None], scores, masked_value)
        top_score = jnp.max(scores, axis=-1, keepdims=True)
        exponent = jnp.exp(scores - top_score)
        row_total = jnp.sum(exponent, axis=-1, keepdims=True)
        probability = (exponent / row_total).astype(jnp.bfloat16)
        attended_parts.append(
            jnp.einsum(
                "hqk,khd->qhd",
                probability,
                value_rows[:query_hi],
                preferred_element_type=jnp.float32,
            )
        )
        lse_parts.append(top_score + jnp.log(row_total))
    attended = (
        jnp.concatenate(attended_parts, axis=0).reshape(rows_count, width).astype(jnp.bfloat16)
    )
    middle = (
        values_in
        + jnp.dot(attended, out_matrix, preferred_element_type=jnp.float32)
        + out_bias.astype(jnp.float32)
    )
    gain_two, bias_two, up_matrix, up_bias, down_matrix, down_bias = gather_feed(
        ln2_gain, ln2_bias, w_up, b_up, w_down, b_down
    )
    gain_two_f = gain_two.astype(jnp.float32)
    normed_two, unit_two, inv_two = normalize(middle, gain_two_f, bias_two.astype(jnp.float32))
    normed_two = normed_two.astype(jnp.bfloat16)
    upward = jnp.dot(normed_two, up_matrix, preferred_element_type=jnp.float32) + up_bias.astype(
        jnp.float32
    )
    activated = jax.nn.gelu(upward, approximate=False).astype(jnp.bfloat16)
    result_rows = (
        middle
        + jnp.dot(activated, down_matrix, preferred_element_type=jnp.float32)
        + down_bias.astype(jnp.float32)
    )
    output = result_rows.astype(jnp.bfloat16)
    grad_b_down_local = jnp.sum(cotangent.astype(jnp.float32), axis=0)
    grad_w_down_local = jnp.einsum(
        "tf,td->fd", activated, cotangent, preferred_element_type=jnp.float32
    )
    grad_activated = jnp.einsum(
        "td,fd->tf", cotangent, down_matrix, preferred_element_type=jnp.float32
    )
    cdf_part = 0.5 * (1.0 + lax.erf(upward * inv_sqrt_two))
    pdf_part = jnp.exp(-0.5 * upward * upward) * inv_sqrt_tau
    grad_up = (grad_activated * (cdf_part + upward * pdf_part)).astype(jnp.bfloat16)
    grad_b_up_local = jnp.sum(grad_up.astype(jnp.float32), axis=0)
    grad_w_up_local = jnp.einsum(
        "td,tf->df", normed_two, grad_up, preferred_element_type=jnp.float32
    )
    grad_normed_two = jnp.einsum(
        "tf,df->td", grad_up, up_matrix, preferred_element_type=jnp.float32
    )
    grad_gain_two = jnp.sum(grad_normed_two * unit_two, axis=0)
    grad_bias_two = jnp.sum(grad_normed_two, axis=0)
    feed_sums = reduce_feed(
        grad_gain_two,
        grad_bias_two,
        grad_w_up_local,
        grad_b_up_local,
        grad_w_down_local,
        grad_b_down_local,
    )
    grad_middle = cotangent.astype(jnp.float32) + norm_back(
        grad_normed_two, unit_two, inv_two, gain_two_f
    )
    grad_branch = grad_middle.astype(jnp.bfloat16)
    grad_b_out_local = jnp.sum(grad_branch.astype(jnp.float32), axis=0)
    grad_w_out_local = jnp.einsum(
        "te,td->ed", attended, grad_branch, preferred_element_type=jnp.float32
    )
    grad_attended = jnp.einsum(
        "td,ed->te", grad_branch, out_matrix, preferred_element_type=jnp.float32
    )
    grad_attended = grad_attended.astype(jnp.bfloat16).reshape(rows_count, heads_count, HEAD)
    grad_query_parts = []
    grad_key = jnp.zeros((rows_count, heads_count, HEAD), jnp.float32)
    grad_value = jnp.zeros((rows_count, heads_count, HEAD), jnp.float32)
    for block_index in range(block_count):
        query_lo = block_index * block_rows
        query_hi = query_lo + block_rows
        allowed = visibility(frame_ids, pad_mask, offset_row, query_lo, query_hi, query_hi)
        query_block = query[query_lo:query_hi]
        key_block = key_rows[:query_hi]
        grad_block = grad_attended[query_lo:query_hi]
        scores = (
            jnp.einsum("qhd,khd->hqk", query_block, key_block, preferred_element_type=jnp.float32)
            * score_scale
        )
        scores = jnp.where(allowed[None], scores, masked_value)
        probs_back = jnp.exp(scores - lse_parts[block_index])
        grad_probs = jnp.einsum(
            "qhd,khd->hqk", grad_block, value_rows[:query_hi], preferred_element_type=jnp.float32
        )
        row_delta = jnp.sum(grad_probs * probs_back, axis=-1, keepdims=True)
        grad_scores = (probs_back * (grad_probs - row_delta)).astype(jnp.bfloat16)
        grad_query_parts.append(
            jnp.einsum("hqk,khd->qhd", grad_scores, key_block, preferred_element_type=jnp.float32)
            * score_scale
        )
        grad_key = grad_key.at[:query_hi].add(
            jnp.einsum("hqk,qhd->khd", grad_scores, query_block, preferred_element_type=jnp.float32)
            * score_scale
        )
        grad_value = grad_value.at[:query_hi].add(
            jnp.einsum(
                "hqk,qhd->khd",
                probs_back.astype(jnp.bfloat16),
                grad_block,
                preferred_element_type=jnp.float32,
            )
        )
    grad_query = jnp.concatenate(grad_query_parts, axis=0)
    negative_sine = -sine_table
    grad_mixed = jnp.concatenate(
        [
            rotate(grad_query, cosine, negative_sine).reshape(rows_count, width),
            rotate(grad_key, cosine, negative_sine).reshape(rows_count, width),
            grad_value.reshape(rows_count, width),
        ],
        axis=1,
    ).astype(jnp.bfloat16)
    grad_b_qkv_local = jnp.sum(grad_mixed.astype(jnp.float32), axis=0).reshape(3, width)
    grad_w_qkv_local = jnp.einsum(
        "td,tm->dm", normed_one, grad_mixed, preferred_element_type=jnp.float32
    )
    grad_normed_one = jnp.einsum(
        "tm,dm->td", grad_mixed, qkv_matrix, preferred_element_type=jnp.float32
    )
    grad_gain_one = jnp.sum(grad_normed_one * unit_one, axis=0)
    grad_bias_one = jnp.sum(grad_normed_one, axis=0)
    attn_sums = reduce_attention(
        grad_gain_one,
        grad_bias_one,
        grad_w_qkv_local,
        grad_b_qkv_local,
        grad_w_out_local,
        grad_b_out_local,
    )
    grad_tokens = grad_middle + norm_back(grad_normed_one, unit_one, inv_one, gain_one_f)
    return (
        output,
        grad_tokens,
        attn_sums[0],
        attn_sums[1],
        attn_sums[2],
        attn_sums[3],
        attn_sums[4],
        attn_sums[5],
        feed_sums[0],
        feed_sums[1],
        feed_sums[2],
        feed_sums[3],
        feed_sums[4],
        feed_sums[5],
    )


def solution(mesh):
    placed = (
        P(("dp", "fsdp"), None),
        P(("dp", "fsdp")),
        P(("dp", "fsdp")),
        P(("dp", "fsdp"), None),
        P(("dp", "fsdp")),
        P(("dp", "fsdp")),
        P(("dp", "fsdp"), None),
        P(None, ("dp", "fsdp")),
        P(("dp", "fsdp"), None),
        P(("dp", "fsdp")),
        P(("dp", "fsdp")),
        P(("dp", "fsdp")),
        P(("dp", "fsdp"), None),
        P(("dp", "fsdp")),
        P(("dp", "fsdp"), None),
        P(("dp", "fsdp")),
        P(("dp", "fsdp"), None),
    )
    return jax.shard_map(
        body,
        mesh=mesh,
        in_specs=placed,
        out_specs=(
            P(("dp", "fsdp"), None),
            P(("dp", "fsdp"), None),
            P(("dp", "fsdp")),
            P(("dp", "fsdp")),
            P(("dp", "fsdp"), None),
            P(None, ("dp", "fsdp")),
            P(("dp", "fsdp"), None),
            P(("dp", "fsdp")),
            P(("dp", "fsdp")),
            P(("dp", "fsdp")),
            P(("dp", "fsdp"), None),
            P(("dp", "fsdp")),
            P(("dp", "fsdp"), None),
            P(("dp", "fsdp")),
        ),
        check_vma=False,
    )
```

profile of v0, /device:TPU:1, one launch (start us, length us, event | category | flops | bytes accessed | tf_op | source)
XLA Modules:
  0.0 1909.0 jit_solution(17772351758718620704)
XLA Ops:
  25.7 42.5 %all-reduce.16 = (bf16[1024]{0:T(1024)(128)(2,1)S(1)}, bf16[1024]{0:T(1024)(128)(2,1)S(1)}, bf16[1024]{0:T(1024)(128)(2,1)S(1)}, bf16[1024]{0:T(1024)(128)(2,1)S...) all-reduce(bf16[1024]{0:T(1024)(128)(2,1)S(1)} %dynamic-update-slic, ...), channel_id=1, replica_groups=mesh['dp'=4,'fsdp'=8] {'dp','fsdp'}, use_global_device_ids=true, to_apply=%add.3 | all-reduce | flops 6144 | bytes 24576
  71.3 59.7 %all-gather.1 = bf16[32,1,128]{2,1,0:T(2,128)(2,1)S(1)} all-gather(bf16[1,1,128]{2,1,0:T(2,128)(2,1)S(1)} %bitcast.128), channel_id=1, replica_groups=mesh['dp'=4,'fsdp'=8] {'dp','fsdp'}, dimensions={0}, use_global_device_ids=true | all-gather | bytes 8448 | tf_op jit(solution)/shard_map/all_gather | solution.py:100
  131.6 61.7 %all-gather = bf16[32,32,3]{1,2,0:T(4,128)(2,1)S(1)} all-gather(bf16[1,32,3]{1,2,0:T(4,128)(2,1)S(1)} %bitcast.127), channel_id=1, replica_groups=mesh['dp'=4,'fsdp'=8] {'dp','fsdp'}, dimensions={0}, use_global_device_ids=true | all-gather | bytes 6336 | tf_op jit(solution)/shard_map/all_gather | solution.py:88
  195.6 9.9 fusion.102
  236.7 36.8 %concatenate.59 = bf16[1032,16,64]{0,2,1:T(8,128)(2,1)S(1)} concatenate(bf16[1032,16,12]{0,2,1:T(8,128)(2,1)} %get-tuple-element.144, bf16[1032,16,12]{0,2,1:T(8,128)(2,1)} %get-tuple-element.145, bf16[1032,16,10]{0,2,1:T(8,128)(2,1)} %get-tuple-element.132, bf16[1032,16,10]{0,2,1:T(8,128)(2,1)} %get-tuple-element.133, bf16[1032,16,10]{0,2,1:T(8,128)(2,1)} %get-tuple-element.123, ...), dimensions={2} | concatenate | bytes 4227072 | tf_op jit(solution)/shard_map/concatenate | solution.py:53
  273.5 42.6 %concatenate.58 = bf16[1032,16,64]{0,2,1:T(8,128)(2,1)} concatenate(bf16[1032,16,12]{0,2,1:T(8,128)(2,1)} %get-tuple-element.121, bf16[1032,16,12]{0,2,1:T(8,128)(2,1)} %get-tuple-element.120, bf16[1032,16,10]{0,2,1:T(8,128)(2,1)} %get-tuple-element.130, bf16[1032,16,10]{0,2,1:T(8,128)(2,1)} %get-tuple-element.131, bf16[1032,16,10]{0,2,1:T(8,128)(2,1)} %get-tuple-element.117, ...), dimensions={2} | concatenate | bytes 4227072 | tf_op jit(solution)/shard_map/concatenate | solution.py:53
  316.1 12.3 fusion.104
  328.4 17.2 fusion.103
  354.7 15.2 fusion
  369.9 14.4 fusion.55
  404.9 50.3 %fusion.9 = (bf16[1032,4096]{1,0:T(8,128)(2,1)}, f32[1032,4096]{1,0:T(8,128)}) fusion(f32[4096]{0:T(1024)S(1)} %bitcast.126, bf16[1024,4096]{1,0:T(8,128)(2,1)} %all-gather.11.cloned.1.call-done, f32[1032,1024]{1,0:T(8,128)} %copy-done.8, f32[1024]{0:T(1024)S(1)} %copy-done.50, f32[1024]{0:T(1024)S(1)} %copy-done.44, f32[1032]{0:T(1024)S(1)} %add_rsqrt_fusion, ...), kind=kOutput, calls=%fused_computation.24 | convolution fusion | flops 8941314048 | bytes 38010944 | tf_op jit(solution)/shard_map/dot_general | solution.py:218
  455.3 19.1 %convert_reduce_fusion = (f32[4096]{0:T(1024)}, bf16[1032,4096]{1,0:T(8,128)(2,1)}) fusion(f32[1032,4096]{1,0:T(8,128)} %get-tuple-element.175, bf16[1032,1024]{1,0:T(8,128)(2,1)S(1)} %copy-done.17, bf16[4096,1024]{1,0:T(8,128)(2,1)} %all-gather.13.cloned.1.call-done), kind=kOutput, calls=%fused_computation.29 | convolution fusion | flops 8707764224 | bytes 35880960 | tf_op jit(solution)/shard_map/td,fd->tf/dot_general | solution.py:232
  474.4 16.6 multiply_reduce_fusion.2
  498.4 12.2 fusion.49
  510.6 13.7 multiply_reduce_fusion.1
  524.4 14.6 multiply_convert_fusion.1
  550.7 25.8 %multiply_reduce_fusion = (f32[16,516]{1,0:T(8,128)S(1)}, f32[16,516,1032]{2,1,0:T(8,128)}) fusion(f32[16,516,1032]{2,1,0:T(8,128)} %get-tuple-element.169, f32[16,516]{1,0:T(8,128)S(1)} %copy-done.16, bf16[516,16,64]{0,2,1:T(8,128)(2,1)} %bitcast.104, bf16[1032,16,64]{0,2,1:T(8,128)(2,1)} %bitcast.109), kind=kOutput, calls=%fused_computation.1 | convolution fusion | flops 1116136960 | bytes 71397888 | tf_op jit(solution)/shard_map/qhd,khd->hqk/dot_general | solution.py:283
  576.5 18.3 fusion.33
  594.8 31.2 %multiply_convert_fusion = bf16[16,516,1032]{2,1,0:T(8,128)(2,1)} fusion(f32[16,516,1032]{2,1,0:T(8,128)} %get-tuple-element.178, f32[16,516,1032]{2,1,0:T(8,128)} %get-tuple-element.169, f32[16,516]{1,0:T(8,128)S(1)} %get-tuple-element.177, f32[16,516]{1,0:T(8,128)S(1)} %copy-done.16), kind=kLoop, calls=%fused_computation | loop fusion | flops 34080768 | bytes 85267968 | tf_op jit(solution)/shard_map/convert_element_type | solution.py:287
  626.0 10.3 multiply_bitcast_fusion.1
  651.3 39.5 %concatenate.67 = bf16[1032,16,64]{0,2,1:T(8,128)(2,1)} concatenate(bf16[1032,16,12]{0,2,1:T(8,128)(2,1)S(1)} %get-tuple-element.140, bf16[1032,16,12]{0,2,1:T(8,128)(2,1)S(1)} %get-tuple-element.141, bf16[1032,16,10]{0,2,1:T(8,128)(2,1)} %get-tuple-element.128, bf16[1032,16,10]{0,2,1:T(8,128)(2,1)} %get-tuple-element.129, bf16[1032,16,10]{0,2,1:T(8,128)(2,1)S(1)} %get-tuple-element.111, ...), dimensions={2} | concatenate | bytes 4227072 | tf_op jit(solution)/shard_map/concatenate | solution.py:53
  690.8 41.8 %concatenate.66 = bf16[1032,16,64]{0,2,1:T(8,128)(2,1)} concatenate(bf16[1032,16,12]{0,2,1:T(8,128)(2,1)} %get-tuple-element.108, bf16[1032,16,12]{0,2,1:T(8,128)(2,1)S(1)} %get-tuple-element.107, bf16[1032,16,10]{0,2,1:T(8,128)(2,1)} %get-tuple-element.138, bf16[1032,16,10]{0,2,1:T(8,128)(2,1)} %get-tuple-element.139, bf16[1032,16,10]{0,2,1:T(8,128)(2,1)} %get-tuple-element.137, ...), dimensions={2} | concatenate | bytes 4227072 | tf_op jit(solution)/shard_map/concatenate | solution.py:53
  745.7 16.3 fusion.93
  762.7 19.1 %fusion.97 = f32[1024,4096]{1,0:T(8,128)} fusion(bf16[1032,4096]{1,0:T(8,128)(2,1)} %get-tuple-element.183, f32[1032,1024]{1,0:T(8,128)} %copy-done.8, f32[1024]{0:T(1024)S(1)} %copy-done.51, f32[1024]{0:T(1024)S(1)} %copy-done.45, f32[1032]{0:T(1024)S(1)} %copy-done.39, f32[1032]{0:T(1024)S(1)} %copy-done.34), kind=kOutput, calls=%fused_computation.225 | convolution fusion | flops 8662327296 | bytes 29474880 | tf_op jit(solution)/shard_map/td,tf->df/dot_general | solution.py:239
  781.9 18.0 fusion.106
  800.6 14.2 fusion.44
  814.8 47.2 %all-reduce.15 = (f32[1024]{0:T(1024)S(1)}, f32[1024]{0:T(1024)S(1)}, f32[1024]{0:T(1024)S(1)}, f32[1024]{0:T(1024)S(1)}, f32[1024]{0:T(1024)S(1)}, /*index=5*/f32[4096]{0:T(1024)S(1)}, f32[1024]{0:T(1024)S(1)}) all-reduce(f32[1024]{0:T(1024)S(1)} %get-tuple-element.80, ...), channel_id=2, replica_groups=mesh['dp'=4,'fsdp'=8] {'dp','fsdp'}, use_global_device_ids=true, to_apply=%region_15.16.clone | all-reduce | flops 10240 | bytes 81920
  872.2 15.6 fusion.46
  889.1 124.4 %reduce-scatter.10.cloned.1.call-done = f32[32,1024]{1,0:T(8,128)} async-done(((f32[1024,1024]{1,0:T(8,128)}), f32[32,1024]{1,0:T(8,128)}) %reduce-scatter.10.cloned.1.call-update) | async-done | bytes 131088 | tf_op jit(solution)/shard_map/reduce_scatter | solution.py:113
  1013.5 167.8 %reduce-scatter.8.cloned.1.call-done = f32[32,3072]{1,0:T(8,128)} async-done(((f32[1024,3072]{1,0:T(8,128)}), f32[32,3072]{1,0:T(8,128)}) %reduce-scatter.8.cloned.1.call-update) | async-done | bytes 393232 | tf_op jit(solution)/shard_map/reduce_scatter | solution.py:111
  1181.3 360.7 %reduce-scatter.12.cloned.1.call-done = f32[32,4096]{1,0:T(8,128)} async-done(((f32[1024,4096]{1,0:T(8,128)}), f32[32,4096]{1,0:T(8,128)}) %reduce-scatter.12.cloned.1.call-update) | async-done | bytes 524304 | tf_op jit(solution)/shard_map/reduce_scatter | solution.py:123
  1542.0 360.2 %reduce-scatter.14.cloned.1.call-done = f32[128,1024]{1,0:T(8,128)} async-done(((f32[4096,1024]{1,0:T(8,128)}), f32[128,1024]{1,0:T(8,128)}) %reduce-scatter.14.cloned.1.call-update) | async-done | bytes 524304 | tf_op jit(solution)/shard_map/reduce_scatter | solution.py:125
  (243 shorter events, 144.6 us)
Async XLA Ops:
  7.2 63.0 %copy-start.6 = (bf16[1032,1024]{1,0:T(8,128)(2,1)S(1)}, bf16[1032,1024]{1,0:T(8,128)(2,1)}, u32[]{:S(2)}) copy-start(bf16[1032,1024]{1,0:T(8,128)(2,1)} %param.29) | copy-start | bytes 6340612
  7.2 64.1 %copy-start.57 = (bf16[128]{0:T(256)(128)(2,1)S(1)}, bf16[128]{0:T(256)(128)(2,1)}, u32[]{:S(2)}) copy-start(bf16[128]{0:T(256)(128)(2,1)} %param.42) | copy-start | bytes 772
  7.2 124.4 %copy-start.56 = (bf16[3,32]{1,0:T(4,128)(2,1)S(1)}, bf16[3,32]{1,0:T(4,128)(2,1)}, u32[]{:S(2)}) copy-start(bf16[3,32]{1,0:T(4,128)(2,1)} %param.36) | copy-start | bytes 580
  7.2 188.3 %all-gather.7.cloned.1.call-start = ((), (), s32[]{:S(2)}) async-start(), calls=%async_computation.5 | async-start | bytes 6488064 | tf_op jit(solution)/shard_map/all_gather | solution.py:87
  7.9 387.9 %all-gather.9.cloned.1.call-start = ((), (), s32[]{:S(2)}) async-start(), calls=%async_computation.6 | async-start | bytes 2162688 | tf_op jit(solution)/shard_map/all_gather | solution.py:89
  8.7 396.2 %all-gather.11.cloned.1.call-start = ((), (), s32[]{:S(2)}) async-start(), calls=%async_computation.7 | async-start | bytes 8650752 | tf_op jit(solution)/shard_map/all_gather | solution.py:99
  9.4 185.1 %copy-start.35 = (s32[1032]{0:T(1024)S(1)}, s32[1032]{0:T(1024)}, u32[]{:S(2)}) copy-start(s32[1032]{0:T(1024)} %param.30) | copy-start | bytes 12388
  9.4 445.8 %all-gather.13.cloned.1.call-start = ((), (), s32[]{:S(2)}) async-start(), calls=%async_computation.8 | async-start | bytes 8650752 | tf_op jit(solution)/shard_map/all_gather | solution.py:101
  10.0 877.8 %reduce-scatter.16.cloned.1.call-start = ((), (), s32[]{:S(2)}) async-start(), calls=%async_computation.13 | async-start | bytes 540672
  19.4 215.2 %copy-start.22 = (f32[1032,12]{0,1:T(8,128)}, f32[1032,12]{0,1:T(8,128)S(1)}, u32[]{:S(2)}) copy-start(f32[1032,12]{0,1:T(8,128)S(1)} %slice_bitcast_fusion.8) | copy-start | bytes 148612
  19.4 212.9 %copy-start.18 = (f32[1032,10]{0,1:T(8,128)}, f32[1032,10]{0,1:T(8,128)S(1)}, u32[]{:S(2)}) copy-start(f32[1032,10]{0,1:T(8,128)S(1)} %get-tuple-element.146) | copy-start | bytes 123844
  19.4 212.8 %copy-start.20 = (f32[1032,10]{0,1:T(8,128)}, f32[1032,10]{0,1:T(8,128)S(1)}, u32[]{:S(2)}) copy-start(f32[1032,10]{0,1:T(8,128)S(1)} %get-tuple-element.147) | copy-start | bytes 123844
  68.3 137.2 %copy-start.52 = (f32[1024]{0:T(1024)}, f32[1024]{0:T(1024)S(1)}, u32[]{:S(2)}) copy-start(f32[1024]{0:T(1024)S(1)} %convert_element_type.189) | copy-start | bytes 12292
  68.3 137.2 %copy-start.42 = (f32[1024]{0:T(1024)}, f32[1024]{0:T(1024)S(1)}, u32[]{:S(2)}) copy-start(f32[1024]{0:T(1024)S(1)} %convert_element_type.188) | copy-start | bytes 12292
  70.5 135.0 %copy-start.31 = (f32[1032]{0:T(1024)}, f32[1032]{0:T(1024)S(1)}, u32[]{:S(2)}) copy-start(f32[1032]{0:T(1024)S(1)} %broadcast_multiply_fusion.5) | copy-start | bytes 12388
  71.2 134.3 %copy-start.36 = (f32[1032]{0:T(1024)}, f32[1032]{0:T(1024)S(1)}, u32[]{:S(2)}) copy-start(f32[1032]{0:T(1024)S(1)} %add_rsqrt_fusion.1) | copy-start | bytes 12388
  273.4 54.9 %copy-start = (bf16[1032,16,64]{0,2,1:T(8,128)(2,1)}, bf16[1032,16,64]{0,2,1:T(8,128)(2,1)S(1)}, u32[]{:S(2)}) copy-start(bf16[1032,16,64]{0,2,1:T(8,128)(2,1)S(1)} %concatenate.59) | copy-start | bytes 6340612
  354.7 15.2 copy-start.11
  369.9 14.5 copy-start.13
  401.0 90.0 %copy-start.33 = (f32[1032]{0:T(1024)}, f32[1032]{0:T(1024)S(1)}, u32[]{:S(2)}) copy-start(f32[1032]{0:T(1024)S(1)} %broadcast_multiply_fusion.4) | copy-start | bytes 12388
  403.6 87.4 %copy-start.38 = (f32[1032]{0:T(1024)}, f32[1032]{0:T(1024)S(1)}, u32[]{:S(2)}) copy-start(f32[1032]{0:T(1024)S(1)} %add_rsqrt_fusion) | copy-start | bytes 12388
  404.9 50.3 %copy-start.17 = (bf16[1032,1024]{1,0:T(8,128)(2,1)S(1)}, bf16[1032,1024]{1,0:T(8,128)(2,1)}, u32[]{:S(2)}) copy-start(bf16[1032,1024]{1,0:T(8,128)(2,1)} %param.45) | copy-start | bytes 6340612
  455.3 19.2 %copy-start.9 = (f32[1032,1024]{1,0:T(8,128)S(1)}, f32[1032,1024]{1,0:T(8,128)}, u32[]{:S(2)}) copy-start(f32[1032,1024]{1,0:T(8,128)} %copy-done.8) | copy-start | bytes 12681220
  524.4 14.6 copy-start.1
  690.8 41.9 %copy-start.5 = (bf16[1032,16,64]{0,2,1:T(8,128)(2,1)S(1)}, bf16[1032,16,64]{0,2,1:T(8,128)(2,1)}, u32[]{:S(2)}) copy-start(bf16[1032,16,64]{0,2,1:T(8,128)(2,1)} %fusion.33) | copy-start | bytes 6340612
  737.8 275.7 %reduce-scatter.10.cloned.1.call-start = ((), (), s32[]{:S(2)}) async-start(), calls=%async_computation.10 | async-start | bytes 4325376 | tf_op jit(solution)/shard_map/reduce_scatter | solution.py:113
  745.6 435.7 %reduce-scatter.8.cloned.1.call-start = ((), (), s32[]{:S(2)}) async-start(), calls=%async_computation.9 | async-start | bytes 12976128 | tf_op jit(solution)/shard_map/reduce_scatter | solution.py:111
  762.0 780.0 %reduce-scatter.12.cloned.1.call-start = ((), (), s32[]{:S(2)}) async-start(), calls=%async_computation.11 | async-start | bytes 17301504 | tf_op jit(solution)/shard_map/reduce_scatter | solution.py:123
  781.8 1120.4 %reduce-scatter.14.cloned.1.call-start = ((), (), s32[]{:S(2)}) async-start(), calls=%async_computation.12 | async-start | bytes 17301504 | tf_op jit(solution)/shard_map/reduce_scatter | solution.py:125
  800.5 14.2 copy-start.46
  800.5 14.2 copy-start.48
  800.5 14.2 copy-start.49
  (38 other events, 207.6 us)
Sparse Core Ops, SparseCore 0:
  11.0 72.8 all-gather.6
  86.8 55.0 all-gather.8
  144.9 76.3 all-gather.10
  224.2 76.0 all-gather.12
  737.8 132.7 reduce-scatter.15
  873.4 140.0 reduce-scatter.9
  1021.1 160.1 reduce-scatter.7
  1184.2 357.8 reduce-scatter.11
  1544.9 357.2 reduce-scatter.13
where the time goes:
time: 1930 us; the launch traced here: 1910 us
  waiting for transfers between devices  1020 us (53%)
  matrix products  347 us (18%)
  blocking collectives  211 us (11%)
  local copies, waits for them, and re-layouts  206 us (11%)
  other arithmetic  114 us (6%)
    reduce_scatter x1, waiting for transfers between devices, reduce_feed(): lax.psum_scatter(grad_matrix, ('dp', 'fsdp'), scatter_dimension=0, tiled=...  361 us
    reduce_scatter x1, waiting for transfers between devices, reduce_feed(): lax.psum_scatter(grad_project, ('dp', 'fsdp'), scatter_dimension=0, tiled...  360 us
    reduce_scatter x1, waiting for transfers between devices, reduce_attention(): lax.psum_scatter(grad_matrix, ('dp', 'fsdp'), scatter_dimension=0, tiled=...  168 us
    concatenate x4, local copies, waits for them, and re-layouts, rotate(): return jnp.concatenate(pieces, axis=-1)  161 us
    reduce_scatter x1, waiting for transfers between devices, reduce_attention(): lax.psum_scatter(grad_project, ('dp', 'fsdp'), scatter_dimension=0, tiled...  124 us
    unnamed x2, blocking collectives  89.7 us
    all_gather x1, blocking collectives, gather_attention(): lax.all_gather(b_qkv, ('dp', 'fsdp'), axis=1, tiled=True)  61.7 us
    all_gather x1, blocking collectives, gather_feed(): lax.all_gather(b_up, ('dp', 'fsdp'), axis=0, tiled=True)  59.7 us
  transfers between devices with their start and end apart: 9, of which 4 were waited for; matrix products, arithmetic and copies ran while one was open for 20% of the time, Pallas kernels for 0%

commit v1 on v0

v1 whole, which is shorter than its diff:
```python
import functools
import math

import jax
import jax.numpy as jnp
import numpy as np
from jax import lax
from jax.experimental import pallas as pl
from jax.experimental.pallas import tpu as pltpu
from jax.sharding import PartitionSpec as P

HEAD = 64
GRID = 16
FRAME_ROWS = 258
FRAMES = 4
PATCH = GRID * GRID
EXTRA = 16
FEW = 8
BODY = FRAMES * PATCH
ROWS = BODY + EXTRA
eps_norm = 1e-06
part_sizes = (24, 20, 20)
masked_value = -1e30
inv_sqrt_two = 1.0 / math.sqrt(2.0)
inv_sqrt_tau = 1.0 / math.sqrt(2.0 * math.pi)
f32 = jnp.float32
bf16 = jnp.bfloat16
vmem_most = 60 * 1024 * 1024


def log2(n):
    return n.bit_length() - 1


def swap(value, bit, sizes):
    count = sizes[0] * sizes[1]
    pairs = [(i, i ^ (1 << bit)) for i in range(count)]
    return lax.ppermute(value, ("dp", "fsdp"), pairs)


def bit_orders(sizes):
    inner, outer = log2(sizes[1]), log2(sizes[0])
    core = inner
    line = list(range(1, inner))
    cross = [0]
    other = list(range(inner + 1, inner + outer))
    return core, line + cross + other, line + other + cross


def gather_pieces(shard, order, core, sizes):
    held = shard[None]
    rel = [0]
    for bit in order[:-1]:
        held = jnp.concatenate([held, swap(held, bit, sizes)], axis=0)
        rel = rel + [p | (1 << bit) for p in rel]
    last = order[-1]
    pieces = [(held, rel), (swap(held, last, sizes), [p | (1 << last) for p in rel])]
    pieces += [(swap(v, core, sizes), [p | (1 << core) for p in q]) for v, q in pieces]
    return pieces


def assemble_kernel(rels, rows, me_ref, *refs):
    pieces, out, sem = refs[: len(rels)], refs[len(rels)], refs[len(rels) + 1]
    me = me_ref[0]
    copies = []
    for piece, rel in zip(pieces, rels):
        for at, p in enumerate(rel):
            owner = lax.bitwise_xor(me, p)
            start = pl.multiple_of(owner * rows, rows)
            copies.append(pltpu.make_async_copy(piece.at[at], out.at[pl.ds(start, rows)], sem))
    for copy in copies:
        copy.start()
    pltpu.make_async_copy(out, out, sem).wait()


def assemble(pieces, me):
    rels = [q for _, q in pieces]
    count = sum(len(q) for q in rels)
    _, rows, cols = pieces[0][0].shape
    return pl.pallas_call(
        functools.partial(assemble_kernel, rels, rows),
        out_shape=jax.ShapeDtypeStruct((count * rows, cols), pieces[0][0].dtype),
        in_specs=[pl.BlockSpec(memory_space=pltpu.SMEM)]
        + [pl.BlockSpec(memory_space=pl.ANY)] * len(pieces),
        scratch_shapes=[pltpu.SemaphoreType.DMA],
        compiler_params=pltpu.CompilerParams(vmem_limit_bytes=vmem_most),
        cost_estimate=pl.CostEstimate(
            flops=0, bytes_accessed=4 * count * rows * cols, transcendentals=0
        ),
    )(me, *[v for v, _ in pieces])


def split_kernel(rels, rows, me_ref, whole, *refs):
    outs, sem = refs[: len(rels)], refs[len(rels)]
    me = me_ref[0]
    copies = []
    for piece, rel in zip(outs, rels):
        for at, p in enumerate(rel):
            owner = lax.bitwise_xor(me, p)
            start = pl.multiple_of(owner * rows, rows)
            copies.append(pltpu.make_async_copy(whole.at[pl.ds(start, rows)], piece.at[at], sem))
    for copy in copies:
        copy.start()
    pltpu.make_async_copy(whole, whole, sem).wait()


def relatives(order, core):
    rel = [0]
    for bit in order:
        rel = rel + [p | (1 << bit) for p in rel]
    return rel, [p | (1 << core) for p in rel]


def split(whole, order, core, me):
    own, other = relatives(order, core)
    rows = whole.shape[0] // (2 * len(own))
    return pl.pallas_call(
        functools.partial(split_kernel, (own, other), rows),
        out_shape=(jax.ShapeDtypeStruct((len(own), rows, whole.shape[1]), whole.dtype),) * 2,
        in_specs=[
            pl.BlockSpec(memory_space=pltpu.SMEM),
            pl.BlockSpec(memory_space=pltpu.VMEM),
        ],
        out_specs=(pl.BlockSpec(memory_space=pl.ANY),) * 2,
        scratch_shapes=[pltpu.SemaphoreType.DMA],
        compiler_params=pltpu.CompilerParams(vmem_limit_bytes=vmem_most),
        cost_estimate=pl.CostEstimate(flops=0, bytes_accessed=4 * whole.size, transcendentals=0),
    )(me, whole)


def reduce_pieces(own, other, order, core, sizes):
    kind = own.dtype
    taken = swap(other, core, sizes)
    kept = own
    for bit in reversed(order):
        half = kept.shape[0] // 2
        total = kept.astype(f32) + taken.astype(f32)
        sent = total[half:].astype(kind)
        kept = total[:half].astype(kind)
        taken = swap(sent, bit, sizes)
    return (kept.astype(f32) + taken.astype(f32))[0]


def gather_small(parts):
    flat = jnp.concatenate([v.reshape(-1) for v in parts])
    lines = -(-flat.size // (16 * 128)) * 16
    flat = jnp.pad(flat, (0, lines * 128 - flat.size)).reshape(lines, 128)
    whole = lax.all_gather(flat, ("dp", "fsdp"), axis=0, tiled=True).reshape(-1, lines * 128)
    found, at = [], 0
    for v in parts:
        block = whole[:, at : at + v.size]
        if v.ndim == 2:
            block = block.reshape(-1, v.shape[0], v.shape[1]).swapaxes(0, 1)
            found.append(block.reshape(v.shape[0], -1))
        else:
            found.append(block.reshape(-1))
        at = at + v.size
    return found


def reduce_small(parts, order, core, sizes, me):
    count = sizes[0] * sizes[1]
    rows = [
        v.reshape(count, -1)
        if v.ndim == 1
        else v.reshape(v.shape[0], count, -1).swapaxes(0, 1).reshape(count, -1)
        for v in parts
    ]
    flat = jnp.concatenate(rows, axis=1)
    own, other = relatives(order, core)
    index = lax.bitwise_xor(jnp.asarray(own + other, jnp.int32), me[0])
    mixed = jnp.take(flat, index, axis=0)
    total = reduce_pieces(
        mixed[: len(own), None], mixed[len(own) :, None], order, core, sizes
    )[0]
    found, at = [], 0
    for v, row in zip(parts, rows):
        block = total[at : at + row.shape[1]]
        found.append(block if v.ndim == 1 else block.reshape(v.shape[0], -1))
        at = at + row.shape[1]
    return found


def dot_t(a, b):
    return lax.dot_general(a, b, (((1,), (1,)), ((), ())), preferred_element_type=f32)


def dot_n(a, b):
    return lax.dot_general(a, b, (((1,), (0,)), ((), ())), preferred_element_type=f32)


def dot_tl(a, b):
    return lax.dot_general(a, b, (((0,), (0,)), ((), ())), preferred_element_type=f32)


def head_lanes(a, rows):
    lane = lax.broadcasted_iota(jnp.int32, (rows, 2 * HEAD), 1)
    return (lane >= HEAD) if a else (lane < HEAD)


def keep_head(x, a):
    return jnp.where(head_lanes(a, x.shape[0]), x, jnp.zeros_like(x))


def stack_heads(x):
    return jnp.concatenate([keep_head(x, 0), keep_head(x, 1)], axis=0)


def join_heads(x):
    return jnp.where(head_lanes(0, FEW), x[:FEW], x[FEW:])


def few_rows(x):
    return jnp.concatenate([x, jnp.zeros_like(x)], axis=0)


def hide_few(s, first, last):
    row = lax.broadcasted_iota(jnp.int32, (EXTRA, s.shape[1]), 0)
    frame = lax.shift_right_logical(row, 1)
    seen = (frame >= first) & (frame <= last)
    count = s.shape[0] - EXTRA
    return jnp.concatenate([s[:count], jnp.where(seen, s[count:], masked_value)], axis=0)


def seen_rows(ref, lo, n):
    return jnp.concatenate([ref[pl.ds(lo, n * PATCH), :], ref[BODY:ROWS, :]], axis=0)


def seen_lanes(ref, a, lo, n):
    return jnp.concatenate(
        [ref[a * HEAD : (a + 1) * HEAD, pl.ds(lo, n * PATCH)], ref[a * HEAD : (a + 1) * HEAD, BODY:ROWS]],
        axis=1,
    )


def attend_kernel(seen_ref, q_ref, k_ref, v_ref, hide_ref, out_ref, lse_ref, few_ref, vt):
    f = pl.program_id(1)

    @pl.when(f == 0)
    def _():
        vt[...] = v_ref[...].T
        qs = stack_heads(q_ref[BODY:ROWS, :].astype(f32)[:FEW]).astype(bf16)
        s = dot_t(k_ref[...], qs) + hide_ref[...]
        top = jnp.max(s, axis=0, keepdims=True)
        p = jnp.exp(s - top)
        total = jnp.sum(p, axis=0, keepdims=True)
        o = dot_tl((p / total).astype(bf16), v_ref[...])
        out_ref[BODY:ROWS, :] = few_rows(join_heads(o)).astype(bf16)
        few_ref[0] = top + jnp.log(total)

    row = pl.multiple_of(f * PATCH, PATCH)
    seen = seen_ref[f]

    @pl.when(seen == 0)
    def _():
        out_ref[pl.ds(row, PATCH), :] = v_ref[pl.ds(row, PATCH), :]
        lse_ref[0, :, pl.ds(row, PATCH)] = jnp.zeros((2, PATCH), f32)

    for n in range(1, FRAMES + 1):

        @pl.when(seen == n)
        def _(n=n):
            first = f - (n - 1)
            lo = pl.multiple_of(first * PATCH, PATCH)
            keys = seen_rows(k_ref, lo, n)
            q = q_ref[pl.ds(row, PATCH), :]
            outs, sums = [], []
            for a in range(2):
                s = hide_few(dot_t(keys, keep_head(q, a)), first, f)
                top = jnp.max(s, axis=0, keepdims=True)
                p = jnp.exp(s - top)
                total = jnp.sum(p, axis=0, keepdims=True)
                o = dot_n(seen_lanes(vt, a, lo, n), p.astype(bf16))
                outs.append(o / total)
                sums.append(top + jnp.log(total))
            out_ref[pl.ds(row, PATCH), :] = jnp.concatenate(outs, axis=0).T.astype(bf16)
            lse_ref[0, :, pl.ds(row, PATCH)] = jnp.concatenate(sums, axis=0)


def attend(seen, qkv, hide):
    width = qkv.shape[1] // 3
    pairs = width // (2 * HEAD)
    lanes = 2 * HEAD
    return pl.pallas_call(
        attend_kernel,
        grid_spec=pltpu.PrefetchScalarGridSpec(
            num_scalar_prefetch=1,
            grid=(pairs, FRAMES),
            in_specs=[
                pl.BlockSpec((ROWS, lanes), lambda h, f, s: (0, h)),
                pl.BlockSpec((ROWS, lanes), lambda h, f, s: (0, pairs + h)),
                pl.BlockSpec((ROWS, lanes), lambda h, f, s: (0, 2 * pairs + h)),
                pl.BlockSpec((ROWS, 2 * FEW), lambda h, f, s: (0, 0)),
            ],
            out_specs=[
                pl.BlockSpec((ROWS, lanes), lambda h, f, s: (0, h)),
                pl.BlockSpec((1, 2, BODY), lambda h, f, s: (h, 0, 0)),
                pl.BlockSpec((1, 1, 2 * FEW), lambda h, f, s: (h, 0, 0)),
            ],
            scratch_shapes=[pltpu.VMEM((lanes, ROWS), bf16)],
        ),
        out_shape=(
            jax.ShapeDtypeStruct((ROWS, width), bf16),
            jax.ShapeDtypeStruct((pairs, 2, BODY), f32),
            jax.ShapeDtypeStruct((pairs, 1, 2 * FEW), f32),
        ),
        compiler_params=pltpu.CompilerParams(vmem_limit_bytes=vmem_most),
        cost_estimate=pl.CostEstimate(
            flops=ROWS * ROWS * width * 4, bytes_accessed=8 * ROWS * width, transcendentals=0
        ),
    )(seen, qkv, qkv, qkv, hide)


def unturn(x, cosine, sine, partner):
    return x * cosine - dot_n(x.astype(bf16), partner) * sine


def attend_back_kernel(
    scale, seen_ref, q_ref, k_ref, v_ref, o_ref, g_ref, lse_ref, few_ref, hide_ref, cos_ref, sin_ref,
    part_ref, out_ref, kt, dq, dk, dv,
):
    f = pl.program_id(1)
    ones = jnp.where(
        (lax.broadcasted_iota(jnp.int32, (8, 2 * HEAD), 1) >= HEAD).astype(jnp.int32)
        == lax.broadcasted_iota(jnp.int32, (8, 2 * HEAD), 0),
        1.0,
        0.0,
    ).astype(bf16)

    @pl.when(f == 0)
    def _():
        kt[...] = k_ref[...].T
        qs = stack_heads(q_ref[BODY:ROWS, :].astype(f32)[:FEW]).astype(bf16)
        gs = stack_heads(g_ref[BODY:ROWS, :].astype(f32)[:FEW])
        os = stack_heads(o_ref[BODY:ROWS, :].astype(f32)[:FEW])
        p = jnp.exp(dot_t(k_ref[...], qs) + hide_ref[...] - few_ref[0])
        gp = dot_t(v_ref[...], gs.astype(bf16))
        delta = jnp.sum(gp * p, axis=0, keepdims=True)
        ds = (p * (gp - delta)).astype(bf16)
        dv[...] = dot_n(p.astype(bf16), gs.astype(bf16))
        dk[...] = dot_n(ds, qs)
        dq[BODY:ROWS, :] = few_rows(join_heads(dot_tl(ds, k_ref[...])))

    row = pl.multiple_of(f * PATCH, PATCH)
    seen = seen_ref[f]

    @pl.when(seen == 0)
    def _():
        dv[pl.ds(row, PATCH), :] += g_ref[pl.ds(row, PATCH), :].astype(f32)
        dq[pl.ds(row, PATCH), :] = jnp.zeros((PATCH, 2 * HEAD), f32)

    for n in range(1, FRAMES + 1):

        @pl.when(seen == n)
        def _(n=n):
            first = f - (n - 1)
            lo = pl.multiple_of(first * PATCH, PATCH)
            keys = seen_rows(k_ref, lo, n)
            values = seen_rows(v_ref, lo, n)
            q = q_ref[pl.ds(row, PATCH), :]
            g = g_ref[pl.ds(row, PATCH), :]
            product = g.astype(f32) * o_ref[pl.ds(row, PATCH), :].astype(f32)
            upper = product.astype(bf16)
            lower = (product - upper.astype(f32)).astype(bf16)
            deltas = dot_t(ones, upper) + dot_t(ones, lower)
            back, add_k, add_v = [], None, None
            for a in range(2):
                qm, gm = keep_head(q, a), keep_head(g, a)
                s = hide_few(dot_t(keys, qm), first, f)
                p = jnp.exp(s - lse_ref[0, a : a + 1, pl.ds(row, PATCH)])
                gp = dot_t(values, gm)
                ds = (p * (gp - deltas[a : a + 1])).astype(bf16)
                more_v, more_k = dot_n(p.astype(bf16), gm), dot_n(ds, qm)
                add_v = more_v if add_v is None else add_v + more_v
                add_k = more_k if add_k is None else add_k + more_k
                back.append(dot_n(seen_lanes(kt, a, lo, n), ds))
            dq[pl.ds(row, PATCH), :] = jnp.concatenate(back, axis=0).T
            count = n * PATCH
            dk[pl.ds(lo, count), :] += add_k[:count]
            dk[BODY:ROWS, :] += add_k[count:]
            dv[pl.ds(lo, count), :] += add_v[:count]
            dv[BODY:ROWS, :] += add_v[count:]

    @pl.when(f == FRAMES - 1)
    def _():
        partner = part_ref[...]
        out_ref[0] = unturn(dq[...] * scale, cos_ref[...], sin_ref[...], partner).astype(bf16)
        out_ref[1] = unturn(dk[...], cos_ref[...], sin_ref[...], partner).astype(bf16)
        out_ref[2] = dv[...].astype(bf16)


def attend_back(seen, qkv, attended, grad, lse, few, hide, cosine, sine, partner, pair_lo, pair_hi):
    width = qkv.shape[1] // 3
    pairs = width // (2 * HEAD)
    lanes = 2 * HEAD
    at = pair_lo

    def whole(h, f, s):
        return (0, 0)

    return pl.pallas_call(
        functools.partial(attend_back_kernel, 1.0 / math.sqrt(HEAD)),
        grid_spec=pltpu.PrefetchScalarGridSpec(
            num_scalar_prefetch=1,
            grid=(pair_hi - pair_lo, FRAMES),
            in_specs=[
                pl.BlockSpec((ROWS, lanes), lambda h, f, s: (0, at + h)),
                pl.BlockSpec((ROWS, lanes), lambda h, f, s: (0, at + pairs + h)),
                pl.BlockSpec((ROWS, lanes), lambda h, f, s: (0, at + 2 * pairs + h)),
                pl.BlockSpec((ROWS, lanes), lambda h, f, s: (0, at + h)),
                pl.BlockSpec((ROWS, lanes), lambda h, f, s: (0, at + h)),
                pl.BlockSpec((1, 2, BODY), lambda h, f, s: (at + h, 0, 0)),
                pl.BlockSpec((1, 1, 2 * FEW), lambda h, f, s: (at + h, 0, 0)),
                pl.BlockSpec((ROWS, 2 * FEW), whole),
                pl.BlockSpec((ROWS, lanes), whole),
                pl.BlockSpec((ROWS, lanes), whole),
                pl.BlockSpec((lanes, lanes), whole),
            ],
            out_specs=pl.BlockSpec((3, ROWS, lanes), lambda h, f, s: (0, 0, h)),
            scratch_shapes=[
                pltpu.VMEM((lanes, ROWS), bf16),
                pltpu.VMEM((ROWS, lanes), f32),
                pltpu.VMEM((ROWS, lanes), f32),
                pltpu.VMEM((ROWS, lanes), f32),
            ],
        ),
        out_shape=jax.ShapeDtypeStruct((3, ROWS, (pair_hi - pair_lo) * lanes), bf16),
        compiler_params=pltpu.CompilerParams(vmem_limit_bytes=vmem_most),
        cost_estimate=pl.CostEstimate(
            flops=ROWS * ROWS * width * 10, bytes_accessed=16 * ROWS * width, transcendentals=0
        ),
    )(seen, qkv, qkv, qkv, attended, grad, lse, few, hide, cosine, sine, partner)


def project_kernel(scale, x_ref, w_ref, b_ref, cos_ref, sin_ref, part_ref, out_ref):
    j = pl.program_id(0)
    third = pl.num_programs(0) // 3
    lanes = 2 * HEAD
    w = w_ref[...]
    mixed = dot_n(x_ref[...], w) + b_ref[...]

    @pl.when(j < 2 * third)
    def _():
        bias = jnp.broadcast_to(b_ref[...], (8, w.shape[1]))
        by = jnp.where(j < third, scale, 1.0)
        for h in range(w.shape[1] // lanes):
            at = slice(h * lanes, (h + 1) * lanes)
            turned = dot_n(w[:, at], part_ref[...]).astype(bf16)
            moved = dot_n(bias[:, at].astype(bf16), part_ref[...])[:1]
            other = dot_n(x_ref[...], turned) + moved
            out_ref[:, at] = ((mixed[:, at] * cos_ref[...] + other * sin_ref[...]) * by).astype(bf16)

    @pl.when(j >= 2 * third)
    def _():
        out_ref[...] = mixed.astype(bf16)


def project(x, w, bias, cosine, sine, partner):
    rows, width = x.shape
    cols = 256
    lanes = 2 * HEAD

    def whole(j):
        return (0, 0)

    return pl.pallas_call(
        functools.partial(project_kernel, 1.0 / math.sqrt(HEAD)),
        grid=(w.shape[1] // cols,),
        in_specs=[
            pl.BlockSpec((rows, width), whole),
            pl.BlockSpec((width, cols), lambda j: (0, j)),
            pl.BlockSpec((1, cols), lambda j: (0, j)),
            pl.BlockSpec((rows, lanes), whole),
            pl.BlockSpec((rows, lanes), whole),
            pl.BlockSpec((lanes, lanes), whole),
        ],
        out_specs=pl.BlockSpec((rows, cols), lambda j: (0, j)),
        out_shape=jax.ShapeDtypeStruct((rows, w.shape[1]), bf16),
        compiler_params=pltpu.CompilerParams(vmem_limit_bytes=vmem_most),
        cost_estimate=pl.CostEstimate(
            flops=3 * rows * w.size, bytes_accessed=2 * (x.size + w.size + 3 * x.size), transcendentals=0
        ),
    )(x, w, bias, cosine, sine, partner)


def turn_tables(frame_ids, rows_of):
    index = jnp.asarray(rows_of, jnp.int32)
    time = frame_ids[jnp.asarray([f * FRAME_ROWS for f in range(FRAMES)])]
    patch = jnp.maximum(index % FRAME_ROWS - 2, 0)
    height = patch // GRID
    breadth = patch % GRID
    time = jnp.repeat(time, PATCH)
    time = jnp.concatenate([time, jnp.repeat(time[::PATCH], 2), jnp.zeros((EXTRA - FEW,), jnp.int32)])
    cosine, sine = [], []
    for position, part in zip((time, height, breadth), part_sizes):
        half = part // 2
        frequency = 10000.0 ** (-jnp.arange(half).astype(f32) / half)
        angles = position.astype(f32)[:, None] * frequency[None, :]
        cosine += [jnp.cos(angles)] * 2
        sine += [-jnp.sin(angles), jnp.sin(angles)]
    return jnp.concatenate(cosine * 2, axis=1), jnp.concatenate(sine * 2, axis=1)


def partner_matrix():
    lanes = 2 * HEAD
    matrix = np.zeros((lanes, lanes), np.float32)
    for head in range(2):
        at = head * HEAD
        for part in part_sizes:
            for i in range(part // 2):
                matrix[at + i, at + i + part // 2] = 1.0
                matrix[at + i + part // 2, at + i] = 1.0
            at += part
    return jnp.asarray(matrix, bf16)


def seen_frames(offset_row):
    frame = jnp.arange(FRAMES, dtype=jnp.int32)
    start = jnp.where(frame >= offset_row[1], offset_row[1], 0)
    return jnp.where(frame < offset_row[2], frame - start + 1, 0)


def hidden_few(seen):
    frame_of = np.concatenate([np.repeat(np.arange(FRAMES), PATCH), np.repeat(np.arange(FRAMES), 2), np.full(EXTRA - FEW, FRAMES)])
    own = np.zeros((ROWS, FEW), bool)
    own[BODY + np.arange(FEW), np.arange(FEW)] = True
    frame = jnp.asarray(frame_of, jnp.int32)[:, None]
    query = jnp.arange(FEW, dtype=jnp.int32)[None, :] // 2
    count = jnp.repeat(seen, 2)[None, :]
    allowed = ((frame <= query) & (frame > query - count)) | jnp.asarray(own)
    return jnp.tile(jnp.where(allowed, 0.0, masked_value), (1, 2))


def row_order():
    patches = [f * FRAME_ROWS + 2 + j for f in range(FRAMES) for j in range(PATCH)]
    first = [f * FRAME_ROWS + j for f in range(FRAMES) for j in range(2)]
    return np.array(patches + first + [0] * (EXTRA - FEW))


def place(p, order, core):
    own, other = relatives(order, core)
    return (1, other.index(p)) if p in other else (0, own.index(p))


def find_piece(rels, p):
    for c, rel in enumerate(rels):
        if p in rel:
            return c, rel.index(p)
    raise ValueError(p)


def feed_kernel(
    up_rels, down_rels, up_order, down_order, core, me_ref, x_ref, g_ref, bias_ref, shift_ref, mid_ref, *refs
):
    n_up, n_down = len(up_rels), len(down_rels)
    up_refs, refs = refs[:n_up], refs[n_up:]
    down_refs, refs = refs[:n_down], refs[n_down:]
    out_ref, gx_ref, gb_ref = refs[:3]
    du_refs, dd_refs = refs[3:5], refs[5:7]
    wu, wd, su, sd, acc, xt, act, gup, in_sem, out_sem, mid_sem = refs[7:]
    count = sum(len(q) for q in up_rels)
    blocks = FEED_BLOCKS
    each = count // blocks
    shift = each.bit_length() - 1
    i = pl.program_id(0)
    me = me_ref[0]
    width = x_ref.shape[1]
    cols = wu.shape[2]
    rows = width // count
    part = cols // each
    slot = lax.rem(i, 2)

    def group(j):
        return lax.bitwise_xor(lax.shift_right_logical(me, shift), j)

    def fetch(j, to):
        at = pl.multiple_of(group(j) * cols, cols)
        for p in range(count):
            c, n = find_piece(up_rels, p)
            start = pl.multiple_of(lax.bitwise_xor(me, p) * rows, rows)
            pltpu.make_async_copy(
                up_refs[c].at[n, :, pl.ds(at, cols)], wu.at[to, pl.ds(start, rows), :], in_sem.at[0, to]
            ).start()
        for k in range(blocks):

            @pl.when(j == k)
            def _():
                for p in range(each):
                    c, n = find_piece(down_rels, (k << shift) | p)
                    start = pl.multiple_of(lax.bitwise_xor(me & (each - 1), p) * part, part)
                    pltpu.make_async_copy(
                        down_refs[c].at[n], wd.at[to, pl.ds(start, part), :], in_sem.at[1, to]
                    ).start()

    middle = pltpu.make_async_copy(mid_ref, acc, mid_sem)

    @pl.when(i == 0)
    def _():
        fetch(i, slot)
        middle.start()
        xt[...] = x_ref[...].T
        gx_ref[...] = jnp.zeros_like(gx_ref)

    @pl.when(i + 1 < blocks)
    def _():
        fetch(i + 1, 1 - slot)

    pltpu.make_async_copy(wu.at[slot], wu.at[slot], in_sem.at[0, slot]).wait()
    pltpu.make_async_copy(wd.at[slot], wd.at[slot], in_sem.at[1, slot]).wait()
    half = cols // 2
    for h in range(2):
        at = slice(h * half, (h + 1) * half)
        u = dot_n(x_ref[...], wu[slot, :, at]) + bias_ref[:, at]
        ga = dot_t(g_ref[...], wd[slot, at, :])
        e = jnp.exp(u * u * -0.5)
        d = 1.0 + jnp.abs(u) * (0.3275911 * inv_sqrt_two)
        t = pl.reciprocal(d, approx=True)
        t = t * (2.0 - d * t)
        poly = t * (0.127414796 + t * (-0.142248368 + t * (0.7107068705 + t * (-0.7265760135 + t * 0.5307027145))))
        tail = poly * e
        phi = jnp.where(u >= 0.0, 1.0 - tail, tail)
        act[:, at] = (u * phi).astype(bf16)
        gu = (ga * (phi + u * (e * inv_sqrt_tau))).astype(bf16)
        gup[:, at] = gu
        gb_ref[:, at] = jnp.sum(gu.astype(f32), axis=0, keepdims=True)

    @pl.when(i == 0)
    def _():
        middle.wait()

    acc[...] += dot_n(act[...], wd[slot])
    gx_ref[...] += dot_t(gup[...], wu[slot])

    @pl.when(i >= 2)
    def _():
        pltpu.make_async_copy(su.at[slot], su.at[slot], out_sem.at[0, slot]).wait()
        pltpu.make_async_copy(sd.at[slot], sd.at[slot], out_sem.at[1, slot]).wait()

    sd[slot] = dot_tl(act[...], g_ref[...]).astype(bf16)
    su[slot] = dot_n(xt[...], gup[...]).astype(bf16)
    at = pl.multiple_of(group(i) * cols, cols)
    for p in range(count):
        c, n = place(p, up_order, core)
        start = pl.multiple_of(lax.bitwise_xor(me, p) * rows, rows)
        pltpu.make_async_copy(
            su.at[slot, pl.ds(start, rows), :], du_refs[c].at[n, :, pl.ds(at, cols)], out_sem.at[0, slot]
        ).start()
    for k in range(blocks):

        @pl.when(i == k)
        def _():
            for p in range(each):
                c, n = place((k << shift) | p, down_order, core)
                start = pl.multiple_of(lax.bitwise_xor(me & (each - 1), p) * part, part)
                pltpu.make_async_copy(
                    sd.at[slot, pl.ds(start, part), :], dd_refs[c].at[n], out_sem.at[1, slot]
                ).start()

    @pl.when(i == blocks - 1)
    def _():
        out_ref[...] = (acc[...] + shift_ref[...]).astype(bf16)
        for s in range(2):
            pltpu.make_async_copy(su.at[s], su.at[s], out_sem.at[0, s]).wait()
            pltpu.make_async_copy(sd.at[s], sd.at[s], out_sem.at[1, s]).wait()


FEED_BLOCKS = 8


def feed(x, grad, middle, bias, shift, up_pieces, down_pieces, up_order, down_order, core, me):
    up_rels = [q for _, q in up_pieces]
    down_rels = [q for _, q in down_pieces]
    count = sum(len(q) for q in up_rels)
    tokens, width = x.shape
    hidden = bias.shape[1]
    cols = hidden // FEED_BLOCKS
    shift_by = (count // FEED_BLOCKS).bit_length() - 1

    def block(i, me_ref):
        return (0, lax.bitwise_xor(lax.shift_right_logical(me_ref[0], shift_by), i))

    def whole(i, me_ref):
        return (0, 0)

    once = pl.Buffered(1)
    anywhere = pl.BlockSpec(memory_space=pl.ANY)
    return pl.pallas_call(
        functools.partial(feed_kernel, up_rels, down_rels, up_order, down_order, core),
        grid_spec=pltpu.PrefetchScalarGridSpec(
            num_scalar_prefetch=1,
            grid=(FEED_BLOCKS,),
            in_specs=[
                pl.BlockSpec((tokens, width), whole, pipeline_mode=once),
                pl.BlockSpec((tokens, width), whole, pipeline_mode=once),
                pl.BlockSpec((1, cols), block),
                pl.BlockSpec((1, width), whole),
                anywhere,
            ]
            + [anywhere] * (len(up_pieces) + len(down_pieces)),
            out_specs=[
                pl.BlockSpec((tokens, width), whole, pipeline_mode=once),
                pl.BlockSpec((tokens, width), whole, pipeline_mode=once),
                pl.BlockSpec((1, cols), block),
            ]
            + [anywhere] * 4,
            scratch_shapes=[
                pltpu.VMEM((2, width, cols), bf16),
                pltpu.VMEM((2, cols, width), bf16),
                pltpu.VMEM((2, width, cols), bf16),
                pltpu.VMEM((2, cols, width), bf16),
                pltpu.VMEM((tokens, width), f32),
                pltpu.VMEM((width, tokens), bf16),
                pltpu.VMEM((tokens, cols), bf16),
                pltpu.VMEM((tokens, cols), bf16),
                pltpu.SemaphoreType.DMA((2, 2)),
                pltpu.SemaphoreType.DMA((2, 2)),
                pltpu.SemaphoreType.DMA,
            ],
        ),
        out_shape=[
            jax.ShapeDtypeStruct((tokens, width), bf16),
            jax.ShapeDtypeStruct((tokens, width), f32),
            jax.ShapeDtypeStruct((1, hidden), f32),
        ]
        + [jax.ShapeDtypeStruct((count // 2, width // count, hidden), bf16)] * 2
        + [jax.ShapeDtypeStruct((count // 2, hidden // count, width), bf16)] * 2,
        compiler_params=pltpu.CompilerParams(vmem_limit_bytes=vmem_most),
        cost_estimate=pl.CostEstimate(
            flops=12 * tokens * width * hidden,
            bytes_accessed=8 * width * hidden + 16 * tokens * width,
            transcendentals=0,
        ),
    )(me, x, grad, bias, shift, middle, *[v for v, _ in up_pieces], *[v for v, _ in down_pieces])


def normalize(values, gain, bias_add):
    center = values - jnp.mean(values, axis=-1, keepdims=True)
    scale_inv = lax.rsqrt(jnp.mean(center * center, axis=-1, keepdims=True) + eps_norm)
    unit_rows = center * scale_inv
    return (unit_rows * gain + bias_add, unit_rows, scale_inv)


def norm_back(grad_out, unit_rows, scale_inv, gain):
    scaled = grad_out * gain
    mean_grad = jnp.mean(scaled, axis=-1, keepdims=True)
    mean_cross = jnp.mean(scaled * unit_rows, axis=-1, keepdims=True)
    return scale_inv * (scaled - mean_grad - unit_rows * mean_cross)


def sort_rows(x):
    frames = x.reshape(FRAMES, FRAME_ROWS, -1)
    few = frames[:, :2].reshape(FEW, -1)
    return jnp.concatenate([frames[:, 2:].reshape(BODY, -1), few, jnp.zeros_like(few)], axis=0)


def unsort_rows(x):
    patches = x[:BODY].reshape(FRAMES, PATCH, -1)
    few = x[BODY : BODY + FEW].reshape(FRAMES, 2, -1)
    return jnp.concatenate([few, patches], axis=1).reshape(FRAMES * FRAME_ROWS, -1)


def body(
    sizes,
    tokens,
    frame_ids,
    pad_mask,
    episode_offsets,
    ln1_gain,
    ln1_bias,
    w_qkv,
    b_qkv,
    w_out,
    b_out,
    ln2_gain,
    ln2_bias,
    w_up,
    b_up,
    w_down,
    b_down,
    cotangent,
):
    width = tokens.shape[1]
    me = (lax.axis_index("dp") * sizes[1] + lax.axis_index("fsdp")).astype(jnp.int32)[None]
    core, order_a, order_b = bit_orders(sizes)
    pieces_q = gather_pieces(w_qkv[:, : 2 * width], order_a, core, sizes)
    pieces_v = gather_pieces(
        jnp.concatenate([w_qkv[:, 2 * width :], w_out], axis=1), order_b, core, sizes
    )
    w_up, w_down, *_ = lax.optimization_barrier((w_up, w_down, pieces_q[0][0], pieces_v[0][0]))
    pieces_up = gather_pieces(w_up, order_a, core, sizes)
    pieces_down = gather_pieces(w_down, order_b, core, sizes)
    gain_one, bias_one, qkv_rows, out_bias, gain_two, bias_two, up_bias, down_bias = [
        v.astype(f32)
        for v in gather_small(
            [ln1_gain, ln1_bias, b_qkv, b_out, ln2_gain, ln2_bias, b_up, b_down]
        )
    ]
    seen = seen_frames(episode_offsets[0])
    hide = hidden_few(seen)
    cosine, sine = turn_tables(frame_ids, row_order())
    partner = partner_matrix()
    values_in = sort_rows(tokens).astype(f32)
    cot = sort_rows(cotangent)
    normed_one, unit_one, inv_one = normalize(values_in, gain_one, bias_one)
    normed_one = normed_one.astype(bf16)
    qk_matrix = assemble(pieces_q, me)
    vo_matrix = assemble(pieces_v, me)
    qkv_matrix = jnp.concatenate([qk_matrix, vo_matrix[:, :width]], axis=1)
    out_matrix = vo_matrix[:, width:]
    qkv = project(normed_one, qkv_matrix, qkv_rows.reshape(1, 3 * width), cosine, sine, partner)
    attended, lse, few = attend(seen, qkv, hide)
    middle = values_in + jnp.dot(attended, out_matrix, preferred_element_type=f32) + out_bias
    normed_two, unit_two, inv_two = normalize(middle, gain_two, bias_two)
    normed_two = normed_two.astype(bf16)
    result, grad_normed_two, grad_b_up_local, up_own, up_other, down_own, down_other = feed(
        normed_two,
        cot,
        middle,
        up_bias[None],
        down_bias[None],
        pieces_up,
        pieces_down,
        order_a,
        order_b,
        core,
        me,
    )
    output = unsort_rows(result)
    grad_b_down_local = jnp.sum(cot.astype(f32), axis=0)
    grad_gain_two = jnp.sum(grad_normed_two * unit_two, axis=0)
    grad_bias_two = jnp.sum(grad_normed_two, axis=0)
    sum_up = reduce_pieces(up_own, up_other, order_a, core, sizes)
    sum_down = reduce_pieces(down_own, down_other, order_b, core, sizes)
    small_feed = reduce_small(
        [grad_gain_two, grad_bias_two, grad_b_up_local[0], grad_b_down_local],
        order_a,
        core,
        sizes,
        me,
    )
    grad_middle = cot.astype(f32) + norm_back(grad_normed_two, unit_two, inv_two, gain_two)
    grad_branch = grad_middle.astype(bf16)
    grad_b_out_local = jnp.sum(grad_branch.astype(f32), axis=0)
    grad_w_out_local = dot_tl(attended, grad_branch)
    grad_attended = dot_t(grad_branch, out_matrix).astype(bf16)
    pairs = width // (2 * HEAD)
    grad_mixed = attend_back(
        seen, qkv, attended, grad_attended, lse, few, hide, cosine, sine, partner, 0, pairs
    )
    grad_b_qkv_local = jnp.sum(grad_mixed.astype(f32), axis=1)
    grad_w_parts = [dot_tl(normed_one, grad_mixed[i]).astype(bf16) for i in range(3)]
    grad_normed_one = (
        dot_t(grad_mixed[0], qk_matrix[:, :width])
        + dot_t(grad_mixed[1], qk_matrix[:, width:])
        + dot_t(grad_mixed[2], vo_matrix[:, :width])
    )
    grad_gain_one = jnp.sum(grad_normed_one * unit_one, axis=0)
    grad_bias_one = jnp.sum(grad_normed_one, axis=0)
    grad_qk = jnp.concatenate(grad_w_parts[:2], axis=1)
    sum_q = reduce_pieces(*split(grad_qk, order_a, core, me), order_a, core, sizes)
    grad_vo = jnp.concatenate([grad_w_parts[2], grad_w_out_local.astype(bf16)], axis=1)
    sum_v = reduce_pieces(*split(grad_vo, order_b, core, me), order_b, core, sizes)
    small_attn = reduce_small(
        [grad_gain_one, grad_bias_one, grad_b_qkv_local, grad_b_out_local],
        order_b,
        core,
        sizes,
        me,
    )
    grad_tokens = unsort_rows(
        grad_middle + norm_back(grad_normed_one, unit_one, inv_one, gain_one)
    )
    return (
        output,
        grad_tokens,
        small_attn[0],
        small_attn[1],
        jnp.concatenate([sum_q, sum_v[:, :width]], axis=1),
        small_attn[2],
        sum_v[:, width:],
        small_attn[3],
        small_feed[0],
        small_feed[1],
        sum_up,
        small_feed[2],
        sum_down,
        small_feed[3],
    )


def solution(mesh):
    placed = (
        P(("dp", "fsdp"), None),
        P(("dp", "fsdp")),
        P(("dp", "fsdp")),
        P(("dp", "fsdp"), None),
        P(("dp", "fsdp")),
        P(("dp", "fsdp")),
        P(("dp", "fsdp"), None),
        P(None, ("dp", "fsdp")),
        P(("dp", "fsdp"), None),
        P(("dp", "fsdp")),
        P(("dp", "fsdp")),
        P(("dp", "fsdp")),
        P(("dp", "fsdp"), None),
        P(("dp", "fsdp")),
        P(("dp", "fsdp"), None),
        P(("dp", "fsdp")),
        P(("dp", "fsdp"), None),
    )
    sizes = (mesh.shape["dp"], mesh.shape["fsdp"])
    return jax.shard_map(
        functools.partial(body, sizes),
        mesh=mesh,
        in_specs=placed,
        out_specs=(
            P(("dp", "fsdp"), None),
            P(("dp", "fsdp"), None),
            P(("dp", "fsdp")),
            P(("dp", "fsdp")),
            P(("dp", "fsdp"), None),
            P(None, ("dp", "fsdp")),
            P(("dp", "fsdp"), None),
            P(("dp", "fsdp")),
            P(("dp", "fsdp")),
            P(("dp", "fsdp")),
            P(("dp", "fsdp"), None),
            P(("dp", "fsdp")),
            P(("dp", "fsdp"), None),
            P(("dp", "fsdp")),
        ),
        check_vma=False,
    )
```

time: 1930 us -> 771 us (0.40)
  waiting for transfers between devices: 1020 us -> 216 us
  matrix products: 347 us -> 47.3 us
  Pallas kernels: 0 us -> 224 us
  local copies, waits for them, and re-layouts: 206 us -> 56.7 us
  blocking collectives: 211 us -> 63.2 us
  starting transfers between devices: 0.36 us -> 61.2 us
  other arithmetic: 114 us -> 94.4 us
    reduce_scatter x4 -> x0, waiting for transfers between devices: 1010 us -> none  [the longest x1 361 us: reduce_feed(): lax.psum_scatter(grad_matrix, ('dp', 'fsdp'), scatter_dimension=0, tiled=...]
    dot_general x24 -> x9, matrix products: 347 us -> 47.3 us  [the longest x4 22.7 us: dot_t(): lax.dot_general(a, b, (((1,), (1,)), ((), ())), preferred_element_type=f32)]
    pallas_call x0 -> x8, Pallas kernels: none -> 224 us  [the longest x1 86.5 us: feed(): pl.pallas_call(functools.partial(feed_kernel, up_rels, down_rels, up_orde...]
    ppermute x0 -> x54, waiting for transfers between devices: none -> 216 us  [swap(): return lax.ppermute(value, ('dp', 'fsdp'), pairs)]
    concatenate x4 -> x7, local copies, waits for them, and re-layouts: 161 us -> 11.9 us  [the longest x1 5.85 us: turn_tables(): jnp.concatenate(sine * 2, axis=1)]
    unnamed x2 -> x0, blocking collectives: 89.7 us -> none
    ppermute x0 -> x54, starting transfers between devices: none -> 61.2 us  [swap(): return lax.ppermute(value, ('dp', 'fsdp'), pairs)]
    all_gather x2 -> x1, blocking collectives: 121 us -> 63.2 us  [gather_small(): lax.all_gather(flat, ('dp', 'fsdp'), axis=0, tiled=True)]
  transfers between devices with their start and end apart: 9 -> 54, of which waited for: 4 -> 24; matrix products, arithmetic and copies ran while one was open for 20% -> 19% of each run, Pallas kernels for 0% -> 11%
where the time goes in v1:
time: 771 us; the launch traced here: 765 us
  Pallas kernels  224 us (29%)
  waiting for transfers between devices  216 us (28%)
  other arithmetic  94.4 us (12%)
  blocking collectives  63.2 us (8%)
  starting transfers between devices  61.2 us (8%)
  local copies, waits for them, and re-layouts  56.7 us (7%)
  matrix products  47.3 us (6%)
    ppermute x54, waiting for transfers between devices, swap(): return lax.ppermute(value, ('dp', 'fsdp'), pairs)  216 us
    pallas_call x1, Pallas kernels, feed(): pl.pallas_call(functools.partial(feed_kernel, up_rels, down_rels, up_orde...  86.5 us
    all_gather x1, blocking collectives, gather_small(): lax.all_gather(flat, ('dp', 'fsdp'), axis=0, tiled=True)  63.2 us
    ppermute x54, starting transfers between devices, swap(): return lax.ppermute(value, ('dp', 'fsdp'), pairs)  61.2 us
    pallas_call x1, Pallas kernels, attend_back(): pl.pallas_call(functools.partial(attend_back_kernel, 1.0 / math.sqrt(HEAD...  50.4 us
    pallas_call x1, Pallas kernels, attend(): pl.pallas_call(attend_kernel, grid_spec=pltpu.PrefetchScalarGridSpec(num_...  45.7 us
    pallas_call x1, Pallas kernels, project(): pl.pallas_call(functools.partial(project_kernel, 1.0 / math.sqrt(HEAD)),...  24.6 us
    dot_general x4, matrix products, dot_t(): lax.dot_general(a, b, (((1,), (1,)), ((), ())), preferred_element_type=f32)  22.7 us
  transfers between devices with their start and end apart: 54, of which 24 were waited for; matrix products, arithmetic and copies ran while one was open for 19% of the time, Pallas kernels for 11%

profile of v1, /device:TPU:1, one launch (start us, length us, event | category | flops | bytes accessed | tf_op | source)
XLA Modules:
  0.0 765.0 jit_solution(8618140271520856212)
XLA Ops:
  24.9 63.2 %all_gather.3 = bf16[512,128]{1,0:T(8,128)(2,1)S(1)} all-gather(bf16[16,128]{1,0:T(8,128)(2,1)S(1)} %pad_bitcast_fusion), channel_id=1, replica_groups=mesh['dp'=4,'fsdp'=8] {'dp','fsdp'}, dimensions={0}, use_global_device_ids=true | all-gather | bytes 135168 | tf_op jit(solution)/shard_map/all_gather | solution.py:148
  92.3 5.1 multiply_sine_fusion
  101.7 16.6 %collective-permute-done.7 = bf16[2,32,2048]{2,1,0:T(8,128)(2,1)} collective-permute-done((bf16[2,32,2048]{2,1,0:T(8,128)(2,1)}, bf16[2,32,2048]{2,1,0:T(8,128)(2,1)}, u32[]{:S(2)}, u32[]{:S(2)}) %collective-permute-start.7) | collective-permute-done | bytes 262176 | tf_op jit(solution)/shard_map/ppermute | solution.py:38
  147.7 5.8 collective-permute-done.12
  157.6 24.2 %collective-permute-done.19 = bf16[2,128,1024]{2,1,0:T(8,128)(2,1)S(1)} collective-permute-done((bf16[2,128,1024]{2,1,0:T(8,128)(2,1)S(1)}, bf16[2,128,1024]{2,1,0:T(8,128)(2,1)S(1)}, u32[]{:S(2)}, u32[]{:S(2)}) %collective-permute-start.19) | collective-permute-done | bytes 524320 | tf_op jit(solution)/shard_map/ppermute | solution.py:38
  184.0 9.0 %collective-permute-done.13 = bf16[2,32,4096]{2,1,0:T(8,128)(2,1)S(1)} collective-permute-done((bf16[2,32,4096]{2,1,0:T(8,128)(2,1)S(1)}, bf16[2,32,4096]{2,1,0:T(8,128)(2,1)S(1)}, u32[]{:S(2)}, u32[]{:S(2)}) %collective-permute-start.13) | collective-permute-done | bytes 524320 | tf_op jit(solution)/shard_map/ppermute | solution.py:38
  201.5 7.0 collective-permute-start.5
  221.5 5.7 concatenate.113.cos_ref
  227.3 5.9 concatenate.114.sin_ref
  234.4 6.2 collective-permute-start.22
  252.3 6.1 pad_maximum_fusion.w_ref
  258.4 24.6 %shard_map.328.q_ref.k_ref.v_ref = bf16[1040,3072]{1,0:T(8,128)(2,1)} custom-call(bf16[1040,1024]{1,0:T(8,128)(2,1)} %fusion.9.x_ref, bf16[1024,3072]{1,0:T(8,128)(2,1)} %pad_maximum_fusion.w_ref, f32[1,3072]{1,0:T(1,128)} %reshape.361.b_ref, f32[1040,128]{1,0:T(8,128)} %concatenate.113.cos_ref, f32[1040,128]{1,0:T(8,128)} %concatenate.114.sin_ref, ...), custom_call_target="tpu_custom_call" | custom-call | flops 9814671360 | bytes 14811136 | tf_op jit(solution)/shard_map/pallas_call | solution.py:466
  283.0 45.7 %shard_map.329 = (bf16[1040,1024]{1,0:T(8,128)(2,1)}, f32[8,2,1024]{2,1,0:T(2,128)}, f32[8,1,16]{2,1,0:T(1,128)}) custom-call(s32[4]{0:T(128)} %copy-done.42, bf16[1040,3072]{1,0:T(8,128)(2,1)} %shard_map.328.q_ref.k_ref.v_ref, bf16[1040,3072]{1,0:T(8,128)(2,1)} %shard_map.328.q_ref.k_ref.v_ref, bf16[1040,3072]{1,0:T(8,128)(2,1)} %shard_map.328.q_ref.k_ref.v_ref, ...), custom_call_target="tpu_custom_call" | custom-call | flops 4430233600 | bytes 8519680 | tf_op jit(solution)/shard_map/pallas_call | solution.py:284
  329.4 5.0 fusion.34
  337.1 86.5 %shard_map.330 = (bf16[1040,1024]{1,0:T(8,128)(2,1)}, f32[1040,1024]{1,0:T(8,128)}, f32[1,4096]{1,0:T(1,128)}, bf16[16,32,4096]{2,1,0:T(8,128)(2,1)}, bf16[16,32...) custom-call(s32[1]{0:T(128)} %bitcast.me_ref, ...), custom_call_target="tpu_custom_call" | custom-call | flops 52344913920 | bytes 50593792 | tf_op jit(solution)/shard_map/pallas_call | solution.py:687
  423.6 5.3 multiply_reduce_fusion
  436.7 50.4 %shard_map.331 = bf16[3,1040,1024]{2,1,0:T(8,128)(2,1)} custom-call(s32[4]{0:T(128)} %copy-done.42, bf16[1040,3072]{1,0:T(8,128)(2,1)} %shard_map.328.q_ref.k_ref.v_ref, bf16[1040,3072]{1,0:T(8,128)(2,1)} %shard_map.328.q_ref.k_ref.v_ref, bf16[1040,3072]{1,0:T(8,128)(2,1)} %shard_map.328.q_ref.k_ref.v_ref, bf16[1040,1024]{1,0:T(8,128)(2,1)} %get-tuple-element.30.o_ref, ...), custom_call_target="tpu_custom_call" | custom-call | flops 11075584000 | bytes 17039360 | tf_op jit(solution)/shard_map/pallas_call | solution.py:401
  487.1 6.7 convolution_convert_fusion.3
  502.1 4.6 convolution_convert_fusion.2
  519.3 4.8 pad_maximum_fusion.2.whole
  528.4 10.1 %fusion.14 = (f32[1024]{0:T(1024)S(1)}, f32[1040]{0:T(1024)S(1)}, f32[1040]{0:T(1024)S(1)}, f32[1024]{0:T(1024)S(1)}, f32[1040,1024]{1,0:T(8,128)}) fusion(f32[1040]{0:T(1024)S(1)} %copy-done.29, f32[1040]{0:T(1024)S(1)} %copy-done.27, bf16[1040]{0:T(1024)(128)(2,1)S(1)} %pad.68.clone, bf16[8,1024]{1,0:T(8,128)(2,1)S(1)} %reshape.337, ...), kind=kOutput, calls=%fused_computation.28 | convolution fusion | flops 2199138304 | bytes 19151136 | tf_op jit(solution)/shard_map/dot_general | solution.py:185
  540.3 5.0 fusion.13
  550.6 5.4 pad_maximum_fusion.1
  557.5 11.9 %collective-permute-start.26 = (f32[4,1,192]{2,0,1:T(4,128)S(1)}, f32[4,1,192]{2,0,1:T(4,128)S(1)}, u32[]{:S(2)}, u32[]{:S(2)}) collective-permute-start(f32[4,1,192]{2,0,1:T(4,128)S(1)} %slice.460), channel_id=1, source_target_pairs={{0,16},{1,17},{2,18},{3,19},{4,20},{5,21},{6,22},{7,23},{8,24},{9,... | collective-permute-start | bytes 9224 | tf_op jit(solution)/shard_map/ppermute | solution.py:38
  575.8 4.7 reshape.349
  603.9 16.0 %collective-permute-done.30 = bf16[8,32,2048]{2,1,0:T(8,128)(2,1)S(1)} collective-permute-done((bf16[8,32,2048]{2,1,0:T(8,128)(2,1)S(1)}, bf16[8,32,2048]{2,1,0:T(8,128)(2,1)S(1)}, u32[]{:S(2)}, u32[]{:S(2)}) %collective-permute-start.30) | collective-permute-done | bytes 1048608 | tf_op jit(solution)/shard_map/ppermute | solution.py:38
  637.1 45.8 %collective-permute-done.36 = bf16[4,32,2048]{2,1,0:T(8,128)(2,1)S(1)} collective-permute-done((bf16[4,32,2048]{2,1,0:T(8,128)(2,1)S(1)}, bf16[4,32,2048]{2,1,0:T(8,128)(2,1)S(1)}, u32[]{:S(2)}, u32[]{:S(2)}) %collective-permute-start.36) | collective-permute-done | bytes 524320 | tf_op jit(solution)/shard_map/ppermute | solution.py:38
  692.2 10.7 %collective-permute-done.51 = bf16[4,128,1024]{2,1,0:T(8,128)(2,1)S(1)} collective-permute-done((bf16[4,128,1024]{2,1,0:T(8,128)(2,1)S(1)}, bf16[4,128,1024]{2,1,0:T(8,128)(2,1)S(1)}, u32[]{:S(2)}, u32[]{:S(2)}) %collective-permute-start.51) | collective-permute-done | bytes 1048608 | tf_op jit(solution)/shard_map/ppermute | solution.py:38
  709.0 32.5 %collective-permute-done.52 = bf16[2,128,1024]{2,1,0:T(8,128)(2,1)S(1)} collective-permute-done((bf16[2,128,1024]{2,1,0:T(8,128)(2,1)S(1)}, bf16[2,128,1024]{2,1,0:T(8,128)(2,1)S(1)}, u32[]{:S(2)}, u32[]{:S(2)}) %collective-permute-start.52) | collective-permute-done | bytes 524320 | tf_op jit(solution)/shard_map/ppermute | solution.py:38
  741.8 11.0 %collective-permute-done.47 = bf16[2,32,4096]{2,1,0:T(8,128)(2,1)S(1)} collective-permute-done((bf16[2,32,4096]{2,1,0:T(8,128)(2,1)S(1)}, bf16[2,32,4096]{2,1,0:T(8,128)(2,1)S(1)}, u32[]{:S(2)}, u32[]{:S(2)}) %collective-permute-start.47) | collective-permute-done | bytes 524320 | tf_op jit(solution)/shard_map/ppermute | solution.py:38
  753.8 4.6 collective-permute-done.53
  759.2 4.8 collective-permute-done.48
  (385 shorter events, 212.2 us)
Async XLA Ops:
  2.4 95.1 %collective-permute-start.6 = (bf16[1,32,2048]{2,1,0:T(8,128)(2,1)S(1)}, bf16[1,32,2048]{2,1,0:T(8,128)(2,1)S(1)}, u32[]{:S(2)}, u32[]{:S(2)}) collective-permute-start(bf16[1,32,2048]{2,1,0:T(8,128)(2,1)S(1)} %maximum_bitcast_fusion), channel_id=1, source_target_pairs={{0,2},{1,3},{2,0},{3,1},{4,6},{5,7},{6,4},{7,5},{8,10},{9,11},{10,... | collective-permute-start | bytes 393224 | tf_op jit(solution)/shard_map/ppermute | solution.py:38
  5.5 92.7 %collective-permute-start = (bf16[1,32,2048]{2,1,0:T(8,128)(2,1)S(1)}, bf16[1,32,2048]{2,1,0:T(8,128)(2,1)S(1)}, u32[]{:S(2)}, u32[]{:S(2)}) collective-permute-start(bf16[1,32,2048]{2,1,0:T(8,128)(2,1)S(1)} %slice_bitcast_fusion.9), channel_id=1, source_target_pairs={{0,2},{1,3},{2,0},{3,1},{4,6},{5,7},{6,4},{7,5},{8,10},{9,11},{10,... | collective-permute-start | bytes 393224 | tf_op jit(solution)/shard_map/ppermute | solution.py:38
  98.2 20.0 %collective-permute-start.7 = (bf16[2,32,2048]{2,1,0:T(8,128)(2,1)}, bf16[2,32,2048]{2,1,0:T(8,128)(2,1)}, u32[]{:S(2)}, u32[]{:S(2)}) collective-permute-start(bf16[2,32,2048]{2,1,0:T(8,128)(2,1)} %pad_maximum_fusion.17), channel_id=1, source_target_pairs={{0,4},{1,5},{2,6},{3,7},{4,0},{5,1},{6,2},{7,3},{8,12},{9,13},{10,... | collective-permute-start | bytes 786440 | tf_op jit(solution)/shard_map/ppermute | solution.py:38
  99.0 24.9 %collective-permute-start.1 = (bf16[2,32,2048]{2,1,0:T(8,128)(2,1)}, bf16[2,32,2048]{2,1,0:T(8,128)(2,1)}, u32[]{:S(2)}, u32[]{:S(2)}) collective-permute-start(bf16[2,32,2048]{2,1,0:T(8,128)(2,1)} %pad_maximum_fusion.16), channel_id=1, source_target_pairs={{0,4},{1,5},{2,6},{3,7},{4,0},{5,1},{6,2},{7,3},{8,12},{9,13},{10,... | collective-permute-start | bytes 786440 | tf_op jit(solution)/shard_map/ppermute | solution.py:38
  147.2 34.6 %collective-permute-start.19 = (bf16[2,128,1024]{2,1,0:T(8,128)(2,1)S(1)}, bf16[2,128,1024]{2,1,0:T(8,128)(2,1)S(1)}, u32[]{:S(2)}, u32[]{:S(2)}) collective-permute-start(bf16[2,128,1024]{2,1,0:T(8,128)(2,1)S(1)} %pad_maximum_fusion.14), channel_id=1, source_target_pairs={{0,4},{1,5},{2,6},{3,7},{4,0},{5,1},{6,2},{7,3},{8,12},{9,13},{10,... | collective-permute-start | bytes 1572872 | tf_op jit(solution)/shard_map/ppermute | solution.py:38
  154.5 38.5 %collective-permute-start.13 = (bf16[2,32,4096]{2,1,0:T(8,128)(2,1)S(1)}, bf16[2,32,4096]{2,1,0:T(8,128)(2,1)S(1)}, u32[]{:S(2)}, u32[]{:S(2)}) collective-permute-start(bf16[2,32,4096]{2,1,0:T(8,128)(2,1)S(1)} %pad_maximum_fusion.13), channel_id=1, source_target_pairs={{0,4},{1,5},{2,6},{3,7},{4,0},{5,1},{6,2},{7,3},{8,12},{9,13},{10,... | collective-permute-start | bytes 1572872 | tf_op jit(solution)/shard_map/ppermute | solution.py:38
  154.7 45.4 %collective-permute-start.9 = (bf16[8,32,2048]{2,1,0:T(8,128)(2,1)}, bf16[8,32,2048]{2,1,0:T(8,128)(2,1)}, u32[]{:S(2)}, u32[]{:S(2)}) collective-permute-start(bf16[8,32,2048]{2,1,0:T(8,128)(2,1)} %pad_maximum_fusion.8.refs_0_), channel_id=1, source_target_pairs={{0,1},{1,0},{2,3},{3,2},{4,5},{5,4},{6,7},{7,6},{8,9},{9,8},{10,11... | collective-permute-start | bytes 3145736 | tf_op jit(solution)/shard_map/ppermute | solution.py:38
  156.4 43.6 %collective-permute-start.3 = (bf16[8,32,2048]{2,1,0:T(8,128)(2,1)}, bf16[8,32,2048]{2,1,0:T(8,128)(2,1)}, u32[]{:S(2)}, u32[]{:S(2)}) collective-permute-start(bf16[8,32,2048]{2,1,0:T(8,128)(2,1)} %pad_maximum_fusion.7.refs_0_), channel_id=1, source_target_pairs={{0,16},{1,17},{2,18},{3,19},{4,20},{5,21},{6,22},{7,23},{8,24},{9,... | collective-permute-start | bytes 3145736 | tf_op jit(solution)/shard_map/ppermute | solution.py:38
  193.2 21.5 %collective-permute-start.14 = (bf16[4,32,4096]{2,1,0:T(8,128)(2,1)S(1)}, bf16[4,32,4096]{2,1,0:T(8,128)(2,1)S(1)}, u32[]{:S(2)}, u32[]{:S(2)}) collective-permute-start(bf16[4,32,4096]{2,1,0:T(8,128)(2,1)S(1)} %pad_maximum_fusion.9), channel_id=1, source_target_pairs={{0,1},{1,0},{2,3},{3,2},{4,5},{5,4},{6,7},{7,6},{8,9},{9,8},{10,11... | collective-permute-start | bytes 3145736 | tf_op jit(solution)/shard_map/ppermute | solution.py:38
  193.5 22.7 %collective-permute-start.10 = (bf16[8,32,2048]{2,1,0:T(8,128)(2,1)S(1)}, bf16[8,32,2048]{2,1,0:T(8,128)(2,1)S(1)}, u32[]{:S(2)}, u32[]{:S(2)}) collective-permute-start(bf16[8,32,2048]{2,1,0:T(8,128)(2,1)S(1)} %copy-done.12), channel_id=1, source_target_pairs={{0,8},{1,9},{2,10},{3,11},{4,12},{5,13},{6,14},{7,15},{8,0},{9,1},... | collective-permute-start | bytes 3145736 | tf_op jit(solution)/shard_map/ppermute | solution.py:38
  200.1 47.9 %collective-permute-start.4 = (bf16[8,32,2048]{2,1,0:T(8,128)(2,1)}, bf16[8,32,2048]{2,1,0:T(8,128)(2,1)}, u32[]{:S(2)}, u32[]{:S(2)}) collective-permute-start(bf16[8,32,2048]{2,1,0:T(8,128)(2,1)} %pad_maximum_fusion.7.refs_0_), channel_id=1, source_target_pairs={{0,8},{1,9},{2,10},{3,11},{4,12},{5,13},{6,14},{7,15},{8,0},{9,1},... | collective-permute-start | bytes 3145736 | tf_op jit(solution)/shard_map/ppermute | solution.py:38
  200.1 34.3 %collective-permute-start.11 = (bf16[8,32,2048]{2,1,0:T(8,128)(2,1)}, bf16[8,32,2048]{2,1,0:T(8,128)(2,1)}, u32[]{:S(2)}, u32[]{:S(2)}) collective-permute-start(bf16[8,32,2048]{2,1,0:T(8,128)(2,1)} %collective-permute-done.9.refs_1_), channel_id=1, source_target_pairs={{0,8},{1,9},{2,10},{3,11},{4,12},{5,13},{6,14},{7,15},{8,0},{9,1},... | collective-permute-start | bytes 3145736 | tf_op jit(solution)/shard_map/ppermute | solution.py:38
  201.5 46.5 %collective-permute-start.5 = (bf16[8,32,2048]{2,1,0:T(8,128)(2,1)}, bf16[8,32,2048]{2,1,0:T(8,128)(2,1)}, u32[]{:S(2)}, u32[]{:S(2)}) collective-permute-start(bf16[8,32,2048]{2,1,0:T(8,128)(2,1)} %collective-permute-done.3.refs_1_), channel_id=1, source_target_pairs={{0,8},{1,9},{2,10},{3,11},{4,12},{5,13},{6,14},{7,15},{8,0},{9,1},... | collective-permute-start | bytes 3145736 | tf_op jit(solution)/shard_map/ppermute | solution.py:38
  214.6 114.1 %collective-permute-start.21 = (bf16[8,128,1024]{2,1,0:T(8,128)(2,1)}, bf16[8,128,1024]{2,1,0:T(8,128)(2,1)}, u32[]{:S(2)}, u32[]{:S(2)}) collective-permute-start(bf16[8,128,1024]{2,1,0:T(8,128)(2,1)} %pad_maximum_fusion.6.refs_4_), channel_id=1, source_target_pairs={{0,1},{1,0},{2,3},{3,2},{4,5},{5,4},{6,7},{7,6},{8,9},{9,8},{10,11... | collective-permute-start | bytes 6291464 | tf_op jit(solution)/shard_map/ppermute | solution.py:38
  217.1 112.1 %collective-permute-start.15 = (bf16[8,32,4096]{2,1,0:T(8,128)(2,1)}, bf16[8,32,4096]{2,1,0:T(8,128)(2,1)}, u32[]{:S(2)}, u32[]{:S(2)}) collective-permute-start(bf16[8,32,4096]{2,1,0:T(8,128)(2,1)} %pad_maximum_fusion.5.refs_0_), channel_id=1, source_target_pairs={{0,16},{1,17},{2,18},{3,19},{4,20},{5,21},{6,22},{7,23},{8,24},{9,... | collective-permute-start | bytes 6291464 | tf_op jit(solution)/shard_map/ppermute | solution.py:38
  234.4 102.7 %collective-permute-start.22 = (bf16[8,128,1024]{2,1,0:T(8,128)(2,1)}, bf16[8,128,1024]{2,1,0:T(8,128)(2,1)}, u32[]{:S(2)}, u32[]{:S(2)}) collective-permute-start(bf16[8,128,1024]{2,1,0:T(8,128)(2,1)} %pad_maximum_fusion.6.refs_4_), channel_id=1, source_target_pairs={{0,8},{1,9},{2,10},{3,11},{4,12},{5,13},{6,14},{7,15},{8,0},{9,1},... | collective-permute-start | bytes 6291464 | tf_op jit(solution)/shard_map/ppermute | solution.py:38
  248.0 89.1 %collective-permute-start.16 = (bf16[8,32,4096]{2,1,0:T(8,128)(2,1)}, bf16[8,32,4096]{2,1,0:T(8,128)(2,1)}, u32[]{:S(2)}, u32[]{:S(2)}) collective-permute-start(bf16[8,32,4096]{2,1,0:T(8,128)(2,1)} %pad_maximum_fusion.5.refs_0_), channel_id=1, source_target_pairs={{0,8},{1,9},{2,10},{3,11},{4,12},{5,13},{6,14},{7,15},{8,0},{9,1},... | collective-permute-start | bytes 6291464 | tf_op jit(solution)/shard_map/ppermute | solution.py:38
  517.3 104.7 %collective-permute-start.49 = (bf16[16,128,1024]{2,1,0:T(8,128)(2,1)}, bf16[16,128,1024]{2,1,0:T(8,128)(2,1)}, u32[]{:S(2)}, u32[]{:S(2)}) collective-permute-start(bf16[16,128,1024]{2,1,0:T(8,128)(2,1)} %get-tuple-element.45), channel_id=1, source_target_pairs={{0,8},{1,9},{2,10},{3,11},{4,12},{5,13},{6,14},{7,15},{8,0},{9,1},... | collective-permute-start | bytes 12582920 | tf_op jit(solution)/shard_map/ppermute | solution.py:38
  517.8 108.5 %collective-permute-start.44 = (bf16[16,32,4096]{2,1,0:T(8,128)(2,1)}, bf16[16,32,4096]{2,1,0:T(8,128)(2,1)}, u32[]{:S(2)}, u32[]{:S(2)}) collective-permute-start(bf16[16,32,4096]{2,1,0:T(8,128)(2,1)} %get-tuple-element.43), channel_id=1, source_target_pairs={{0,8},{1,9},{2,10},{3,11},{4,12},{5,13},{6,14},{7,15},{8,0},{9,1},... | collective-permute-start | bytes 12582920 | tf_op jit(solution)/shard_map/ppermute | solution.py:38
  518.8 64.6 %collective-permute-start.39 = (f32[16,1,224]{2,0,1:T(8,128)S(1)}, f32[16,1,224]{2,0,1:T(8,128)S(1)}, u32[]{:S(2)}, u32[]{:S(2)}) collective-permute-start(f32[16,1,224]{2,0,1:T(8,128)S(1)} %slice_bitcast_fusion.10), channel_id=1, source_target_pairs={{0,8},{1,9},{2,10},{3,11},{4,12},{5,13},{6,14},{7,15},{8,0},{9,1},... | collective-permute-start | bytes 43016 | tf_op jit(solution)/shard_map/ppermute | solution.py:38
  528.2 69.4 %collective-permute-start.29 = (bf16[16,32,2048]{2,1,0:T(8,128)(2,1)}, bf16[16,32,2048]{2,1,0:T(8,128)(2,1)}, u32[]{:S(2)}, u32[]{:S(2)}) collective-permute-start(bf16[16,32,2048]{2,1,0:T(8,128)(2,1)} %get-tuple-element.38), channel_id=1, source_target_pairs={{0,8},{1,9},{2,10},{3,11},{4,12},{5,13},{6,14},{7,15},{8,0},{9,1},... | collective-permute-start | bytes 6291464 | tf_op jit(solution)/shard_map/ppermute | solution.py:38
  557.5 24.9 %collective-permute-start.26 = (f32[4,1,192]{2,0,1:T(4,128)S(1)}, f32[4,1,192]{2,0,1:T(4,128)S(1)}, u32[]{:S(2)}, u32[]{:S(2)}) collective-permute-start(f32[4,1,192]{2,0,1:T(4,128)S(1)} %slice.460), channel_id=1, source_target_pairs={{0,16},{1,17},{2,18},{3,19},{4,20},{5,21},{6,22},{7,23},{8,24},{9,... | collective-permute-start | bytes 9224 | tf_op jit(solution)/shard_map/ppermute | solution.py:38
  582.5 19.3 %collective-permute-start.34 = (bf16[16,32,2048]{2,1,0:T(8,128)(2,1)}, bf16[16,32,2048]{2,1,0:T(8,128)(2,1)S(1)}, u32[]{:S(2)}, u32[]{:S(2)}) collective-permute-start(bf16[16,32,2048]{2,1,0:T(8,128)(2,1)} %get-tuple-element.40), channel_id=1, source_target_pairs={{0,8},{1,9},{2,10},{3,11},{4,12},{5,13},{6,14},{7,15},{8,0},{9,1},... | collective-permute-start | bytes 6291464 | tf_op jit(solution)/shard_map/ppermute | solution.py:38
  600.9 19.0 %collective-permute-start.30 = (bf16[8,32,2048]{2,1,0:T(8,128)(2,1)S(1)}, bf16[8,32,2048]{2,1,0:T(8,128)(2,1)S(1)}, u32[]{:S(2)}, u32[]{:S(2)}) collective-permute-start(bf16[8,32,2048]{2,1,0:T(8,128)(2,1)S(1)} %slice.468), channel_id=1, source_target_pairs={{0,16},{1,17},{2,18},{3,19},{4,20},{5,21},{6,22},{7,23},{8,24},{9,... | collective-permute-start | bytes 3145736 | tf_op jit(solution)/shard_map/ppermute | solution.py:38
  602.7 28.9 %collective-permute-start.35 = (bf16[8,32,2048]{2,1,0:T(8,128)(2,1)S(1)}, bf16[8,32,2048]{2,1,0:T(8,128)(2,1)S(1)}, u32[]{:S(2)}, u32[]{:S(2)}) collective-permute-start(bf16[8,32,2048]{2,1,0:T(8,128)(2,1)S(1)} %slice.476), channel_id=1, source_target_pairs={{0,1},{1,0},{2,3},{3,2},{4,5},{5,4},{6,7},{7,6},{8,9},{9,8},{10,11... | collective-permute-start | bytes 3145736 | tf_op jit(solution)/shard_map/ppermute | solution.py:38
  625.7 59.9 %collective-permute-start.50 = (bf16[8,128,1024]{2,1,0:T(8,128)(2,1)S(1)}, bf16[8,128,1024]{2,1,0:T(8,128)(2,1)S(1)}, u32[]{:S(2)}, u32[]{:S(2)}) collective-permute-start(bf16[8,128,1024]{2,1,0:T(8,128)(2,1)S(1)} %slice.509), channel_id=1, source_target_pairs={{0,1},{1,0},{2,3},{3,2},{4,5},{5,4},{6,7},{7,6},{8,9},{9,8},{10,11... | collective-permute-start | bytes 6291464 | tf_op jit(solution)/shard_map/ppermute | solution.py:38
  631.4 56.1 %collective-permute-start.45 = (bf16[8,32,4096]{2,1,0:T(8,128)(2,1)S(1)}, bf16[8,32,4096]{2,1,0:T(8,128)(2,1)S(1)}, u32[]{:S(2)}, u32[]{:S(2)}) collective-permute-start(bf16[8,32,4096]{2,1,0:T(8,128)(2,1)S(1)} %slice.500), channel_id=1, source_target_pairs={{0,16},{1,17},{2,18},{3,19},{4,20},{5,21},{6,22},{7,23},{8,24},{9,... | collective-permute-start | bytes 6291464 | tf_op jit(solution)/shard_map/ppermute | solution.py:38
  632.1 50.8 %collective-permute-start.36 = (bf16[4,32,2048]{2,1,0:T(8,128)(2,1)S(1)}, bf16[4,32,2048]{2,1,0:T(8,128)(2,1)S(1)}, u32[]{:S(2)}, u32[]{:S(2)}) collective-permute-start(bf16[4,32,2048]{2,1,0:T(8,128)(2,1)S(1)} %slice.478), channel_id=1, source_target_pairs={{0,16},{1,17},{2,18},{3,19},{4,20},{5,21},{6,22},{7,23},{8,24},{9,... | collective-permute-start | bytes 1572872 | tf_op jit(solution)/shard_map/ppermute | solution.py:38
  635.5 49.4 %collective-permute-start.32 = (bf16[2,32,2048]{2,1,0:T(8,128)(2,1)S(1)}, bf16[2,32,2048]{2,1,0:T(8,128)(2,1)S(1)}, u32[]{:S(2)}, u32[]{:S(2)}) collective-permute-start(bf16[2,32,2048]{2,1,0:T(8,128)(2,1)S(1)} %slice.472), channel_id=1, source_target_pairs={{0,4},{1,5},{2,6},{3,7},{4,0},{5,1},{6,2},{7,3},{8,12},{9,13},{10,... | collective-permute-start | bytes 786440 | tf_op jit(solution)/shard_map/ppermute | solution.py:38
  688.5 19.3 %collective-permute-start.46 = (bf16[4,32,4096]{2,1,0:T(8,128)(2,1)S(1)}, bf16[4,32,4096]{2,1,0:T(8,128)(2,1)S(1)}, u32[]{:S(2)}, u32[]{:S(2)}) collective-permute-start(bf16[4,32,4096]{2,1,0:T(8,128)(2,1)S(1)} %slice.502), channel_id=1, source_target_pairs={{0,1},{1,0},{2,3},{3,2},{4,5},{5,4},{6,7},{7,6},{8,9},{9,8},{10,11... | collective-permute-start | bytes 3145736 | tf_op jit(solution)/shard_map/ppermute | solution.py:38
  703.4 38.1 %collective-permute-start.52 = (bf16[2,128,1024]{2,1,0:T(8,128)(2,1)S(1)}, bf16[2,128,1024]{2,1,0:T(8,128)(2,1)S(1)}, u32[]{:S(2)}, u32[]{:S(2)}) collective-permute-start(bf16[2,128,1024]{2,1,0:T(8,128)(2,1)S(1)} %slice.513), channel_id=1, source_target_pairs={{0,4},{1,5},{2,6},{3,7},{4,0},{5,1},{6,2},{7,3},{8,12},{9,13},{10,... | collective-permute-start | bytes 1572872 | tf_op jit(solution)/shard_map/ppermute | solution.py:38
  708.2 44.6 %collective-permute-start.47 = (bf16[2,32,4096]{2,1,0:T(8,128)(2,1)S(1)}, bf16[2,32,4096]{2,1,0:T(8,128)(2,1)S(1)}, u32[]{:S(2)}, u32[]{:S(2)}) collective-permute-start(bf16[2,32,4096]{2,1,0:T(8,128)(2,1)S(1)} %slice.504), channel_id=1, source_target_pairs={{0,4},{1,5},{2,6},{3,7},{4,0},{5,1},{6,2},{7,3},{8,12},{9,13},{10,... | collective-permute-start | bytes 1572872 | tf_op jit(solution)/shard_map/ppermute | solution.py:38
  (78 other events, 1444.9 us)

commit v2 on v1

--- a/solution.py
+++ b/solution.py
@@ -28,156 +28,208 @@
 vmem_most = 60 * 1024 * 1024
 
 
+def cost(micros):
+    return pl.CostEstimate(flops=int(micros * 1e9), bytes_accessed=0, transcendentals=0)
+
+
 def log2(n):
     return n.bit_length() - 1
 
 
-def swap(value, bit, sizes):
+def swap(value, mask, sizes):
     count = sizes[0] * sizes[1]
-    pairs = [(i, i ^ (1 << bit)) for i in range(count)]
-    return lax.ppermute(value, ("dp", "fsdp"), pairs)
+    return lax.ppermute(value, ("dp", "fsdp"), [(i, i ^ mask) for i in range(count)])
 
 
 def bit_orders(sizes):
     inner, outer = log2(sizes[1]), log2(sizes[0])
-    core = inner
     line = list(range(1, inner))
     cross = [0]
     other = list(range(inner + 1, inner + outer))
-    return core, line + cross + other, line + other + cross
-
-
-def gather_pieces(shard, order, core, sizes):
-    held = shard[None]
+    return inner, line, (cross + other, other + cross)
+
+
+def spread(bits):
     rel = [0]
-    for bit in order[:-1]:
-        held = jnp.concatenate([held, swap(held, bit, sizes)], axis=0)
+    for bit in bits:
         rel = rel + [p | (1 << bit) for p in rel]
-    last = order[-1]
-    pieces = [(held, rel), (swap(held, last, sizes), [p | (1 << last) for p in rel])]
-    pieces += [(swap(v, core, sizes), [p | (1 << core) for p in q]) for v, q in pieces]
-    return pieces
-
-
-def assemble_kernel(rels, rows, me_ref, *refs):
-    pieces, out, sem = refs[: len(rels)], refs[len(rels)], refs[len(rels) + 1]
+    return rel
+
+
+def gather_line(shard, line, sizes):
+    rel = spread(line)
+    held = [shard[None]] + [swap(shard[None], p, sizes) for p in rel[1:]]
+    half = len(rel) // 2
+    return [
+        [(jnp.concatenate(held[at : at + half], axis=0), rel[at : at + half])]
+        for at in (0, half)
+    ]
+
+
+def gather_doubling(shard, line, sizes):
+    held, rel = shard[None], [0]
+    for bit in line[:-1]:
+        held = jnp.concatenate([held, swap(held, 1 << bit, sizes)], axis=0)
+        rel = rel + [p | (1 << bit) for p in rel]
+    return [[(held, rel)], moved([(held, rel)], line[-1], sizes)]
+
+
+def moved(pieces, bit, sizes):
+    return [(swap(v, 1 << bit, sizes), [p | (1 << bit) for p in q]) for v, q in pieces]
+
+
+def relatives(line, orders, core):
+    low, top = line[:-1], 1 << line[-1]
+    rel = spread(low + orders[0]) + [p | top for p in spread(low + orders[1])]
+    return rel, [p | (1 << core) for p in rel]
+
+
+def reduce_start(own, taken, orders, sizes, small=None):
+    half = own.shape[0] // 2
+    found = []
+    for at, order in zip((0, half), orders):
+        kept, came = own[at : at + half], taken[at : at + half]
+        quarter = half // 2
+        pieces = []
+        for low in (0, quarter):
+            total = kept[low : low + quarter].astype(f32) + came[low : low + quarter].astype(f32)
+            if small is not None:
+                total = jnp.concatenate([total, small[at + low : at + low + quarter]], axis=2)
+            pieces.append(total.astype(own.dtype))
+        held, sent = pieces
+        found.append((held, swap(sent, 1 << order[-1], sizes), sent))
+    return found
+
+
+def reduce_step(kept, taken, mask, sizes):
+    kind = kept.dtype
+    half = kept.shape[0] // 2
+    sent = (kept[half:].astype(f32) + taken[half:].astype(f32)).astype(kind)
+    held = (kept[:half].astype(f32) + taken[:half].astype(f32)).astype(kind)
+    return held, swap(sent, mask, sizes), sent
+
+
+def reduce_next(groups, orders, step, sizes):
+    return [
+        reduce_step(*group, 1 << order[-1 - step], sizes) for group, order in zip(groups, orders)
+    ]
+
+
+def after_pieces(pieces, *others):
+    return [(after(v, *others), q) for v, q in pieces]
+
+
+def line_parts(groups):
+    return [
+        kept[n].astype(f32) + taken[n].astype(f32)
+        for kept, taken in groups
+        for n in range(kept.shape[0])
+    ]
+
+
+def reduce_line(parts, line, sizes):
+    total = parts[0]
+    for part, p in zip(parts[1:], spread(line)[1:]):
+        total = total + swap(part, p, sizes).astype(f32)
+    return total
+
+
+def after_kernel(*refs):
+    del refs
+
+
+def after(value, *others):
+    anywhere = pl.BlockSpec(memory_space=pl.ANY)
+    return pl.pallas_call(
+        after_kernel,
+        out_shape=jax.ShapeDtypeStruct(value.shape, value.dtype),
+        in_specs=[anywhere] * (1 + len(others)),
+        out_specs=anywhere,
+        input_output_aliases={0: 0},
+        cost_estimate=cost(0),
+    )(value, *others)
+
+
+def assemble_kernel(rels, parts, me_ref, *refs):
+    pieces, refs = refs[: len(rels)], refs[len(rels) :]
+    outs, sems = refs[: len(parts)], refs[-1]
     me = me_ref[0]
-    copies = []
-    for piece, rel in zip(pieces, rels):
-        for at, p in enumerate(rel):
-            owner = lax.bitwise_xor(me, p)
-            start = pl.multiple_of(owner * rows, rows)
-            copies.append(pltpu.make_async_copy(piece.at[at], out.at[pl.ds(start, rows)], sem))
-    for copy in copies:
-        copy.start()
-    pltpu.make_async_copy(out, out, sem).wait()
-
-
-def assemble(pieces, me):
+    for k, (top, height, left, cols) in enumerate(parts):
+        for piece, rel in zip(pieces, rels):
+            for at, p in enumerate(rel):
+                start = pl.multiple_of(lax.bitwise_xor(me, p) * height, height)
+                pltpu.make_async_copy(
+                    piece.at[at, pl.ds(top, height), pl.ds(left, cols)],
+                    outs[k].at[pl.ds(start, height)],
+                    sems.at[k],
+                ).start()
+    for k, out in enumerate(outs):
+        pltpu.make_async_copy(out, out, sems.at[k]).wait()
+
+
+def assemble(pieces, me, parts):
     rels = [q for _, q in pieces]
     count = sum(len(q) for q in rels)
-    _, rows, cols = pieces[0][0].shape
+    total = sum(h * c for _, h, _, c in parts)
     return pl.pallas_call(
-        functools.partial(assemble_kernel, rels, rows),
-        out_shape=jax.ShapeDtypeStruct((count * rows, cols), pieces[0][0].dtype),
+        functools.partial(assemble_kernel, rels, parts),
+        out_shape=[jax.ShapeDtypeStruct((count * h, c), bf16) for _, h, _, c in parts],
         in_specs=[pl.BlockSpec(memory_space=pltpu.SMEM)]
         + [pl.BlockSpec(memory_space=pl.ANY)] * len(pieces),
-        scratch_shapes=[pltpu.SemaphoreType.DMA],
+        scratch_shapes=[pltpu.SemaphoreType.DMA((len(parts),))],
         compiler_params=pltpu.CompilerParams(vmem_limit_bytes=vmem_most),
-        cost_estimate=pl.CostEstimate(
-            flops=0, bytes_accessed=4 * count * rows * cols, transcendentals=0
-        ),
+        cost_estimate=cost(1.5),
     )(me, *[v for v, _ in pieces])
 
 
-def split_kernel(rels, rows, me_ref, whole, *refs):
-    outs, sem = refs[: len(rels)], refs[len(rels)]
-    me = me_ref[0]
-    copies = []
-    for piece, rel in zip(outs, rels):
-        for at, p in enumerate(rel):
-            owner = lax.bitwise_xor(me, p)
-            start = pl.multiple_of(owner * rows, rows)
-            copies.append(pltpu.make_async_copy(whole.at[pl.ds(start, rows)], piece.at[at], sem))
-    for copy in copies:
-        copy.start()
-    pltpu.make_async_copy(whole, whole, sem).wait()
-
-
-def relatives(order, core):
-    rel = [0]
-    for bit in order:
-        rel = rel + [p | (1 << bit) for p in rel]
-    return rel, [p | (1 << core) for p in rel]
-
-
-def split(whole, order, core, me):
-    own, other = relatives(order, core)
-    rows = whole.shape[0] // (2 * len(own))
-    return pl.pallas_call(
-        functools.partial(split_kernel, (own, other), rows),
-        out_shape=(jax.ShapeDtypeStruct((len(own), rows, whole.shape[1]), whole.dtype),) * 2,
-        in_specs=[
-            pl.BlockSpec(memory_space=pltpu.SMEM),
-            pl.BlockSpec(memory_space=pltpu.VMEM),
-        ],
-        out_specs=(pl.BlockSpec(memory_space=pl.ANY),) * 2,
-        scratch_shapes=[pltpu.SemaphoreType.DMA],
-        compiler_params=pltpu.CompilerParams(vmem_limit_bytes=vmem_most),
-        cost_estimate=pl.CostEstimate(flops=0, bytes_accessed=4 * whole.size, transcendentals=0),
-    )(me, whole)
-
-
-def reduce_pieces(own, other, order, core, sizes):
-    kind = own.dtype
-    taken = swap(other, core, sizes)
-    kept = own
-    for bit in reversed(order):
-        half = kept.shape[0] // 2
-        total = kept.astype(f32) + taken.astype(f32)
-        sent = total[half:].astype(kind)
-        kept = total[:half].astype(kind)
-        taken = swap(sent, bit, sizes)
-    return (kept.astype(f32) + taken.astype(f32))[0]
-
-
-def gather_small(parts):
-    flat = jnp.concatenate([v.reshape(-1) for v in parts])
-    lines = -(-flat.size // (16 * 128)) * 16
-    flat = jnp.pad(flat, (0, lines * 128 - flat.size)).reshape(lines, 128)
-    whole = lax.all_gather(flat, ("dp", "fsdp"), axis=0, tiled=True).reshape(-1, lines * 128)
-    found, at = [], 0
+def pack_small(parts, rows):
+    def fill(blocks):
+        blocks = [jnp.pad(v, ((0, 0), (0, 128 - v.shape[1]))) for v in blocks]
+        used = sum(v.shape[0] for v in blocks)
+        return jnp.concatenate(blocks + [jnp.zeros((rows - used, 128), bf16)], axis=0)
+
+    flat = fill([v[None] for v in parts if v.ndim == 1])
+    return jnp.concatenate([flat] + [fill([v]) for v in parts if v.ndim == 2], axis=1)
+
+
+def unpack_small(whole, rows, parts):
+    whole = whole.reshape(-1, rows, whole.shape[1]).astype(f32)
+    found, at, left = [], 0, 128
     for v in parts:
-        block = whole[:, at : at + v.size]
+        size = v.shape[-1]
         if v.ndim == 2:
-            block = block.reshape(-1, v.shape[0], v.shape[1]).swapaxes(0, 1)
+            block = whole[:, : v.shape[0], left : left + size].swapaxes(0, 1)
             found.append(block.reshape(v.shape[0], -1))
+            left += 128
         else:
-            found.append(block.reshape(-1))
-        at = at + v.size
+            found.append(whole[:, at, :size].reshape(-1))
+            at += 1
     return found
 
 
-def reduce_small(parts, order, core, sizes, me):
-    count = sizes[0] * sizes[1]
-    rows = [
+def small_units(parts, rows, where, me):
+    count = sum(len(q) for q in where)
+    blocks = [
         v.reshape(count, -1)
         if v.ndim == 1
         else v.reshape(v.shape[0], count, -1).swapaxes(0, 1).reshape(count, -1)
         for v in parts
     ]
-    flat = jnp.concatenate(rows, axis=1)
-    own, other = relatives(order, core)
-    index = lax.bitwise_xor(jnp.asarray(own + other, jnp.int32), me[0])
+    flat = jnp.concatenate(blocks, axis=1)
+    flat = jnp.pad(flat, ((0, 0), (0, rows * 128 - flat.shape[1]))).reshape(count, rows, 128)
+    index = lax.bitwise_xor(jnp.asarray(where[0] + where[1], jnp.int32), me[0])
     mixed = jnp.take(flat, index, axis=0)
-    total = reduce_pieces(
-        mixed[: len(own), None], mixed[len(own) :, None], order, core, sizes
-    )[0]
+    return mixed[: count // 2], mixed[count // 2 :]
+
+
+def small_parts(unit, parts, count):
+    flat = unit.reshape(-1)
     found, at = [], 0
-    for v, row in zip(parts, rows):
-        block = total[at : at + row.shape[1]]
+    for v in parts:
+        size = v.size // count
+        block = flat[at : at + size]
         found.append(block if v.ndim == 1 else block.reshape(v.shape[0], -1))
-        at = at + row.shape[1]
+        at = at + size
     return found
 
 
@@ -277,23 +329,34 @@
             lse_ref[0, :, pl.ds(row, PATCH)] = jnp.concatenate(sums, axis=0)
 
 
-def attend(seen, qkv, hide):
+def attend(seen, qkv, hide, pair_lo, pair_hi, kept=None):
     width = qkv.shape[1] // 3
     pairs = width // (2 * HEAD)
     lanes = 2 * HEAD
+    at = pair_lo
+    some = pair_hi - pair_lo
+    kernel = attend_kernel
+    more, alias = [], {}
+    if kept is not None:
+        more, alias = [kept], {5: 0}
+
+        def kernel(seen_ref, q_ref, k_ref, v_ref, hide_ref, kept_ref, *refs):
+            attend_kernel(seen_ref, q_ref, k_ref, v_ref, hide_ref, *refs)
+
     return pl.pallas_call(
-        attend_kernel,
+        kernel,
         grid_spec=pltpu.PrefetchScalarGridSpec(
             num_scalar_prefetch=1,
-            grid=(pairs, FRAMES),
+            grid=(some, FRAMES),
             in_specs=[
-                pl.BlockSpec((ROWS, lanes), lambda h, f, s: (0, h)),
-                pl.BlockSpec((ROWS, lanes), lambda h, f, s: (0, pairs + h)),
-                pl.BlockSpec((ROWS, lanes), lambda h, f, s: (0, 2 * pairs + h)),
+                pl.BlockSpec((ROWS, lanes), lambda h, f, s: (0, at + h)),
+                pl.BlockSpec((ROWS, lanes), lambda h, f, s: (0, at + pairs + h)),
+                pl.BlockSpec((ROWS, lanes), lambda h, f, s: (0, at + 2 * pairs + h)),
                 pl.BlockSpec((ROWS, 2 * FEW), lambda h, f, s: (0, 0)),
-            ],
+            ]
+            + [pl.BlockSpec(memory_space=pl.ANY)] * len(more),
             out_specs=[
-                pl.BlockSpec((ROWS, lanes), lambda h, f, s: (0, h)),
+                pl.BlockSpec((ROWS, lanes), lambda h, f, s: (0, at + h)),
                 pl.BlockSpec((1, 2, BODY), lambda h, f, s: (h, 0, 0)),
                 pl.BlockSpec((1, 1, 2 * FEW), lambda h, f, s: (h, 0, 0)),
             ],
@@ -301,14 +364,13 @@
         ),
         out_shape=(
             jax.ShapeDtypeStruct((ROWS, width), bf16),
-            jax.ShapeDtypeStruct((pairs, 2, BODY), f32),
-            jax.ShapeDtypeStruct((pairs, 1, 2 * FEW), f32),
+            jax.ShapeDtypeStruct((some, 2, BODY), f32),
+            jax.ShapeDtypeStruct((some, 1, 2 * FEW), f32),
         ),
+        input_output_aliases=alias,
         compiler_params=pltpu.CompilerParams(vmem_limit_bytes=vmem_most),
-        cost_estimate=pl.CostEstimate(
-            flops=ROWS * ROWS * width * 4, bytes_accessed=8 * ROWS * width, transcendentals=0
-        ),
-    )(seen, qkv, qkv, qkv, hide)
+        cost_estimate=cost(1.6 * some),
+    )(seen, qkv, qkv, qkv, hide, *more)
 
 
 def unturn(x, cosine, sine, partner):
@@ -389,34 +451,46 @@
         out_ref[2] = dv[...].astype(bf16)
 
 
-def attend_back(seen, qkv, attended, grad, lse, few, hide, cosine, sine, partner, pair_lo, pair_hi):
+def attend_back(
+    seen, qkv, attended, grad, lse, few, hide, cosine, sine, partner, pair_lo, pair_hi, kept=None
+):
     width = qkv.shape[1] // 3
     pairs = width // (2 * HEAD)
     lanes = 2 * HEAD
     at = pair_lo
+    some = pair_hi - pair_lo
+    inner = functools.partial(attend_back_kernel, 1.0 / math.sqrt(HEAD))
+    kernel = inner
+    more, alias = [], {}
+    if kept is not None:
+        more, alias = [kept], {12: 0}
+
+        def kernel(*refs):
+            inner(*refs[:12], *refs[13:])
 
     def whole(h, f, s):
         return (0, 0)
 
     return pl.pallas_call(
-        functools.partial(attend_back_kernel, 1.0 / math.sqrt(HEAD)),
+        kernel,
         grid_spec=pltpu.PrefetchScalarGridSpec(
             num_scalar_prefetch=1,
-            grid=(pair_hi - pair_lo, FRAMES),
+            grid=(some, FRAMES),
             in_specs=[
                 pl.BlockSpec((ROWS, lanes), lambda h, f, s: (0, at + h)),
                 pl.BlockSpec((ROWS, lanes), lambda h, f, s: (0, at + pairs + h)),
                 pl.BlockSpec((ROWS, lanes), lambda h, f, s: (0, at + 2 * pairs + h)),
                 pl.BlockSpec((ROWS, lanes), lambda h, f, s: (0, at + h)),
                 pl.BlockSpec((ROWS, lanes), lambda h, f, s: (0, at + h)),
-                pl.BlockSpec((1, 2, BODY), lambda h, f, s: (at + h, 0, 0)),
-                pl.BlockSpec((1, 1, 2 * FEW), lambda h, f, s: (at + h, 0, 0)),
+                pl.BlockSpec((1, 2, BODY), lambda h, f, s: (h, 0, 0)),
+                pl.BlockSpec((1, 1, 2 * FEW), lambda h, f, s: (h, 0, 0)),
                 pl.BlockSpec((ROWS, 2 * FEW), whole),
                 pl.BlockSpec((ROWS, lanes), whole),
                 pl.BlockSpec((ROWS, lanes), whole),
                 pl.BlockSpec((lanes, lanes), whole),
-            ],
-            out_specs=pl.BlockSpec((3, ROWS, lanes), lambda h, f, s: (0, 0, h)),
+            ]
+            + [pl.BlockSpec(memory_space=pl.ANY)] * len(more),
+            out_specs=pl.BlockSpec((3, ROWS, lanes), lambda h, f, s: (0, 0, at + h)),
             scratch_shapes=[
                 pltpu.VMEM((lanes, ROWS), bf16),
                 pltpu.VMEM((ROWS, lanes), f32),
@@ -424,12 +498,11 @@
                 pltpu.VMEM((ROWS, lanes), f32),
             ],
         ),
-        out_shape=jax.ShapeDtypeStruct((3, ROWS, (pair_hi - pair_lo) * lanes), bf16),
+        out_shape=jax.ShapeDtypeStruct((3, ROWS, width), bf16),
+        input_output_aliases=alias,
         compiler_params=pltpu.CompilerParams(vmem_limit_bytes=vmem_most),
-        cost_estimate=pl.CostEstimate(
-            flops=ROWS * ROWS * width * 10, bytes_accessed=16 * ROWS * width, transcendentals=0
-        ),
-    )(seen, qkv, qkv, qkv, attended, grad, lse, few, hide, cosine, sine, partner)
+        cost_estimate=cost(1.9 * some),
+    )(seen, qkv, qkv, qkv, attended, grad, lse, few, hide, cosine, sine, partner, *more)
 
 
 def project_kernel(scale, x_ref, w_ref, b_ref, cos_ref, sin_ref, part_ref, out_ref):
@@ -477,28 +550,32 @@
         out_specs=pl.BlockSpec((rows, cols), lambda j: (0, j)),
         out_shape=jax.ShapeDtypeStruct((rows, w.shape[1]), bf16),
         compiler_params=pltpu.CompilerParams(vmem_limit_bytes=vmem_most),
-        cost_estimate=pl.CostEstimate(
-            flops=3 * rows * w.size, bytes_accessed=2 * (x.size + w.size + 3 * x.size), transcendentals=0
-        ),
+        cost_estimate=cost(6),
     )(x, w, bias, cosine, sine, partner)
 
 
-def turn_tables(frame_ids, rows_of):
-    index = jnp.asarray(rows_of, jnp.int32)
-    time = frame_ids[jnp.asarray([f * FRAME_ROWS for f in range(FRAMES)])]
-    patch = jnp.maximum(index % FRAME_ROWS - 2, 0)
-    height = patch // GRID
-    breadth = patch % GRID
-    time = jnp.repeat(time, PATCH)
-    time = jnp.concatenate([time, jnp.repeat(time[::PATCH], 2), jnp.zeros((EXTRA - FEW,), jnp.int32)])
-    cosine, sine = [], []
-    for position, part in zip((time, height, breadth), part_sizes):
+def turn_tables(frame_ids):
+    frequency, which, sign = [], [], []
+    for kind, part in enumerate(part_sizes):
         half = part // 2
-        frequency = 10000.0 ** (-jnp.arange(half).astype(f32) / half)
-        angles = position.astype(f32)[:, None] * frequency[None, :]
-        cosine += [jnp.cos(angles)] * 2
-        sine += [-jnp.sin(angles), jnp.sin(angles)]
-    return jnp.concatenate(cosine * 2, axis=1), jnp.concatenate(sine * 2, axis=1)
+        frequency += [10000.0 ** (-i / half) for i in range(half)] * 2
+        which += [kind] * part
+        sign += [-1.0] * half + [1.0] * half
+    frequency = jnp.asarray(np.tile(np.array(frequency, np.float32), 2))
+    which = np.tile(np.array(which), 2)
+    sign = np.tile(np.array(sign, np.float32), 2)
+    time = frame_ids[:: FRAME_ROWS].astype(f32)[:, None] * frequency
+    place = np.arange(GRID, dtype=np.float32)[:, None] * frequency
+
+    def table(of, empty):
+        by_time, by_place = of(time), of(place)
+        still = jnp.full((FRAMES, 2, which.size), empty, f32)
+        patches = jnp.where(which == 1, by_place[:, None], by_place[None]).reshape(1, PATCH, -1)
+        patches = jnp.where(which == 0, by_time[:, None], patches).reshape(BODY, -1)
+        few = jnp.where(which == 0, by_time[:, None], still).reshape(FEW, -1)
+        return jnp.concatenate([patches, few, jnp.zeros_like(few)], axis=0)
+
+    return table(jnp.cos, 1.0), table(lambda v: jnp.sin(v) * sign, 0.0)
 
 
 def partner_matrix():
@@ -531,14 +608,8 @@
     return jnp.tile(jnp.where(allowed, 0.0, masked_value), (1, 2))
 
 
-def row_order():
-    patches = [f * FRAME_ROWS + 2 + j for f in range(FRAMES) for j in range(PATCH)]
-    first = [f * FRAME_ROWS + j for f in range(FRAMES) for j in range(2)]
-    return np.array(patches + first + [0] * (EXTRA - FEW))
-
-
-def place(p, order, core):
-    own, other = relatives(order, core)
+def place(p, line, orders, core):
+    own, other = relatives(line, orders, core)
     return (1, other.index(p)) if p in other else (0, own.index(p))
 
 
@@ -550,15 +621,13 @@
 
 
 def feed_kernel(
-    up_rels, down_rels, up_order, down_order, core, me_ref, x_ref, g_ref, bias_ref, shift_ref, mid_ref, *refs
+    rels, where, me_ref, x_ref, g_ref, bias_ref, shift_ref, mid_ref, up_ref, *refs
 ):
-    n_up, n_down = len(up_rels), len(down_rels)
-    up_refs, refs = refs[:n_up], refs[n_up:]
-    down_refs, refs = refs[:n_down], refs[n_down:]
+    pieces, refs = refs[: len(rels)], refs[len(rels) :]
     out_ref, gx_ref, gb_ref = refs[:3]
-    du_refs, dd_refs = refs[3:5], refs[5:7]
-    wu, wd, su, sd, acc, xt, act, gup, in_sem, out_sem, mid_sem = refs[7:]
-    count = sum(len(q) for q in up_rels)
+    grads = refs[3:5]
+    wu, wd, su, sd, acc, xt, act, gup, in_sem, out_sem, mid_sem = refs[5:]
+    count = sum(len(q) for q in rels)
     blocks = FEED_BLOCKS
     each = count // blocks
     shift = each.bit_length() - 1
@@ -568,6 +637,8 @@
     cols = wu.shape[2]
     rows = width // count
     part = cols // each
+    hidden = blocks * cols
+    stacks = part // rows
     slot = lax.rem(i, 2)
 
     def group(j):
@@ -575,22 +646,20 @@
 
     def fetch(j, to):
         at = pl.multiple_of(group(j) * cols, cols)
-        for p in range(count):
-            c, n = find_piece(up_rels, p)
-            start = pl.multiple_of(lax.bitwise_xor(me, p) * rows, rows)
-            pltpu.make_async_copy(
-                up_refs[c].at[n, :, pl.ds(at, cols)], wu.at[to, pl.ds(start, rows), :], in_sem.at[0, to]
-            ).start()
+        pltpu.make_async_copy(up_ref.at[:, pl.ds(at, cols)], wu.at[to], in_sem.at[0, to]).start()
         for k in range(blocks):
 
             @pl.when(j == k)
             def _():
                 for p in range(each):
-                    c, n = find_piece(down_rels, (k << shift) | p)
+                    c, n = find_piece(rels, (k << shift) | p)
                     start = pl.multiple_of(lax.bitwise_xor(me & (each - 1), p) * part, part)
-                    pltpu.make_async_copy(
-                        down_refs[c].at[n], wd.at[to, pl.ds(start, part), :], in_sem.at[1, to]
-                    ).start()
+                    for q in range(stacks):
+                        pltpu.make_async_copy(
+                            pieces[c].at[n, :, pl.ds(q * width, width)],
+                            wd.at[to, pl.ds(start + q * rows, rows), :],
+                            in_sem.at[1, to],
+                        ).start()
 
     middle = pltpu.make_async_copy(mid_ref, acc, mid_sem)
 
@@ -640,21 +709,26 @@
     su[slot] = dot_n(xt[...], gup[...]).astype(bf16)
     at = pl.multiple_of(group(i) * cols, cols)
     for p in range(count):
-        c, n = place(p, up_order, core)
+        c, n = place(p, *where)
         start = pl.multiple_of(lax.bitwise_xor(me, p) * rows, rows)
         pltpu.make_async_copy(
-            su.at[slot, pl.ds(start, rows), :], du_refs[c].at[n, :, pl.ds(at, cols)], out_sem.at[0, slot]
+            su.at[slot, pl.ds(start, rows), :],
+            grads[c].at[n, :, pl.ds(at, cols)],
+            out_sem.at[0, slot],
         ).start()
     for k in range(blocks):
 
         @pl.when(i == k)
         def _():
             for p in range(each):
-                c, n = place((k << shift) | p, down_order, core)
+                c, n = place((k << shift) | p, *where)
                 start = pl.multiple_of(lax.bitwise_xor(me & (each - 1), p) * part, part)
-                pltpu.make_async_copy(
-                    sd.at[slot, pl.ds(start, part), :], dd_refs[c].at[n], out_sem.at[1, slot]
-                ).start()
+                for q in range(stacks):
+                    pltpu.make_async_copy(
+                        sd.at[slot, pl.ds(start + q * rows, rows), :],
+                        grads[c].at[n, :, pl.ds(hidden + q * width, width)],
+                        out_sem.at[1, slot],
+                    ).start()
 
     @pl.when(i == blocks - 1)
     def _():
@@ -667,10 +741,9 @@
 FEED_BLOCKS = 8
 
 
-def feed(x, grad, middle, bias, shift, up_pieces, down_pieces, up_order, down_order, core, me):
-    up_rels = [q for _, q in up_pieces]
-    down_rels = [q for _, q in down_pieces]
-    count = sum(len(q) for q in up_rels)
+def feed(x, grad, middle, bias, shift, up, pieces, line, orders, core, me):
+    rels = [q for _, q in pieces]
+    count = sum(len(q) for q in rels)
     tokens, width = x.shape
     hidden = bias.shape[1]
     cols = hidden // FEED_BLOCKS
@@ -685,7 +758,7 @@
     once = pl.Buffered(1)
     anywhere = pl.BlockSpec(memory_space=pl.ANY)
     return pl.pallas_call(
-        functools.partial(feed_kernel, up_rels, down_rels, up_order, down_order, core),
+        functools.partial(feed_kernel, rels, (line, orders, core)),
         grid_spec=pltpu.PrefetchScalarGridSpec(
             num_scalar_prefetch=1,
             grid=(FEED_BLOCKS,),
@@ -695,14 +768,15 @@
                 pl.BlockSpec((1, cols), block),
                 pl.BlockSpec((1, width), whole),
                 anywhere,
+                anywhere,
             ]
-            + [anywhere] * (len(up_pieces) + len(down_pieces)),
+            + [anywhere] * len(pieces),
             out_specs=[
                 pl.BlockSpec((tokens, width), whole, pipeline_mode=once),
                 pl.BlockSpec((tokens, width), whole, pipeline_mode=once),
                 pl.BlockSpec((1, cols), block),
             ]
-            + [anywhere] * 4,
+            + [anywhere] * 2,
             scratch_shapes=[
                 pltpu.VMEM((2, width, cols), bf16),
                 pltpu.VMEM((2, cols, width), bf16),
@@ -722,15 +796,199 @@
             jax.ShapeDtypeStruct((tokens, width), f32),
             jax.ShapeDtypeStruct((1, hidden), f32),
         ]
-        + [jax.ShapeDtypeStruct((count // 2, width // count, hidden), bf16)] * 2
-        + [jax.ShapeDtypeStruct((count // 2, hidden // count, width), bf16)] * 2,
+        + [jax.ShapeDtypeStruct((count // 2, width // count, 2 * hidden), bf16)] * 2,
         compiler_params=pltpu.CompilerParams(vmem_limit_bytes=vmem_most),
-        cost_estimate=pl.CostEstimate(
-            flops=12 * tokens * width * hidden,
-            bytes_accessed=8 * width * hidden + 16 * tokens * width,
-            transcendentals=0,
+        cost_estimate=cost(20),
+    )(me, x, grad, bias, shift, middle, up, *[v for v, _ in pieces])
+
+
+def weight_kernel(where, left, count, me_ref, x_ref, g_ref, *refs):
+    outs, (xt, staged, sem) = refs[-5:-3], refs[-3:]
+    j = pl.program_id(0)
+    me = me_ref[0]
+    slot = lax.rem(j, 2)
+    width, cols = staged.shape[1:]
+    rows = width // count
+
+    @pl.when(j == 0)
+    def _():
+        xt[...] = x_ref[...].T
+
+    @pl.when(j >= 2)
+    def _():
+        pltpu.make_async_copy(staged.at[slot], staged.at[slot], sem.at[slot]).wait()
+
+    staged[slot] = dot_n(xt[...], g_ref[...].reshape(g_ref.shape[-2:])).astype(bf16)
+    at = pl.multiple_of(left + j * cols, cols)
+    for out, rel in zip(outs, where):
+        for n, p in enumerate(rel):
+            start = pl.multiple_of(lax.bitwise_xor(me, p) * rows, rows)
+            pltpu.make_async_copy(
+                staged.at[slot, pl.ds(start, rows), :], out.at[n, :, pl.ds(at, cols)], sem.at[slot]
+            ).start()
+
+    @pl.when(j == pl.num_programs(0) - 1)
+    def _():
+        for s in range(2):
+            pltpu.make_async_copy(staged.at[s], staged.at[s], sem.at[s]).wait()
+
+
+def weight_grad(x, grad, where, left, total, me, into=()):
+    tokens, width = x.shape
+    count = sum(len(q) for q in where)
+    cols = 512
+    deep = grad.ndim == 3
+    found = grad.shape[-1] * (grad.shape[0] if deep else 1)
+    per = grad.shape[-1] // cols
+    if deep:
+        spec = pl.BlockSpec((1, tokens, cols), lambda j, m: (j // per, 0, j % per))
+    else:
+        spec = pl.BlockSpec((tokens, cols), lambda j, m: (0, j))
+    anywhere = pl.BlockSpec(memory_space=pl.ANY)
+    return pl.pallas_call(
+        functools.partial(weight_kernel, where, left, count),
+        grid_spec=pltpu.PrefetchScalarGridSpec(
+            num_scalar_prefetch=1,
+            grid=(found // cols,),
+            in_specs=[pl.BlockSpec((tokens, width), lambda j, m: (0, 0)), spec]
+            + [anywhere] * len(into),
+            out_specs=[anywhere] * 2,
+            scratch_shapes=[
+                pltpu.VMEM((width, tokens), bf16),
+                pltpu.VMEM((2, width, cols), bf16),
+                pltpu.SemaphoreType.DMA((2,)),
+            ],
         ),
-    )(me, x, grad, bias, shift, middle, *[v for v, _ in up_pieces], *[v for v, _ in down_pieces])
+        out_shape=[jax.ShapeDtypeStruct((count // 2, width // count, total), bf16)] * 2,
+        input_output_aliases={3 + i: i for i in range(len(into))},
+        compiler_params=pltpu.CompilerParams(vmem_limit_bytes=vmem_most),
+        cost_estimate=cost(0.5 * found / 512),
+    )(me, x, grad, *into)
+
+
+def sort_kernel(x_ref, g_ref, x_out, g_out, sum_ref, wide):
+    for source, target in ((x_ref, x_out), (g_ref, g_out)):
+        wide[...] = source[...].astype(f32)
+        for f in range(FRAMES):
+            at = f * FRAME_ROWS + 2
+            target[f * PATCH : (f + 1) * PATCH, :] = wide[at : at + PATCH, :].astype(bf16)
+        few = [wide[f * FRAME_ROWS : f * FRAME_ROWS + 2, :] for f in range(FRAMES)]
+        few = jnp.concatenate(few + [jnp.zeros((EXTRA - FEW, wide.shape[1]), f32)], axis=0)
+        target[BODY:ROWS, :] = few.astype(bf16)
+    sum_ref[...] = jnp.sum(wide[...], axis=0, keepdims=True)
+
+
+def sort_rows(x, grad):
+    tokens, width = x.shape
+    return pl.pallas_call(
+        sort_kernel,
+        out_shape=[jax.ShapeDtypeStruct((ROWS, width), bf16)] * 2
+        + [jax.ShapeDtypeStruct((1, width), f32)],
+        scratch_shapes=[pltpu.VMEM((tokens, width), f32)],
+        compiler_params=pltpu.CompilerParams(vmem_limit_bytes=vmem_most),
+        cost_estimate=cost(1),
+    )(x, grad)
+
+
+def unsort_kernel(x_ref, out_ref, *scratch):
+    wide = scratch[0] if scratch else out_ref
+    for f in range(FRAMES):
+        at = f * FRAME_ROWS
+        wide[at + 2 : at + FRAME_ROWS, :] = x_ref[f * PATCH : (f + 1) * PATCH, :].astype(f32)
+    few = x_ref[BODY:ROWS, :].astype(f32)
+    for f in range(FRAMES):
+        wide[f * FRAME_ROWS : f * FRAME_ROWS + 2, :] = few[2 * f : 2 * f + 2]
+    if scratch:
+        out_ref[...] = wide[...].astype(out_ref.dtype)
+
+
+def unsort_rows(x):
+    tokens, width = FRAMES * FRAME_ROWS, x.shape[1]
+    return pl.pallas_call(
+        unsort_kernel,
+        out_shape=jax.ShapeDtypeStruct((tokens, width), x.dtype),
+        scratch_shapes=[] if x.dtype == f32 else [pltpu.VMEM((tokens, width), f32)],
+        compiler_params=pltpu.CompilerParams(vmem_limit_bytes=vmem_most),
+        cost_estimate=cost(1),
+    )(x)
+
+
+def last_kernel(g_ref, w_ref, x_ref, mid_ref, gain_ref, out_ref, gain_out, bias_out, sum_ref, acc):
+    i = pl.program_id(0)
+    g = g_ref[0]
+    more = dot_t(g, w_ref[...])
+
+    @pl.when(i == 0)
+    def _():
+        acc[...] = more
+
+    @pl.when(i > 0)
+    def _():
+        acc[...] += more
+
+    sum_ref[0] = jnp.sum(g.astype(f32), axis=0, keepdims=True)
+
+    @pl.when(i == pl.num_programs(0) - 1)
+    def _():
+        gain = gain_ref[...]
+        gain_sum, bias_sum = 0.0, 0.0
+        spans = [(f * PATCH, PATCH) for f in range(FRAMES)] + [(BODY, EXTRA)]
+        for at, size in spans:
+            rows = slice(at, at + size)
+            x = x_ref[rows, :].astype(f32)
+            center = x - jnp.mean(x, axis=-1, keepdims=True)
+            inverse = lax.rsqrt(jnp.mean(center * center, axis=-1, keepdims=True) + eps_norm)
+            unit = center * inverse
+            grad = acc[rows, :]
+            gain_sum += jnp.sum(grad * unit, axis=0, keepdims=True)
+            bias_sum += jnp.sum(grad, axis=0, keepdims=True)
+            scaled = grad * gain
+            mean_grad = jnp.mean(scaled, axis=-1, keepdims=True)
+            mean_cross = jnp.mean(scaled * unit, axis=-1, keepdims=True)
+            found = mid_ref[rows, :] + inverse * (scaled - mean_grad - unit * mean_cross)
+            if size == PATCH:
+                start = at // PATCH * FRAME_ROWS + 2
+                out_ref[start : start + PATCH, :] = found
+            else:
+                for f in range(FRAMES):
+                    out_ref[f * FRAME_ROWS : f * FRAME_ROWS + 2, :] = found[2 * f : 2 * f + 2]
+        gain_out[...] = gain_sum
+        bias_out[...] = bias_sum
+
+
+def last_step(grad_mixed, w, x, middle, gain):
+    parts, rows, width = grad_mixed.shape
+
+    def whole(i):
+        return (0, 0)
+
+    once = pl.Buffered(1)
+    return pl.pallas_call(
+        last_kernel,
+        grid=(parts,),
+        in_specs=[
+            pl.BlockSpec((1, rows, width), lambda i: (i, 0, 0)),
+            pl.BlockSpec((width, width), lambda i: (0, i)),
+            pl.BlockSpec((rows, width), whole, pipeline_mode=once),
+            pl.BlockSpec((rows, width), whole, pipeline_mode=once),
+            pl.BlockSpec((1, width), whole),
+        ],
+        out_specs=[
+            pl.BlockSpec((FRAMES * FRAME_ROWS, width), whole, pipeline_mode=once),
+            pl.BlockSpec((1, width), whole),
+            pl.BlockSpec((1, width), whole),
+            pl.BlockSpec((1, 1, width), lambda i: (i, 0, 0)),
+        ],
+        out_shape=[
+            jax.ShapeDtypeStruct((FRAMES * FRAME_ROWS, width), f32),
+            jax.ShapeDtypeStruct((1, width), f32),
+            jax.ShapeDtypeStruct((1, width), f32),
+            jax.ShapeDtypeStruct((parts, 1, width), f32),
+        ],
+        scratch_shapes=[pltpu.VMEM((rows, width), f32)],
+        compiler_params=pltpu.CompilerParams(vmem_limit_bytes=vmem_most),
+        cost_estimate=cost(5),
+    )(grad_mixed, w, x, middle, gain)
 
 
 def normalize(values, gain, bias_add):
@@ -747,16 +1005,24 @@
     return scale_inv * (scaled - mean_grad - unit_rows * mean_cross)
 
 
-def sort_rows(x):
-    frames = x.reshape(FRAMES, FRAME_ROWS, -1)
-    few = frames[:, :2].reshape(FEW, -1)
-    return jnp.concatenate([frames[:, 2:].reshape(BODY, -1), few, jnp.zeros_like(few)], axis=0)
-
-
-def unsort_rows(x):
-    patches = x[:BODY].reshape(FRAMES, PATCH, -1)
-    few = x[BODY : BODY + FEW].reshape(FRAMES, 2, -1)
-    return jnp.concatenate([few, patches], axis=1).reshape(FRAMES * FRAME_ROWS, -1)
+def gather_joined(groups, orders, core, sizes):
+    found = []
+    for pieces, order in zip(groups, orders):
+        for bit in order[:-1]:
+            pieces = pieces + moved(pieces, bit, sizes)
+        arrays, rels = zip(*pieces)
+        pieces = [(jnp.concatenate(arrays, axis=0), sum(rels, []))]
+        found += pieces + moved(pieces, order[-1], sizes)
+    return found + moved(found, core, sizes)
+
+
+def gather_rest(groups, orders, core, sizes):
+    found = []
+    for pieces, order in zip(groups, orders):
+        for bit in order:
+            pieces = pieces + moved(pieces, bit, sizes)
+        found += pieces
+    return found + moved(found, core, sizes)
 
 
 def body(
@@ -780,111 +1046,147 @@
     cotangent,
 ):
     width = tokens.shape[1]
+    count = sizes[0] * sizes[1]
     me = (lax.axis_index("dp") * sizes[1] + lax.axis_index("fsdp")).astype(jnp.int32)[None]
-    core, order_a, order_b = bit_orders(sizes)
-    pieces_q = gather_pieces(w_qkv[:, : 2 * width], order_a, core, sizes)
-    pieces_v = gather_pieces(
-        jnp.concatenate([w_qkv[:, 2 * width :], w_out], axis=1), order_b, core, sizes
-    )
-    w_up, w_down, *_ = lax.optimization_barrier((w_up, w_down, pieces_q[0][0], pieces_v[0][0]))
-    pieces_up = gather_pieces(w_up, order_a, core, sizes)
-    pieces_down = gather_pieces(w_down, order_b, core, sizes)
-    gain_one, bias_one, qkv_rows, out_bias, gain_two, bias_two, up_bias, down_bias = [
-        v.astype(f32)
-        for v in gather_small(
-            [ln1_gain, ln1_bias, b_qkv, b_out, ln2_gain, ln2_bias, b_up, b_down]
-        )
-    ]
+    core, line, orders = bit_orders(sizes)
+    where = relatives(line, orders, core)
+    out_matrix = lax.all_gather(w_out, ("dp", "fsdp"), axis=0, tiled=True)
+    up_matrix = lax.all_gather(w_up, ("dp", "fsdp"), axis=0, tiled=True)
+    smalls = [ln1_gain, ln1_bias, b_qkv, b_out, ln2_gain, ln2_bias, b_up, b_down]
+    rows, third = w_qkv.shape
+    first_unit = jnp.concatenate([w_qkv, pack_small(smalls, rows)], axis=1)
+    firsts = gather_line(first_unit, line, sizes)
+    tokens_in, cot, grad_b_down_local = sort_rows(tokens, cotangent)
+    first = gather_joined(firsts, orders, core, sizes)
     seen = seen_frames(episode_offsets[0])
     hide = hidden_few(seen)
-    cosine, sine = turn_tables(frame_ids, row_order())
+    cosine, sine = turn_tables(frame_ids)
     partner = partner_matrix()
-    values_in = sort_rows(tokens).astype(f32)
-    cot = sort_rows(cotangent)
+    values_in = tokens_in.astype(f32)
+    qkv_matrix, whole_small = assemble(
+        first, me, [(0, rows, 0, third), (0, rows, third, first_unit.shape[1] - third)]
+    )
+    gain_one, bias_one, qkv_rows, out_bias, gain_two, bias_two, up_bias, down_bias = unpack_small(
+        whole_small, rows, smalls
+    )
+    stacked = [w_down[at : at + rows] for at in range(0, w_down.shape[0], rows)]
+    second_unit = after(jnp.concatenate(stacked, axis=1), qkv_matrix)
+    seconds = gather_line(second_unit, line, sizes)
     normed_one, unit_one, inv_one = normalize(values_in, gain_one, bias_one)
     normed_one = normed_one.astype(bf16)
-    qk_matrix = assemble(pieces_q, me)
-    vo_matrix = assemble(pieces_v, me)
-    qkv_matrix = jnp.concatenate([qk_matrix, vo_matrix[:, :width]], axis=1)
-    out_matrix = vo_matrix[:, width:]
     qkv = project(normed_one, qkv_matrix, qkv_rows.reshape(1, 3 * width), cosine, sine, partner)
-    attended, lse, few = attend(seen, qkv, hide)
+    pairs = width // (2 * HEAD)
+    seconds = [after_pieces(pieces, qkv) for pieces in seconds]
+    seconds = [
+        [pieces, moved(pieces, order[0], sizes) + moved(pieces, order[1], sizes)]
+        for pieces, order in zip(seconds, orders)
+    ]
+    attended, lse_a, few_a = attend(seen, qkv, hide, 0, pairs // 2)
+    seconds = [[near, after_pieces(far, attended)] for near, far in seconds]
+    found = []
+    for (near, far), order in zip(seconds, orders):
+        pieces = near + far + moved(far[:1], order[1], sizes)
+        for bit in order[2:]:
+            pieces = pieces + moved(pieces, bit, sizes)
+        found.append(pieces)
+    attended, lse_b, few_b = attend(seen, qkv, hide, pairs // 2, pairs, attended)
+    second = []
+    for pieces in found:
+        arrays, rels = zip(*pieces)
+        pieces = [(after(jnp.concatenate(arrays, axis=0), attended), sum(rels, []))]
+        second += pieces + moved(pieces, core, sizes)
+    hidden = w_up.shape[1]
     middle = values_in + jnp.dot(attended, out_matrix, preferred_element_type=f32) + out_bias
     normed_two, unit_two, inv_two = normalize(middle, gain_two, bias_two)
     normed_two = normed_two.astype(bf16)
-    result, grad_normed_two, grad_b_up_local, up_own, up_other, down_own, down_other = feed(
+    result, grad_normed_two, grad_b_up_local, feed_own, feed_other = feed(
         normed_two,
         cot,
         middle,
         up_bias[None],
         down_bias[None],
-        pieces_up,
-        pieces_down,
-        order_a,
-        order_b,
+        up_matrix,
+        second,
+        line,
+        orders,
         core,
         me,
     )
-    output = unsort_rows(result)
-    grad_b_down_local = jnp.sum(cot.astype(f32), axis=0)
+    feed_taken = swap(feed_other, 1 << core, sizes)
     grad_gain_two = jnp.sum(grad_normed_two * unit_two, axis=0)
     grad_bias_two = jnp.sum(grad_normed_two, axis=0)
-    sum_up = reduce_pieces(up_own, up_other, order_a, core, sizes)
-    sum_down = reduce_pieces(down_own, down_other, order_b, core, sizes)
-    small_feed = reduce_small(
-        [grad_gain_two, grad_bias_two, grad_b_up_local[0], grad_b_down_local],
-        order_a,
-        core,
-        sizes,
-        me,
-    )
     grad_middle = cot.astype(f32) + norm_back(grad_normed_two, unit_two, inv_two, gain_two)
     grad_branch = grad_middle.astype(bf16)
     grad_b_out_local = jnp.sum(grad_branch.astype(f32), axis=0)
-    grad_w_out_local = dot_tl(attended, grad_branch)
+    grads = weight_grad(attended, grad_branch, where, third, third + width, me)
     grad_attended = dot_t(grad_branch, out_matrix).astype(bf16)
-    pairs = width // (2 * HEAD)
+    feed_sums = reduce_start(feed_own, feed_taken, orders, sizes)
+    grad_attended = after(grad_attended, grads[0], *[v for group in feed_sums for v in group[:1] + group[2:]])
+    feed_sums = [group[:2] for group in feed_sums]
+    back = (hide, cosine, sine, partner)
     grad_mixed = attend_back(
-        seen, qkv, attended, grad_attended, lse, few, hide, cosine, sine, partner, 0, pairs
+        seen, qkv, attended, grad_attended, lse_a, few_a, *back, 0, pairs // 2
     )
-    grad_b_qkv_local = jnp.sum(grad_mixed.astype(f32), axis=1)
-    grad_w_parts = [dot_tl(normed_one, grad_mixed[i]).astype(bf16) for i in range(3)]
-    grad_normed_one = (
-        dot_t(grad_mixed[0], qk_matrix[:, :width])
-        + dot_t(grad_mixed[1], qk_matrix[:, width:])
-        + dot_t(grad_mixed[2], vo_matrix[:, :width])
+    grad_mixed = attend_back(
+        seen, qkv, attended, grad_attended, lse_b, few_b, *back, pairs // 2, pairs, grad_mixed
     )
-    grad_gain_one = jnp.sum(grad_normed_one * unit_one, axis=0)
-    grad_bias_one = jnp.sum(grad_normed_one, axis=0)
-    grad_qk = jnp.concatenate(grad_w_parts[:2], axis=1)
-    sum_q = reduce_pieces(*split(grad_qk, order_a, core, me), order_a, core, sizes)
-    grad_vo = jnp.concatenate([grad_w_parts[2], grad_w_out_local.astype(bf16)], axis=1)
-    sum_v = reduce_pieces(*split(grad_vo, order_b, core, me), order_b, core, sizes)
-    small_attn = reduce_small(
-        [grad_gain_one, grad_bias_one, grad_b_qkv_local, grad_b_out_local],
-        order_b,
-        core,
-        sizes,
-        me,
+    steps = len(orders[0])
+    for step in range(1, steps):
+        feed_sums = reduce_next(feed_sums, orders, step, sizes)
+        grad_mixed = after(grad_mixed, *[v for group in feed_sums for v in group[:1] + group[2:]])
+        feed_sums = [group[:2] for group in feed_sums]
+    own, other = weight_grad(normed_one, grad_mixed, where, 0, third + width, me, grads)
+    taken = swap(other, 1 << core, sizes)
+    grad_mixed = after(grad_mixed, other)
+    grad_tokens, grad_gain_one, grad_bias_one, grad_b_qkv_local = last_step(
+        grad_mixed, qkv_matrix, tokens_in, grad_middle, gain_one[None]
     )
-    grad_tokens = unsort_rows(
-        grad_middle + norm_back(grad_normed_one, unit_one, inv_one, gain_one)
+    vectors = [
+        grad_gain_one[0],
+        grad_bias_one[0],
+        grad_b_qkv_local[:, 0],
+        grad_b_out_local,
+        grad_gain_two,
+        grad_bias_two,
+        grad_b_up_local[0],
+        grad_b_down_local[0],
+    ]
+    small_own, small_other = small_units(vectors, rows, where, me)
+    sums = reduce_start(
+        own, taken, orders, sizes, jnp.concatenate([small_own, small_other], axis=2)
     )
+    feed_parts = line_parts(feed_sums)
+    going = [v for group in sums for v in group[:1] + group[2:]]
+    feed_parts = feed_parts[:1] + [after(v.astype(bf16), *going) for v in feed_parts[1:]]
+    sums = [group[:2] for group in sums]
+    for step in range(1, steps):
+        sums = [group[:2] for group in reduce_next(sums, orders, step, sizes)]
+    parts = line_parts(sums)
+    parts = parts[:1] + [v.astype(bf16) for v in parts[1:]]
+    feed_parts[0] = after(feed_parts[0], *parts[1:])
+    result = after(result, *going)
+    feed_sum = reduce_line(feed_parts, line, sizes)
+    sum_one = reduce_line(parts, line, sizes)
+    output = unsort_rows(result)
+    small = sum_one[:, third + width :]
+    small = small[:, :128] + swap(small[:, 128:], 1 << core, sizes)
+    small = small_parts(small, vectors, count)
+    sum_down = feed_sum[:, hidden:].reshape(rows, -1, width).swapaxes(0, 1).reshape(-1, width)
     return (
         output,
         grad_tokens,
-        small_attn[0],
-        small_attn[1],
-        jnp.concatenate([sum_q, sum_v[:, :width]], axis=1),
-        small_attn[2],
-        sum_v[:, width:],
-        small_attn[3],
-        small_feed[0],
-        small_feed[1],
-        sum_up,
-        small_feed[2],
+        small[0],
+        small[1],
+        sum_one[:, :third],
+        small[2],
+        sum_one[:, third : third + width],
+        small[3],
+        small[4],
+        small[5],
+        feed_sum[:, :hidden],
+        small[6],
         sum_down,
-        small_feed[3],
+        small[7],
     )
 
 

time: 771 us -> 538 us (0.70)
  the two profiles are of different devices: /device:TPU:1 before, /device:TPU:9 now
where the time goes in v2:
time: 538 us; the launch traced here: 530 us
  Pallas kernels  279 us (52%)
  waiting for transfers between devices  87.4 us (16%)
  other arithmetic  69.6 us (13%)
  starting transfers between devices  35.6 us (7%)
  local copies, waits for them, and re-layouts  32.8 us (6%)
  between operations  15.4 us (3%)
  matrix products  10.1 us (2%)
    pallas_call x1, Pallas kernels, feed(): pl.pallas_call(functools.partial(feed_kernel, rels, (line, orders, core))...  86.6 us
    ppermute x39, waiting for transfers between devices, swap(): lax.ppermute(value, ('dp', 'fsdp'), [(i, i ^ mask) for i in range(count)])  86 us
    pallas_call x2, Pallas kernels, attend_back(): pl.pallas_call(kernel, grid_spec=pltpu.PrefetchScalarGridSpec(num_scalar_...  60.6 us
    pallas_call x2, Pallas kernels, attend(): pl.pallas_call(kernel, grid_spec=pltpu.PrefetchScalarGridSpec(num_scalar_...  53 us
    ppermute x39, starting transfers between devices, swap(): lax.ppermute(value, ('dp', 'fsdp'), [(i, i ^ mask) for i in range(count)])  35.5 us
    pallas_call x1, Pallas kernels, project(): pl.pallas_call(functools.partial(project_kernel, 1.0 / math.sqrt(HEAD)),...  24.7 us
    pallas_call x2, Pallas kernels, weight_grad(): pl.pallas_call(functools.partial(weight_kernel, where, left, count), grid...  20.1 us
    pallas_call x1, Pallas kernels, last_step(): pl.pallas_call(last_kernel, grid=(parts,), in_specs=[pl.BlockSpec((1, row...  19.2 us
  transfers between devices with their start and end apart: 41, of which 13 were waited for; matrix products, arithmetic and copies ran while one was open for 16% of the time, Pallas kernels for 36%

profile of v2, /device:TPU:9, one launch (start us, length us, event | category | flops | bytes accessed | tf_op | source)
XLA Modules:
  0.0 530.0 jit_solution(4228897522355760971)
XLA Ops:
  26.7 5.5 %shard_map.380 = (bf16[1040,1024]{1,0:T(8,128)(2,1)}, bf16[1040,1024]{1,0:T(8,128)(2,1)}, f32[1,1024]{1,0:T(1,128)}) custom-call(bf16[1032,1024]{1,0:T(8,128)(2,1)} %x_ref.1, bf16[1032,1024]{1,0:T(8,128)(2,1)} %g_ref.1), custom_call_target="tpu_custom_call" | custom-call | flops 1000000000 | tf_op jit(solution)/shard_map/pallas_call | solution.py:883
  38.3 6.6 %collective-permute-done.5 = bf16[2,32,3328]{2,1,0:T(8,128)(2,1)S(1)} collective-permute-done((bf16[2,32,3328]{2,1,0:T(8,128)(2,1)S(1)}, bf16[2,32,3328]{2,1,0:T(8,128)(2,1)S(1)}, u32[]{:S(2)}, u32[]{:S(2)}) %collective-permute-start.5) | collective-permute-done | bytes 426016 | tf_op jit(solution)/shard_map/ppermute | solution.py:41
  50.5 5.1 collective-permute-start.9
  55.7 14.8 %collective-permute-done.6.refs_3_ = bf16[4,32,3328]{2,1,0:T(8,128)(2,1)S(1)} collective-permute-done((bf16[4,32,3328]{2,1,0:T(8,128)(2,1)S(1)}, bf16[4,32,3328]{2,1,0:T(8,128)(2,1)S(1)}, u32[]{:S(2)}, u32[]{:S(2)}) %collective-permute-start.6) | collective-permute-done | bytes 852000 | tf_op jit(solution)/shard_map/ppermute | solution.py:41
  70.4 2.6 collective-permute-start.10
  78.9 5.8 %shard_map.381 = (bf16[1024,3072]{1,0:T(8,128)(2,1)}, bf16[1024,256]{1,0:T(8,128)(2,1)}) custom-call(s32[1]{0:T(128)} %bitcast.me_ref, bf16[4,32,3328]{2,1,0:T(8,128)(2,1)} %copy-done.16, bf16[4,32,3328]{2,1,0:T(8,128)(2,1)} %copy-done.33, bf16[4,32,3328]{2,1,0:T(8,128)(2,1)} %copy-done.28, bf16[4,32,3328]{2,1,0:T(8,128)(2,1)} %copy-done.32, ...), custom_call_target="tpu_custom_call" | custom-call | flops 1500000000 | tf_op jit(solution)/shard_map/pallas_call | solution.py:174
  85.3 3.8 collective-permute-start.16
  92.0 2.8 fusion.6.x_ref
  95.4 24.7 %shard_map.382.q_ref.k_ref.v_ref.refs_1_.refs_2_.refs_3_ = bf16[1040,3072]{1,0:T(8,128)(2,1)} custom-call(bf16[1040,1024]{1,0:T(8,128)(2,1)} %fusion.6.x_ref, bf16[1024,3072]{1,0:T(8,128)(2,1)} %get-tuple-element.40.w_ref.refs_1_, f32[1,3072]{1,0:T(1,128)} %reshape_reshape.3.b_ref, f32[1040,128]{1,0:T(8,128)} %get-tuple-element.118.cos_ref.refs_9_, ...), custom_call_target="tpu_custom_call" | custom-call | flops 6000000000 | tf_op jit(solution)/shard_map/pallas_call | solution.py:539
  127.9 26.4 %shard_map.383 = (bf16[1040,1024]{1,0:T(8,128)(2,1)}, f32[4,2,1024]{2,1,0:T(2,128)}, f32[4,1,16]{2,1,0:T(1,128)}) custom-call(s32[4]{0:T(128)} %copy-done.43, bf16[1040,3072]{1,0:T(8,128)(2,1)} %shard_map.382.q_ref.k_ref.v_ref.refs_1_.refs_2_.refs_3_, bf16[1040,3072]{1,0:T(8,128)(2,1)} %shard_map.382.q_ref.k_ref.v_ref.refs_1_.refs_2_.refs_3_, ...), custom_call_target="tpu_custom_call" | custom-call | flops 6400000000 | tf_op jit(solution)/shard_map/pallas_call | solution.py:346
  158.8 26.6 %shard_map.384 = (bf16[1040,1024]{1,0:T(8,128)(2,1)}, f32[4,2,1024]{2,1,0:T(2,128)}, f32[4,1,16]{2,1,0:T(1,128)}) custom-call(s32[4]{0:T(128)} %copy-done.43, bf16[1040,3072]{1,0:T(8,128)(2,1)} %shard_map.382.q_ref.k_ref.v_ref.refs_1_.refs_2_.refs_3_, ...), custom_call_target="tpu_custom_call", output_to_operand_aliasing={{0}: (5, {})} | custom-call | flops 6400000000 | tf_op jit(solution)/shard_map/pallas_call | solution.py:346
  191.5 4.8 fusion.34
  200.3 86.6 %shard_map.394 = (bf16[1040,1024]{1,0:T(8,128)(2,1)}, f32[1040,1024]{1,0:T(8,128)}, f32[1,4096]{1,0:T(1,128)}, bf16[16,32,8192]{2,1,0:T(8,128)(2,1)}, bf16[16,32,8192]{2,1,0:T(8,128)(2,1)}) custom-call(s32[1]{0:T(128)} %bitcast.me_ref, bf16[1040,1024]{1,0:T(8,128)(2,1)} %add_convert_fusion.x_ref, bf16[1040,1024]{1,0:T(8,128)(2,1)} %get-tuple-element.43.g_ref, ...), custom_call_target="tpu_custom_call" | custom-call | flops 20000000000 | tf_op jit(solution)/shard_map/pallas_call | solution.py:760
  289.0 5.3 multiply_reduce_fusion
  294.3 6.2 %collective-permute-done.22 = bf16[16,32,8192]{2,1,0:T(8,128)(2,1)} collective-permute-done((bf16[16,32,8192]{2,1,0:T(8,128)(2,1)}, bf16[16,32,8192]{2,1,0:T(8,128)(2,1)}, u32[]{:S(2)}, u32[]{:S(2)}) %collective-permute-start.22) | collective-permute-done | bytes 8388640 | tf_op jit(solution)/shard_map/ppermute | solution.py:41
  300.6 7.4 %add_convert_fusion.1 = (bf16[4,32,8192]{2,1,0:T(8,128)(2,1)}, bf16[4,32,8192]{2,1,0:T(8,128)(2,1)}, bf16[4,32,8192]{2,1,0:T(8,128)(2,1)}, bf16[4,32,8192]{2,1,0:T(8,128)(2,1)}) fusion(bf16[16,32,8192]{2,1,0:T(8,128)(2,1)} %collective-permute-done.22, bf16[16,32,8192]{2,1,0:T(8,128)(2,1)S(1)} %copy-done.12), kind=kLoop, calls=%fused_computation.17 | loop fusion | flops 16777216 | bytes 25165824 | tf_op jit(solution)/shard_map/convert_element_type | solution.py:98
  310.1 3.6 convert_reduce_fusion.1
  313.9 7.0 %shard_map.395 = (bf16[16,32,4096]{2,1,0:T(8,128)(2,1)}, bf16[16,32,4096]{2,1,0:T(8,128)(2,1)}) custom-call(s32[1]{0:T(128)} %bitcast.me_ref, bf16[1040,1024]{1,0:T(8,128)(2,1)} %get-tuple-element.42.refs_1_.x_ref.o_ref.refs_4_, bf16[1040,1024]{1,0:T(8,128)(2,1)} %get-tuple-element.73.g_ref), custom_call_target="tpu_custom_call" | custom-call | flops 1000000000 | tf_op jit(solution)/shard_map/pallas_call | solution.py:848
  320.9 5.3 %convolution_convert_fusion.refs_0_ = bf16[1040,1024]{1,0:T(8,128)(2,1)} fusion(bf16[1040,1024]{1,0:T(8,128)(2,1)S(1)} %copy-done.11, bf16[1024,1024]{1,0:T(8,128)(2,1)} %all-gather.3.cloned.1.call-done), kind=kOutput, calls=%fused_computation.22 | convolution fusion | flops 2182103040 | bytes 6356992 | tf_op jit(solution)/shard_map/dot_general | solution.py:237
  326.2 30.0 %shard_map.397.refs_12_ = bf16[3,1040,1024]{2,1,0:T(8,128)(2,1)} custom-call(s32[4]{0:T(128)} %copy-done.43, bf16[1040,3072]{1,0:T(8,128)(2,1)} %shard_map.382.q_ref.k_ref.v_ref.refs_1_.refs_2_.refs_3_, bf16[1040,3072]{1,0:T(8,128)(2,1)} %shard_map.382.q_ref.k_ref.v_ref.refs_1_.refs_2_.refs_3_, ...), custom_call_target="tpu_custom_call" | custom-call | flops 7600000000 | tf_op jit(solution)/shard_map/pallas_call | solution.py:474
  356.3 30.6 %shard_map.398.refs_0_ = bf16[3,1040,1024]{2,1,0:T(8,128)(2,1)} custom-call(s32[4]{0:T(128)} %copy-done.43, bf16[1040,3072]{1,0:T(8,128)(2,1)} %shard_map.382.q_ref.k_ref.v_ref.refs_1_.refs_2_.refs_3_, bf16[1040,3072]{1,0:T(8,128)(2,1)} %shard_map.382.q_ref.k_ref.v_ref.refs_1_.refs_2_.refs_3_, ...), custom_call_target="tpu_custom_call", output_to_operand_aliasing={{}: (12, {})} | custom-call | flops 7600000000 | tf_op jit(solution)/shard_map/pallas_call | solution.py:474
  386.8 3.2 add_convert_fusion.9
  390.0 3.8 add_convert_fusion.11
  393.8 13.1 %shard_map.400 = (bf16[16,32,4096]{2,1,0:T(8,128)(2,1)}, bf16[16,32,4096]{2,1,0:T(8,128)(2,1)}) custom-call(s32[1]{0:T(128)} %bitcast.me_ref, bf16[1040,1024]{1,0:T(8,128)(2,1)} %fusion.6.x_ref, bf16[3,1040,1024]{2,1,0:T(8,128)(2,1)} %shard_map.399.g_ref.refs_0_, ...), custom_call_target="tpu_custom_call", output_to_operand_aliasing={{0}: (3, {}), {1}: (4, {})} | custom-call | flops 3000000000 | tf_op jit(solution)/shard_map/pallas_call | solution.py:848
  407.0 19.2 %shard_map.402 = (f32[1032,1024]{1,0:T(8,128)}, f32[1,1024]{1,0:T(1,128)}, f32[1,1024]{1,0:T(1,128)}, f32[3,1,1024]{2,1,0:T(1,128)}) custom-call(bf16[3,1040,1024]{2,1,0:T(8,128)(2,1)} %shard_map.401.g_ref, bf16[1024,3072]{1,0:T(8,128)(2,1)} %get-tuple-element.40.w_ref.refs_1_, bf16[1040,1024]{1,0:T(8,128)(2,1)} %get-tuple-element.38.x_ref, ...), custom_call_target="tpu_custom_call" | custom-call | flops 5000000000 | tf_op jit(solution)/shard_map/pallas_call | solution.py:966
  436.4 3.2 add_convert_fusion.5
  447.3 3.6 shard_map.404
  450.9 14.7 %collective-permute-done.26 = bf16[4,32,4352]{2,1,0:T(8,128)(2,1)} collective-permute-done((bf16[4,32,4352]{2,1,0:T(8,128)(2,1)S(1)}, bf16[4,32,4352]{2,1,0:T(8,128)(2,1)}, u32[]{:S(2)}, u32[]{:S(2)}) %collective-permute-start.26) | collective-permute-done | bytes 1114144 | tf_op jit(solution)/shard_map/ppermute | solution.py:41
  471.5 8.9 %collective-permute-done.27 = bf16[2,32,4352]{2,1,0:T(8,128)(2,1)S(1)} collective-permute-done((bf16[2,32,4352]{2,1,0:T(8,128)(2,1)S(1)}, bf16[2,32,4352]{2,1,0:T(8,128)(2,1)S(1)}, u32[]{:S(2)}, u32[]{:S(2)}) %collective-permute-start.27) | collective-permute-done | bytes 557088 | tf_op jit(solution)/shard_map/ppermute | solution.py:41
  485.3 16.9 %collective-permute-done.37 = bf16[32,8192]{1,0:T(8,128)(2,1)} collective-permute-done((bf16[32,8192]{1,0:T(8,128)(2,1)}, bf16[32,8192]{1,0:T(8,128)(2,1)}, u32[]{:S(2)}, u32[]{:S(2)}) %collective-permute-start.37) | collective-permute-done | bytes 524320 | tf_op jit(solution)/shard_map/ppermute | solution.py:41
  504.2 4.0 collective-permute-done.31
  508.1 7.3 %collective-permute-done.32 = bf16[32,4352]{1,0:T(8,128)(2,1)S(1)} collective-permute-done((bf16[32,4352]{1,0:T(8,128)(2,1)S(1)}, bf16[32,4352]{1,0:T(8,128)(2,1)S(1)}, u32[]{:S(2)}, u32[]{:S(2)}) %collective-permute-start.32) | collective-permute-done | bytes 278560 | tf_op jit(solution)/shard_map/ppermute | solution.py:41
  (304 shorter events, 105.4 us)
Async XLA Ops:
  7.2 183.2 %all-gather.3.cloned.1.call-start = ((), (), s32[]{:S(2)}) async-start(), calls=%async_computation | async-start | bytes 2162688 | tf_op jit(solution)/shard_map/all_gather | solution.py:1053
  7.9 192.4 %all-gather.5.cloned.1.call-start = ((), (), s32[]{:S(2)}) async-start(), calls=%async_computation.1 | async-start | bytes 8650752 | tf_op jit(solution)/shard_map/all_gather | solution.py:1054
  14.5 19.7 %collective-permute-start.4 = (bf16[1,32,3328]{2,1,0:T(8,128)(2,1)S(1)}, bf16[1,32,3328]{2,1,0:T(8,128)(2,1)S(1)}, u32[]{:S(2)}, u32[]{:S(2)}) collective-permute-start(bf16[1,32,3328]{2,1,0:T(8,128)(2,1)S(1)} %fusion.21), channel_id=1, source_target_pairs={{0,6},{1,7},{2,4},{3,5},{4,2},{5,3},{6,0},{7,1},{8,14},{9,15},{10,... | collective-permute-start | bytes 638984 | tf_op jit(solution)/shard_map/ppermute | solution.py:41
  15.8 19.0 %collective-permute-start.3 = (bf16[1,32,3328]{2,1,0:T(8,128)(2,1)S(1)}, bf16[1,32,3328]{2,1,0:T(8,128)(2,1)S(1)}, u32[]{:S(2)}, u32[]{:S(2)}) collective-permute-start(bf16[1,32,3328]{2,1,0:T(8,128)(2,1)S(1)} %fusion.21), channel_id=1, source_target_pairs={{0,4},{1,5},{2,6},{3,7},{4,0},{5,1},{6,2},{7,3},{8,12},{9,13},{10,... | collective-permute-start | bytes 638984 | tf_op jit(solution)/shard_map/ppermute | solution.py:41
  16.9 19.3 %collective-permute-start = (bf16[1,32,3328]{2,1,0:T(8,128)(2,1)S(1)}, bf16[1,32,3328]{2,1,0:T(8,128)(2,1)S(1)}, u32[]{:S(2)}, u32[]{:S(2)}) collective-permute-start(bf16[1,32,3328]{2,1,0:T(8,128)(2,1)S(1)} %fusion.21), channel_id=1, source_target_pairs={{0,2},{1,3},{2,0},{3,1},{4,6},{5,7},{6,4},{7,5},{8,10},{9,11},{10,... | collective-permute-start | bytes 638984 | tf_op jit(solution)/shard_map/ppermute | solution.py:41
  44.9 25.5 %collective-permute-start.6 = (bf16[4,32,3328]{2,1,0:T(8,128)(2,1)S(1)}, bf16[4,32,3328]{2,1,0:T(8,128)(2,1)S(1)}, u32[]{:S(2)}, u32[]{:S(2)}) collective-permute-start(bf16[4,32,3328]{2,1,0:T(8,128)(2,1)S(1)} %constant_dynamic-update-slice_fusion.refs_2_), channel_id=1, source_target_pairs={{0,1},{1,0},{2,3},{3,2},{4,5},{5,4},{6,7},{7,6},{8,9},{9,8},{10,11... | collective-permute-start | bytes 2555912 | tf_op jit(solution)/shard_map/ppermute | solution.py:41
  49.6 23.5 %collective-permute-start.2 = (bf16[4,32,3328]{2,1,0:T(8,128)(2,1)S(1)}, bf16[4,32,3328]{2,1,0:T(8,128)(2,1)S(1)}, u32[]{:S(2)}, u32[]{:S(2)}) collective-permute-start(bf16[4,32,3328]{2,1,0:T(8,128)(2,1)S(1)} %pad_maximum_fusion.6.refs_0_), channel_id=1, source_target_pairs={{0,16},{1,17},{2,18},{3,19},{4,20},{5,21},{6,22},{7,23},{8,24},{9,... | collective-permute-start | bytes 2555912 | tf_op jit(solution)/shard_map/ppermute | solution.py:41
  50.5 26.0 %collective-permute-start.9 = (bf16[4,32,3328]{2,1,0:T(8,128)(2,1)S(1)}, bf16[4,32,3328]{2,1,0:T(8,128)(2,1)S(1)}, u32[]{:S(2)}, u32[]{:S(2)}) collective-permute-start(bf16[4,32,3328]{2,1,0:T(8,128)(2,1)S(1)} %constant_dynamic-update-slice_fusion.refs_2_), channel_id=1, source_target_pairs={{0,8},{1,9},{2,10},{3,11},{4,12},{5,13},{6,14},{7,15},{8,0},{9,1},... | collective-permute-start | bytes 2555912 | tf_op jit(solution)/shard_map/ppermute | solution.py:41
  55.6 20.9 %collective-permute-start.7 = (bf16[4,32,3328]{2,1,0:T(8,128)(2,1)S(1)}, bf16[4,32,3328]{2,1,0:T(8,128)(2,1)S(1)}, u32[]{:S(2)}, u32[]{:S(2)}) collective-permute-start(bf16[4,32,3328]{2,1,0:T(8,128)(2,1)S(1)} %pad_maximum_fusion.6.refs_0_), channel_id=1, source_target_pairs={{0,8},{1,9},{2,10},{3,11},{4,12},{5,13},{6,14},{7,15},{8,0},{9,1},... | collective-permute-start | bytes 2555912 | tf_op jit(solution)/shard_map/ppermute | solution.py:41
  84.7 39.9 %collective-permute-start.17 = (bf16[1,32,4096]{2,1,0:T(8,128)(2,1)}, bf16[1,32,4096]{2,1,0:T(8,128)(2,1)S(1)}, u32[]{:S(2)}, u32[]{:S(2)}) collective-permute-start(bf16[1,32,4096]{2,1,0:T(8,128)(2,1)} %bitcast.91), channel_id=1, source_target_pairs={{0,6},{1,7},{2,4},{3,5},{4,2},{5,3},{6,0},{7,1},{8,14},{9,15},{10,... | collective-permute-start | bytes 786440 | tf_op jit(solution)/shard_map/ppermute | solution.py:41
  85.3 39.3 %collective-permute-start.16 = (bf16[1,32,4096]{2,1,0:T(8,128)(2,1)}, bf16[1,32,4096]{2,1,0:T(8,128)(2,1)}, u32[]{:S(2)}, u32[]{:S(2)}) collective-permute-start(bf16[1,32,4096]{2,1,0:T(8,128)(2,1)} %bitcast.92), channel_id=1, source_target_pairs={{0,4},{1,5},{2,6},{3,7},{4,0},{5,1},{6,2},{7,3},{8,12},{9,13},{10,... | collective-permute-start | bytes 786440 | tf_op jit(solution)/shard_map/ppermute | solution.py:41
  89.1 31.9 %collective-permute-start.11 = (bf16[1,32,4096]{2,1,0:T(8,128)(2,1)}, bf16[1,32,4096]{2,1,0:T(8,128)(2,1)}, u32[]{:S(2)}, u32[]{:S(2)}) collective-permute-start(bf16[1,32,4096]{2,1,0:T(8,128)(2,1)} %bitcast.93), channel_id=1, source_target_pairs={{0,2},{1,3},{2,0},{3,1},{4,6},{5,7},{6,4},{7,5},{8,10},{9,11},{10,... | collective-permute-start | bytes 786440 | tf_op jit(solution)/shard_map/ppermute | solution.py:41
  122.8 35.2 %collective-permute-start.13 = (bf16[2,32,4096]{2,1,0:T(8,128)(2,1)}, bf16[2,32,4096]{2,1,0:T(8,128)(2,1)S(1)}, u32[]{:S(2)}, u32[]{:S(2)}) collective-permute-start(bf16[2,32,4096]{2,1,0:T(8,128)(2,1)} %shard_map.386), channel_id=1, source_target_pairs={{0,16},{1,17},{2,18},{3,19},{4,20},{5,21},{6,22},{7,23},{8,24},{9,... | collective-permute-start | bytes 1572872 | tf_op jit(solution)/shard_map/ppermute | solution.py:41
  123.1 31.3 %collective-permute-start.12 = (bf16[2,32,4096]{2,1,0:T(8,128)(2,1)}, bf16[2,32,4096]{2,1,0:T(8,128)(2,1)S(1)}, u32[]{:S(2)}, u32[]{:S(2)}) collective-permute-start(bf16[2,32,4096]{2,1,0:T(8,128)(2,1)} %shard_map.386), channel_id=1, source_target_pairs={{0,1},{1,0},{2,3},{3,2},{4,5},{5,4},{6,7},{7,6},{8,9},{9,8},{10,11... | collective-permute-start | bytes 1572872 | tf_op jit(solution)/shard_map/ppermute | solution.py:41
  126.5 30.7 %collective-permute-start.19 = (bf16[2,32,4096]{2,1,0:T(8,128)(2,1)}, bf16[2,32,4096]{2,1,0:T(8,128)(2,1)S(1)}, u32[]{:S(2)}, u32[]{:S(2)}) collective-permute-start(bf16[2,32,4096]{2,1,0:T(8,128)(2,1)} %shard_map.390), channel_id=1, source_target_pairs={{0,1},{1,0},{2,3},{3,2},{4,5},{5,4},{6,7},{7,6},{8,9},{9,8},{10,11... | collective-permute-start | bytes 1572872 | tf_op jit(solution)/shard_map/ppermute | solution.py:41
  126.5 28.7 %collective-permute-start.18 = (bf16[2,32,4096]{2,1,0:T(8,128)(2,1)}, bf16[2,32,4096]{2,1,0:T(8,128)(2,1)S(1)}, u32[]{:S(2)}, u32[]{:S(2)}) collective-permute-start(bf16[2,32,4096]{2,1,0:T(8,128)(2,1)} %shard_map.390), channel_id=1, source_target_pairs={{0,16},{1,17},{2,18},{3,19},{4,20},{5,21},{6,22},{7,23},{8,24},{9,... | collective-permute-start | bytes 1572872 | tf_op jit(solution)/shard_map/ppermute | solution.py:41
  155.2 31.8 %collective-permute-start.14 = (bf16[2,32,4096]{2,1,0:T(8,128)(2,1)}, bf16[2,32,4096]{2,1,0:T(8,128)(2,1)S(1)}, u32[]{:S(2)}, u32[]{:S(2)}) collective-permute-start(bf16[2,32,4096]{2,1,0:T(8,128)(2,1)} %shard_map.387), channel_id=1, source_target_pairs={{0,16},{1,17},{2,18},{3,19},{4,20},{5,21},{6,22},{7,23},{8,24},{9,... | collective-permute-start | bytes 1572872 | tf_op jit(solution)/shard_map/ppermute | solution.py:41
  156.0 29.4 %collective-permute-start.20 = (bf16[2,32,4096]{2,1,0:T(8,128)(2,1)}, bf16[2,32,4096]{2,1,0:T(8,128)(2,1)S(1)}, u32[]{:S(2)}, u32[]{:S(2)}) collective-permute-start(bf16[2,32,4096]{2,1,0:T(8,128)(2,1)} %shard_map.391), channel_id=1, source_target_pairs={{0,1},{1,0},{2,3},{3,2},{4,5},{5,4},{6,7},{7,6},{8,9},{9,8},{10,11... | collective-permute-start | bytes 1572872 | tf_op jit(solution)/shard_map/ppermute | solution.py:41
  287.0 13.6 %collective-permute-start.22 = (bf16[16,32,8192]{2,1,0:T(8,128)(2,1)}, bf16[16,32,8192]{2,1,0:T(8,128)(2,1)}, u32[]{:S(2)}, u32[]{:S(2)}) collective-permute-start(bf16[16,32,8192]{2,1,0:T(8,128)(2,1)} %get-tuple-element.48), channel_id=1, source_target_pairs={{0,8},{1,9},{2,10},{3,11},{4,12},{5,13},{6,14},{7,15},{8,0},{9,1},... | collective-permute-start | bytes 25165832 | tf_op jit(solution)/shard_map/ppermute | solution.py:41
  308.0 78.8 %collective-permute-start.24 = (bf16[4,32,8192]{2,1,0:T(8,128)(2,1)}, bf16[4,32,8192]{2,1,0:T(8,128)(2,1)}, u32[]{:S(2)}, u32[]{:S(2)}) collective-permute-start(bf16[4,32,8192]{2,1,0:T(8,128)(2,1)} %get-tuple-element.75.refs_5_), channel_id=1, source_target_pairs={{0,1},{1,0},{2,3},{3,2},{4,5},{5,4},{6,7},{7,6},{8,9},{9,8},{10,11... | collective-permute-start | bytes 6291464 | tf_op jit(solution)/shard_map/ppermute | solution.py:41
  326.2 63.8 %collective-permute-start.23 = (bf16[4,32,8192]{2,1,0:T(8,128)(2,1)}, bf16[4,32,8192]{2,1,0:T(8,128)(2,1)}, u32[]{:S(2)}, u32[]{:S(2)}) collective-permute-start(bf16[4,32,8192]{2,1,0:T(8,128)(2,1)} %get-tuple-element.77.refs_3_), channel_id=1, source_target_pairs={{0,16},{1,17},{2,18},{3,19},{4,20},{5,21},{6,22},{7,23},{8,24},{9,... | collective-permute-start | bytes 6291464 | tf_op jit(solution)/shard_map/ppermute | solution.py:41
  390.0 41.2 %collective-permute-start.36 = (bf16[2,32,8192]{2,1,0:T(8,128)(2,1)S(1)}, bf16[2,32,8192]{2,1,0:T(8,128)(2,1)}, u32[]{:S(2)}, u32[]{:S(2)}) collective-permute-start(bf16[2,32,8192]{2,1,0:T(8,128)(2,1)S(1)} %get-tuple-element.83.refs_4_), channel_id=1, source_target_pairs={{0,16},{1,17},{2,18},{3,19},{4,20},{5,21},{6,22},{7,23},{8,24},{9,... | collective-permute-start | bytes 3145736 | tf_op jit(solution)/shard_map/ppermute | solution.py:41
  393.8 40.0 %collective-permute-start.34 = (bf16[2,32,8192]{2,1,0:T(8,128)(2,1)}, bf16[2,32,8192]{2,1,0:T(8,128)(2,1)}, u32[]{:S(2)}, u32[]{:S(2)}) collective-permute-start(bf16[2,32,8192]{2,1,0:T(8,128)(2,1)} %get-tuple-element.85.refs_2_), channel_id=1, source_target_pairs={{0,1},{1,0},{2,3},{3,2},{4,5},{5,4},{6,7},{7,6},{8,9},{9,8},{10,11... | collective-permute-start | bytes 3145736 | tf_op jit(solution)/shard_map/ppermute | solution.py:41
  406.9 29.4 %collective-permute-start.25 = (bf16[16,32,4096]{2,1,0:T(8,128)(2,1)}, bf16[16,32,4096]{2,1,0:T(8,128)(2,1)}, u32[]{:S(2)}, u32[]{:S(2)}) collective-permute-start(bf16[16,32,4096]{2,1,0:T(8,128)(2,1)} %get-tuple-element.55.refs_1_), channel_id=1, source_target_pairs={{0,8},{1,9},{2,10},{3,11},{4,12},{5,13},{6,14},{7,15},{8,0},{9,1},... | collective-permute-start | bytes 12582920 | tf_op jit(solution)/shard_map/ppermute | solution.py:41
  439.7 25.9 %collective-permute-start.26 = (bf16[4,32,4352]{2,1,0:T(8,128)(2,1)S(1)}, bf16[4,32,4352]{2,1,0:T(8,128)(2,1)}, u32[]{:S(2)}, u32[]{:S(2)}) collective-permute-start(bf16[4,32,4352]{2,1,0:T(8,128)(2,1)S(1)} %pad_maximum_fusion.4.refs_2_), channel_id=1, source_target_pairs={{0,16},{1,17},{2,18},{3,19},{4,20},{5,21},{6,22},{7,23},{8,24},{9,... | collective-permute-start | bytes 3342344 | tf_op jit(solution)/shard_map/ppermute | solution.py:41
  441.0 27.9 %collective-permute-start.29 = (bf16[4,32,4352]{2,1,0:T(8,128)(2,1)S(1)}, bf16[4,32,4352]{2,1,0:T(8,128)(2,1)}, u32[]{:S(2)}, u32[]{:S(2)}) collective-permute-start(bf16[4,32,4352]{2,1,0:T(8,128)(2,1)S(1)} %pad_maximum_fusion.5.refs_4_), channel_id=1, source_target_pairs={{0,1},{1,0},{2,3},{3,2},{4,5},{5,4},{6,7},{7,6},{8,9},{9,8},{10,11... | collective-permute-start | bytes 3342344 | tf_op jit(solution)/shard_map/ppermute | solution.py:41
  444.7 39.9 %collective-permute-start.38 = (bf16[32,8192]{1,0:T(8,128)(2,1)}, bf16[32,8192]{1,0:T(8,128)(2,1)}, u32[]{:S(2)}, u32[]{:S(2)}) collective-permute-start(bf16[32,8192]{1,0:T(8,128)(2,1)} %shard_map.408), channel_id=1, source_target_pairs={{0,6},{1,7},{2,4},{3,5},{4,2},{5,3},{6,0},{7,1},{8,14},{9,15},{10,... | collective-permute-start | bytes 1572872 | tf_op jit(solution)/shard_map/ppermute | solution.py:41
  444.7 57.6 %collective-permute-start.37 = (bf16[32,8192]{1,0:T(8,128)(2,1)}, bf16[32,8192]{1,0:T(8,128)(2,1)}, u32[]{:S(2)}, u32[]{:S(2)}) collective-permute-start(bf16[32,8192]{1,0:T(8,128)(2,1)} %shard_map.407), channel_id=1, source_target_pairs={{0,4},{1,5},{2,6},{3,7},{4,0},{5,1},{6,2},{7,3},{8,12},{9,13},{10,... | collective-permute-start | bytes 1572872 | tf_op jit(solution)/shard_map/ppermute | solution.py:41
  447.0 55.3 %collective-permute-start.35 = (bf16[32,8192]{1,0:T(8,128)(2,1)}, bf16[32,8192]{1,0:T(8,128)(2,1)}, u32[]{:S(2)}, u32[]{:S(2)}) collective-permute-start(bf16[32,8192]{1,0:T(8,128)(2,1)} %shard_map.406), channel_id=1, source_target_pairs={{0,2},{1,3},{2,0},{3,1},{4,6},{5,7},{6,4},{7,5},{8,10},{9,11},{10,... | collective-permute-start | bytes 1572872 | tf_op jit(solution)/shard_map/ppermute | solution.py:41
  480.5 23.7 %collective-permute-start.28 = (bf16[32,4352]{1,0:T(8,128)(2,1)S(1)}, bf16[32,4352]{1,0:T(8,128)(2,1)S(1)}, u32[]{:S(2)}, u32[]{:S(2)}) collective-permute-start(bf16[32,4352]{1,0:T(8,128)(2,1)S(1)} %fusion.17.refs_1_), channel_id=1, source_target_pairs={{0,2},{1,3},{2,0},{3,1},{4,6},{5,7},{6,4},{7,5},{8,10},{9,11},{10,... | collective-permute-start | bytes 835592 | tf_op jit(solution)/shard_map/ppermute | solution.py:41
  483.8 24.3 %collective-permute-start.31 = (bf16[32,4352]{1,0:T(8,128)(2,1)S(1)}, bf16[32,4352]{1,0:T(8,128)(2,1)S(1)}, u32[]{:S(2)}, u32[]{:S(2)}) collective-permute-start(bf16[32,4352]{1,0:T(8,128)(2,1)S(1)} %get-tuple-element.95.refs_2_), channel_id=1, source_target_pairs={{0,4},{1,5},{2,6},{3,7},{4,0},{5,1},{6,2},{7,3},{8,12},{9,13},{10,... | collective-permute-start | bytes 835592 | tf_op jit(solution)/shard_map/ppermute | solution.py:41
  484.9 30.6 %collective-permute-start.32 = (bf16[32,4352]{1,0:T(8,128)(2,1)S(1)}, bf16[32,4352]{1,0:T(8,128)(2,1)S(1)}, u32[]{:S(2)}, u32[]{:S(2)}) collective-permute-start(bf16[32,4352]{1,0:T(8,128)(2,1)S(1)} %copy-done.29), channel_id=1, source_target_pairs={{0,6},{1,7},{2,4},{3,5},{4,2},{5,3},{6,0},{7,1},{8,14},{9,15},{10,... | collective-permute-start | bytes 835592 | tf_op jit(solution)/shard_map/ppermute | solution.py:41
  (60 other events, 671.9 us)
Sparse Core Ops, SparseCore 0:
  11.0 66.4 all-gather.2
  80.4 106.2 all-gather.4

commit v3 on v2

--- a/solution.py
+++ b/solution.py
@@ -84,21 +84,12 @@
     return rel, [p | (1 << core) for p in rel]
 
 
-def reduce_start(own, taken, orders, sizes, small=None):
+def reduce_start(own, taken, orders, sizes):
     half = own.shape[0] // 2
-    found = []
-    for at, order in zip((0, half), orders):
-        kept, came = own[at : at + half], taken[at : at + half]
-        quarter = half // 2
-        pieces = []
-        for low in (0, quarter):
-            total = kept[low : low + quarter].astype(f32) + came[low : low + quarter].astype(f32)
-            if small is not None:
-                total = jnp.concatenate([total, small[at + low : at + low + quarter]], axis=2)
-            pieces.append(total.astype(own.dtype))
-        held, sent = pieces
-        found.append((held, swap(sent, 1 << order[-1], sizes), sent))
-    return found
+    return [
+        reduce_step(own[at : at + half], taken[at : at + half], 1 << order[-1], sizes)
+        for at, order in zip((0, half), orders)
+    ]
 
 
 def reduce_step(kept, taken, mask, sizes):
@@ -113,6 +104,12 @@
     return [
         reduce_step(*group, 1 << order[-1 - step], sizes) for group, order in zip(groups, orders)
     ]
+
+
+def together(groups):
+    (kept, came), (other_kept, other_came) = groups
+    came = after(came, other_came)
+    return [(kept, came), (other_kept, after(other_came, came))]
 
 
 def after_pieces(pieces, *others):
@@ -255,11 +252,18 @@
 
 
 def stack_heads(x):
-    return jnp.concatenate([keep_head(x, 0), keep_head(x, 1)], axis=0)
+    head = lax.broadcasted_iota(jnp.int32, x.shape, 1) // HEAD
+    heads = x.shape[1] // HEAD
+    return jnp.concatenate([jnp.where(head == a, x, jnp.zeros_like(x)) for a in range(heads)], axis=0)
 
 
 def join_heads(x):
-    return jnp.where(head_lanes(0, FEW), x[:FEW], x[FEW:])
+    heads = x.shape[0] // FEW
+    head = lax.broadcasted_iota(jnp.int32, (FEW, x.shape[1]), 1) // HEAD
+    found = x[:FEW]
+    for a in range(1, heads):
+        found = jnp.where(head == a, x[a * FEW : (a + 1) * FEW], found)
+    return found
 
 
 def few_rows(x):
@@ -274,19 +278,23 @@
     return jnp.concatenate([s[:count], jnp.where(seen, s[count:], masked_value)], axis=0)
 
 
-def seen_rows(ref, lo, n):
-    return jnp.concatenate([ref[pl.ds(lo, n * PATCH), :], ref[BODY:ROWS, :]], axis=0)
+def seen_rows(ref, lanes, lo, n):
+    return jnp.concatenate([ref[pl.ds(lo, n * PATCH), lanes], ref[BODY:ROWS, lanes]], axis=0)
 
 
 def seen_lanes(ref, a, lo, n):
-    return jnp.concatenate(
-        [ref[a * HEAD : (a + 1) * HEAD, pl.ds(lo, n * PATCH)], ref[a * HEAD : (a + 1) * HEAD, BODY:ROWS]],
-        axis=1,
-    )
+    rows = slice(a * HEAD, (a + 1) * HEAD)
+    return jnp.concatenate([ref[rows, pl.ds(lo, n * PATCH)], ref[rows, BODY:ROWS]], axis=1)
+
+
+def pair_lanes(a):
+    at = a // 2 * 2 * HEAD
+    return slice(at, at + 2 * HEAD)
 
 
 def attend_kernel(seen_ref, q_ref, k_ref, v_ref, hide_ref, out_ref, lse_ref, few_ref, vt):
     f = pl.program_id(1)
+    heads = q_ref.shape[1] // HEAD
 
     @pl.when(f == 0)
     def _():
@@ -306,7 +314,7 @@
     @pl.when(seen == 0)
     def _():
         out_ref[pl.ds(row, PATCH), :] = v_ref[pl.ds(row, PATCH), :]
-        lse_ref[0, :, pl.ds(row, PATCH)] = jnp.zeros((2, PATCH), f32)
+        lse_ref[0, :, pl.ds(row, PATCH)] = jnp.zeros((heads, PATCH), f32)
 
     for n in range(1, FRAMES + 1):
 
@@ -314,14 +322,22 @@
         def _(n=n):
             first = f - (n - 1)
             lo = pl.multiple_of(first * PATCH, PATCH)
-            keys = seen_rows(k_ref, lo, n)
-            q = q_ref[pl.ds(row, PATCH), :]
+
+            def score(a):
+                lanes = pair_lanes(a)
+                q = keep_head(q_ref[pl.ds(row, PATCH), lanes], a % 2)
+                return hide_few(dot_t(seen_rows(k_ref, lanes, lo, n), q), first, f)
+
+            ahead = 4
+            scores = [score(a) for a in range(ahead)]
             outs, sums = [], []
-            for a in range(2):
-                s = hide_few(dot_t(keys, keep_head(q, a)), first, f)
+            for a in range(heads):
+                s = scores[a]
                 top = jnp.max(s, axis=0, keepdims=True)
                 p = jnp.exp(s - top)
                 total = jnp.sum(p, axis=0, keepdims=True)
+                if a + ahead < heads:
+                    scores.append(score(a + ahead))
                 o = dot_n(seen_lanes(vt, a, lo, n), p.astype(bf16))
                 outs.append(o / total)
                 sums.append(top + jnp.log(total))
@@ -329,12 +345,15 @@
             lse_ref[0, :, pl.ds(row, PATCH)] = jnp.concatenate(sums, axis=0)
 
 
+PAIRS = 4
+
+
 def attend(seen, qkv, hide, pair_lo, pair_hi, kept=None):
     width = qkv.shape[1] // 3
-    pairs = width // (2 * HEAD)
-    lanes = 2 * HEAD
-    at = pair_lo
-    some = pair_hi - pair_lo
+    lanes = 2 * HEAD * PAIRS
+    groups = width // lanes
+    at = pair_lo // PAIRS
+    some = (pair_hi - pair_lo) // PAIRS
     kernel = attend_kernel
     more, alias = [], {}
     if kept is not None:
@@ -350,26 +369,26 @@
             grid=(some, FRAMES),
             in_specs=[
                 pl.BlockSpec((ROWS, lanes), lambda h, f, s: (0, at + h)),
-                pl.BlockSpec((ROWS, lanes), lambda h, f, s: (0, at + pairs + h)),
-                pl.BlockSpec((ROWS, lanes), lambda h, f, s: (0, at + 2 * pairs + h)),
-                pl.BlockSpec((ROWS, 2 * FEW), lambda h, f, s: (0, 0)),
+                pl.BlockSpec((ROWS, lanes), lambda h, f, s: (0, at + groups + h)),
+                pl.BlockSpec((ROWS, lanes), lambda h, f, s: (0, at + 2 * groups + h)),
+                pl.BlockSpec((ROWS, 2 * PAIRS * FEW), lambda h, f, s: (0, 0)),
             ]
             + [pl.BlockSpec(memory_space=pl.ANY)] * len(more),
             out_specs=[
                 pl.BlockSpec((ROWS, lanes), lambda h, f, s: (0, at + h)),
-                pl.BlockSpec((1, 2, BODY), lambda h, f, s: (h, 0, 0)),
-                pl.BlockSpec((1, 1, 2 * FEW), lambda h, f, s: (h, 0, 0)),
+                pl.BlockSpec((1, 2 * PAIRS, BODY), lambda h, f, s: (h, 0, 0)),
+                pl.BlockSpec((1, 1, 2 * PAIRS * FEW), lambda h, f, s: (h, 0, 0)),
             ],
             scratch_shapes=[pltpu.VMEM((lanes, ROWS), bf16)],
         ),
         out_shape=(
             jax.ShapeDtypeStruct((ROWS, width), bf16),
-            jax.ShapeDtypeStruct((some, 2, BODY), f32),
-            jax.ShapeDtypeStruct((some, 1, 2 * FEW), f32),
+            jax.ShapeDtypeStruct((some, 2 * PAIRS, BODY), f32),
+            jax.ShapeDtypeStruct((some, 1, 2 * PAIRS * FEW), f32),
         ),
         input_output_aliases=alias,
         compiler_params=pltpu.CompilerParams(vmem_limit_bytes=vmem_most),
-        cost_estimate=cost(1.6 * some),
+        cost_estimate=cost(6.4 * some),
     )(seen, qkv, qkv, qkv, hide, *more)
 
 
@@ -382,6 +401,8 @@
     part_ref, out_ref, kt, dq, dk, dv,
 ):
     f = pl.program_id(1)
+    heads = q_ref.shape[1] // HEAD
+    pairs = [slice(p * 2 * HEAD, (p + 1) * 2 * HEAD) for p in range(heads // 2)]
     ones = jnp.where(
         (lax.broadcasted_iota(jnp.int32, (8, 2 * HEAD), 1) >= HEAD).astype(jnp.int32)
         == lax.broadcasted_iota(jnp.int32, (8, 2 * HEAD), 0),
@@ -393,13 +414,12 @@
     def _():
         kt[...] = k_ref[...].T
         qs = stack_heads(q_ref[BODY:ROWS, :].astype(f32)[:FEW]).astype(bf16)
-        gs = stack_heads(g_ref[BODY:ROWS, :].astype(f32)[:FEW])
-        os = stack_heads(o_ref[BODY:ROWS, :].astype(f32)[:FEW])
+        gs = stack_heads(g_ref[BODY:ROWS, :].astype(f32)[:FEW]).astype(bf16)
         p = jnp.exp(dot_t(k_ref[...], qs) + hide_ref[...] - few_ref[0])
-        gp = dot_t(v_ref[...], gs.astype(bf16))
+        gp = dot_t(v_ref[...], gs)
         delta = jnp.sum(gp * p, axis=0, keepdims=True)
         ds = (p * (gp - delta)).astype(bf16)
-        dv[...] = dot_n(p.astype(bf16), gs.astype(bf16))
+        dv[...] = dot_n(p.astype(bf16), gs)
         dk[...] = dot_n(ds, qs)
         dq[BODY:ROWS, :] = few_rows(join_heads(dot_tl(ds, k_ref[...])))
 
@@ -409,7 +429,7 @@
     @pl.when(seen == 0)
     def _():
         dv[pl.ds(row, PATCH), :] += g_ref[pl.ds(row, PATCH), :].astype(f32)
-        dq[pl.ds(row, PATCH), :] = jnp.zeros((PATCH, 2 * HEAD), f32)
+        dq[pl.ds(row, PATCH), :] = jnp.zeros((PATCH, heads * HEAD), f32)
 
     for n in range(1, FRAMES + 1):
 
@@ -417,37 +437,55 @@
         def _(n=n):
             first = f - (n - 1)
             lo = pl.multiple_of(first * PATCH, PATCH)
-            keys = seen_rows(k_ref, lo, n)
-            values = seen_rows(v_ref, lo, n)
-            q = q_ref[pl.ds(row, PATCH), :]
-            g = g_ref[pl.ds(row, PATCH), :]
-            product = g.astype(f32) * o_ref[pl.ds(row, PATCH), :].astype(f32)
-            upper = product.astype(bf16)
-            lower = (product - upper.astype(f32)).astype(bf16)
-            deltas = dot_t(ones, upper) + dot_t(ones, lower)
+            count = n * PATCH
+
+            def start(a):
+                lanes = pair_lanes(a)
+                q = keep_head(q_ref[pl.ds(row, PATCH), lanes], a % 2)
+                g = keep_head(g_ref[pl.ds(row, PATCH), lanes], a % 2)
+                s = hide_few(dot_t(seen_rows(k_ref, lanes, lo, n), q), first, f)
+                return q, g, s, dot_t(seen_rows(v_ref, lanes, lo, n), g)
+
+            deltas = []
+            for lanes in pairs:
+                g = g_ref[pl.ds(row, PATCH), lanes].astype(f32)
+                product = g * o_ref[pl.ds(row, PATCH), lanes].astype(f32)
+                upper = product.astype(bf16)
+                lower = (product - upper.astype(f32)).astype(bf16)
+                deltas.append(dot_t(ones, upper) + dot_t(ones, lower))
+            ahead = 4
+            started = [start(a) for a in range(ahead)]
             back, add_k, add_v = [], None, None
-            for a in range(2):
-                qm, gm = keep_head(q, a), keep_head(g, a)
-                s = hide_few(dot_t(keys, qm), first, f)
+            for a in range(heads):
+                q, g, s, gp = started[a]
                 p = jnp.exp(s - lse_ref[0, a : a + 1, pl.ds(row, PATCH)])
-                gp = dot_t(values, gm)
-                ds = (p * (gp - deltas[a : a + 1])).astype(bf16)
-                more_v, more_k = dot_n(p.astype(bf16), gm), dot_n(ds, qm)
-                add_v = more_v if add_v is None else add_v + more_v
-                add_k = more_k if add_k is None else add_k + more_k
+                ds = (p * (gp - deltas[a // 2][a % 2 : a % 2 + 1])).astype(bf16)
+                p = p.astype(bf16)
+                if a + ahead < heads:
+                    started.append(start(a + ahead))
+                more_v, more_k = dot_n(p, g), dot_n(ds, q)
                 back.append(dot_n(seen_lanes(kt, a, lo, n), ds))
+                if a % 2 == 0:
+                    add_v, add_k = more_v, more_k
+                else:
+                    lanes = pairs[a // 2]
+                    add_v, add_k = add_v + more_v, add_k + more_k
+                    dk[pl.ds(lo, count), lanes] += add_k[:count]
+                    dk[BODY:ROWS, lanes] += add_k[count:]
+                    dv[pl.ds(lo, count), lanes] += add_v[:count]
+                    dv[BODY:ROWS, lanes] += add_v[count:]
             dq[pl.ds(row, PATCH), :] = jnp.concatenate(back, axis=0).T
-            count = n * PATCH
-            dk[pl.ds(lo, count), :] += add_k[:count]
-            dk[BODY:ROWS, :] += add_k[count:]
-            dv[pl.ds(lo, count), :] += add_v[:count]
-            dv[BODY:ROWS, :] += add_v[count:]
 
     @pl.when(f == FRAMES - 1)
     def _():
         partner = part_ref[...]
-        out_ref[0] = unturn(dq[...] * scale, cos_ref[...], sin_ref[...], partner).astype(bf16)
-        out_ref[1] = unturn(dk[...], cos_ref[...], sin_ref[...], partner).astype(bf16)
+        for lanes in pairs:
+            out_ref[0, :, lanes] = unturn(
+                dq[:, lanes] * scale, cos_ref[...], sin_ref[...], partner
+            ).astype(bf16)
+            out_ref[1, :, lanes] = unturn(
+                dk[:, lanes], cos_ref[...], sin_ref[...], partner
+            ).astype(bf16)
         out_ref[2] = dv[...].astype(bf16)
 
 
@@ -455,10 +493,11 @@
     seen, qkv, attended, grad, lse, few, hide, cosine, sine, partner, pair_lo, pair_hi, kept=None
 ):
     width = qkv.shape[1] // 3
-    pairs = width // (2 * HEAD)
-    lanes = 2 * HEAD
-    at = pair_lo
-    some = pair_hi - pair_lo
+    pair = 2 * HEAD
+    lanes = pair * PAIRS
+    groups = width // lanes
+    at = pair_lo // PAIRS
+    some = (pair_hi - pair_lo) // PAIRS
     inner = functools.partial(attend_back_kernel, 1.0 / math.sqrt(HEAD))
     kernel = inner
     more, alias = [], {}
@@ -478,16 +517,16 @@
             grid=(some, FRAMES),
             in_specs=[
                 pl.BlockSpec((ROWS, lanes), lambda h, f, s: (0, at + h)),
-                pl.BlockSpec((ROWS, lanes), lambda h, f, s: (0, at + pairs + h)),
-                pl.BlockSpec((ROWS, lanes), lambda h, f, s: (0, at + 2 * pairs + h)),
+                pl.BlockSpec((ROWS, lanes), lambda h, f, s: (0, at + groups + h)),
+                pl.BlockSpec((ROWS, lanes), lambda h, f, s: (0, at + 2 * groups + h)),
                 pl.BlockSpec((ROWS, lanes), lambda h, f, s: (0, at + h)),
                 pl.BlockSpec((ROWS, lanes), lambda h, f, s: (0, at + h)),
-                pl.BlockSpec((1, 2, BODY), lambda h, f, s: (h, 0, 0)),
-                pl.BlockSpec((1, 1, 2 * FEW), lambda h, f, s: (h, 0, 0)),
-                pl.BlockSpec((ROWS, 2 * FEW), whole),
-                pl.BlockSpec((ROWS, lanes), whole),
-                pl.BlockSpec((ROWS, lanes), whole),
-                pl.BlockSpec((lanes, lanes), whole),
+                pl.BlockSpec((1, 2 * PAIRS, BODY), lambda h, f, s: (h, 0, 0)),
+                pl.BlockSpec((1, 1, 2 * PAIRS * FEW), lambda h, f, s: (h, 0, 0)),
+                pl.BlockSpec((ROWS, 2 * PAIRS * FEW), whole),
+                pl.BlockSpec((ROWS, pair), whole),
+                pl.BlockSpec((ROWS, pair), whole),
+                pl.BlockSpec((pair, pair), whole),
             ]
             + [pl.BlockSpec(memory_space=pl.ANY)] * len(more),
             out_specs=pl.BlockSpec((3, ROWS, lanes), lambda h, f, s: (0, 0, at + h)),
@@ -501,7 +540,7 @@
         out_shape=jax.ShapeDtypeStruct((3, ROWS, width), bf16),
         input_output_aliases=alias,
         compiler_params=pltpu.CompilerParams(vmem_limit_bytes=vmem_most),
-        cost_estimate=cost(1.9 * some),
+        cost_estimate=cost(7.6 * some),
     )(seen, qkv, qkv, qkv, attended, grad, lse, few, hide, cosine, sine, partner, *more)
 
 
@@ -509,19 +548,22 @@
     j = pl.program_id(0)
     third = pl.num_programs(0) // 3
     lanes = 2 * HEAD
+    wide = part_ref.shape[0]
     w = w_ref[...]
     mixed = dot_n(x_ref[...], w) + b_ref[...]
 
     @pl.when(j < 2 * third)
     def _():
-        bias = jnp.broadcast_to(b_ref[...], (8, w.shape[1]))
         by = jnp.where(j < third, scale, 1.0)
-        for h in range(w.shape[1] // lanes):
-            at = slice(h * lanes, (h + 1) * lanes)
-            turned = dot_n(w[:, at], part_ref[...]).astype(bf16)
-            moved = dot_n(bias[:, at].astype(bf16), part_ref[...])[:1]
-            other = dot_n(x_ref[...], turned) + moved
-            out_ref[:, at] = ((mixed[:, at] * cos_ref[...] + other * sin_ref[...]) * by).astype(bf16)
+        for left in range(0, w.shape[1], wide):
+            x = mixed[:, left : left + wide]
+            upper = x.astype(bf16)
+            lower = (x - upper.astype(f32)).astype(bf16)
+            other = dot_n(upper, part_ref[...]) + dot_n(lower, part_ref[...])
+            for at in range(0, wide, lanes):
+                here = mixed[:, left + at : left + at + lanes] * cos_ref[...]
+                there = other[:, at : at + lanes] * sin_ref[...]
+                out_ref[:, left + at : left + at + lanes] = ((here + there) * by).astype(bf16)
 
     @pl.when(j >= 2 * third)
     def _():
@@ -530,8 +572,11 @@
 
 def project(x, w, bias, cosine, sine, partner):
     rows, width = x.shape
-    cols = 256
+    cols = 512
     lanes = 2 * HEAD
+    wide = 2 * lanes
+    zero = jnp.zeros_like(partner)
+    partner = jnp.block([[partner, zero], [zero, partner]])
 
     def whole(j):
         return (0, 0)
@@ -545,12 +590,12 @@
             pl.BlockSpec((1, cols), lambda j: (0, j)),
             pl.BlockSpec((rows, lanes), whole),
             pl.BlockSpec((rows, lanes), whole),
-            pl.BlockSpec((lanes, lanes), whole),
+            pl.BlockSpec((wide, wide), whole),
         ],
         out_specs=pl.BlockSpec((rows, cols), lambda j: (0, j)),
         out_shape=jax.ShapeDtypeStruct((rows, w.shape[1]), bf16),
         compiler_params=pltpu.CompilerParams(vmem_limit_bytes=vmem_most),
-        cost_estimate=cost(6),
+        cost_estimate=cost(4),
     )(x, w, bias, cosine, sine, partner)
 
 
@@ -605,7 +650,7 @@
     query = jnp.arange(FEW, dtype=jnp.int32)[None, :] // 2
     count = jnp.repeat(seen, 2)[None, :]
     allowed = ((frame <= query) & (frame > query - count)) | jnp.asarray(own)
-    return jnp.tile(jnp.where(allowed, 0.0, masked_value), (1, 2))
+    return jnp.tile(jnp.where(allowed, 0.0, masked_value), (1, 2 * PAIRS))
 
 
 def place(p, line, orders, core):
@@ -677,36 +722,47 @@
     pltpu.make_async_copy(wu.at[slot], wu.at[slot], in_sem.at[0, slot]).wait()
     pltpu.make_async_copy(wd.at[slot], wd.at[slot], in_sem.at[1, slot]).wait()
     half = cols // 2
-    for h in range(2):
-        at = slice(h * half, (h + 1) * half)
-        u = dot_n(x_ref[...], wu[slot, :, at]) + bias_ref[:, at]
-        ga = dot_t(g_ref[...], wd[slot, at, :])
-        e = jnp.exp(u * u * -0.5)
+    low, high = slice(0, half), slice(half, cols)
+
+    def curves(u, ga):
+        e = jnp.exp2(u * u * (-0.5 * math.log2(math.e)))
         d = 1.0 + jnp.abs(u) * (0.3275911 * inv_sqrt_two)
         t = pl.reciprocal(d, approx=True)
         t = t * (2.0 - d * t)
         poly = t * (0.127414796 + t * (-0.142248368 + t * (0.7107068705 + t * (-0.7265760135 + t * 0.5307027145))))
         tail = poly * e
         phi = jnp.where(u >= 0.0, 1.0 - tail, tail)
-        act[:, at] = (u * phi).astype(bf16)
-        gu = (ga * (phi + u * (e * inv_sqrt_tau))).astype(bf16)
-        gup[:, at] = gu
-        gb_ref[:, at] = jnp.sum(gu.astype(f32), axis=0, keepdims=True)
+        gu = ga * (phi + u * (e * inv_sqrt_tau))
+        return (u * phi).astype(bf16), gu.astype(bf16), jnp.sum(gu, axis=0, keepdims=True)
+
+    u0 = dot_n(x_ref[...], wu[slot, :, low]) + bias_ref[:, low]
+    g0 = dot_t(g_ref[...], wd[slot, low, :])
+    u1 = dot_n(x_ref[...], wu[slot, :, high]) + bias_ref[:, high]
+    g1 = dot_t(g_ref[...], wd[slot, high, :])
+    a, g, total = curves(u0, g0)
+    act[:, low] = a
+    gup[:, low] = g
+    gb_ref[:, low] = total
+
+    @pl.when(i >= 2)
+    def _():
+        pltpu.make_async_copy(su.at[slot], su.at[slot], out_sem.at[0, slot]).wait()
+        pltpu.make_async_copy(sd.at[slot], sd.at[slot], out_sem.at[1, slot]).wait()
 
     @pl.when(i == 0)
     def _():
         middle.wait()
 
+    sd[slot, low, :] = dot_tl(act[:, low], g_ref[...]).astype(bf16)
+    su[slot, :, low] = dot_n(xt[...], gup[:, low]).astype(bf16)
+    a, g, total = curves(u1, g1)
+    act[:, high] = a
+    gup[:, high] = g
+    gb_ref[:, high] = total
     acc[...] += dot_n(act[...], wd[slot])
     gx_ref[...] += dot_t(gup[...], wu[slot])
-
-    @pl.when(i >= 2)
-    def _():
-        pltpu.make_async_copy(su.at[slot], su.at[slot], out_sem.at[0, slot]).wait()
-        pltpu.make_async_copy(sd.at[slot], sd.at[slot], out_sem.at[1, slot]).wait()
-
-    sd[slot] = dot_tl(act[...], g_ref[...]).astype(bf16)
-    su[slot] = dot_n(xt[...], gup[...]).astype(bf16)
+    sd[slot, high, :] = dot_tl(act[:, high], g_ref[...]).astype(bf16)
+    su[slot, :, high] = dot_n(xt[...], gup[:, high]).astype(bf16)
     at = pl.multiple_of(group(i) * cols, cols)
     for p in range(count):
         c, n = place(p, *where)
@@ -738,7 +794,7 @@
             pltpu.make_async_copy(sd.at[s], sd.at[s], out_sem.at[1, s]).wait()
 
 
-FEED_BLOCKS = 8
+FEED_BLOCKS = 4
 
 
 def feed(x, grad, middle, bias, shift, up, pieces, line, orders, core, me):
@@ -1132,12 +1188,19 @@
     )
     steps = len(orders[0])
     for step in range(1, steps):
+        feed_sums = [(kept, after(came, grad_mixed)) for kept, came in together(feed_sums)]
         feed_sums = reduce_next(feed_sums, orders, step, sizes)
         grad_mixed = after(grad_mixed, *[v for group in feed_sums for v in group[:1] + group[2:]])
         feed_sums = [group[:2] for group in feed_sums]
     own, other = weight_grad(normed_one, grad_mixed, where, 0, third + width, me, grads)
     taken = swap(other, 1 << core, sizes)
-    grad_mixed = after(grad_mixed, other)
+    feed_parts = line_parts(together(feed_sums))
+    feed_parts = feed_parts[:1] + [v.astype(bf16) for v in feed_parts[1:]]
+    own = after(own, *feed_parts[1:])
+    sums = reduce_start(own, taken, orders, sizes)
+    going = [v for group in sums for v in group[:1] + group[2:]]
+    sums = [group[:2] for group in sums]
+    grad_mixed = after(grad_mixed, *going)
     grad_tokens, grad_gain_one, grad_bias_one, grad_b_qkv_local = last_step(
         grad_mixed, qkv_matrix, tokens_in, grad_middle, gain_one[None]
     )
@@ -1152,19 +1215,22 @@
         grad_b_down_local[0],
     ]
     small_own, small_other = small_units(vectors, rows, where, me)
-    sums = reduce_start(
-        own, taken, orders, sizes, jnp.concatenate([small_own, small_other], axis=2)
-    )
-    feed_parts = line_parts(feed_sums)
-    going = [v for group in sums for v in group[:1] + group[2:]]
-    feed_parts = feed_parts[:1] + [after(v.astype(bf16), *going) for v in feed_parts[1:]]
-    sums = [group[:2] for group in sums]
+    small = jnp.concatenate([small_own, small_other], axis=2).astype(bf16)
+    half = small.shape[0] // 2
+    joined = []
+    for (kept, came), at, order in zip(sums, (0, half), orders):
+        here = small[at : at + half // 2]
+        there = swap(small[at + half // 2 : at + half], 1 << order[-1], sizes)
+        joined.append(
+            (jnp.concatenate([kept, here], axis=2), jnp.concatenate([came, there], axis=2))
+        )
+    sums = joined
     for step in range(1, steps):
         sums = [group[:2] for group in reduce_next(sums, orders, step, sizes)]
     parts = line_parts(sums)
     parts = parts[:1] + [v.astype(bf16) for v in parts[1:]]
     feed_parts[0] = after(feed_parts[0], *parts[1:])
-    result = after(result, *going)
+    result = after(result, *parts[1:])
     feed_sum = reduce_line(feed_parts, line, sizes)
     sum_one = reduce_line(parts, line, sizes)
     output = unsort_rows(result)

time: 538 us -> 491 us (0.913)
  the two profiles are of different devices: /device:TPU:9 before, /device:TPU:1 now
where the time goes in v3:
time: 491 us; the launch traced here: 484 us
  Pallas kernels  207 us (42%)
  waiting for transfers between devices  89.7 us (18%)
  other arithmetic  62 us (13%)
  starting transfers between devices  57.5 us (12%)
  local copies, waits for them, and re-layouts  41.8 us (9%)
  between operations  15 us (3%)
  matrix products  10.8 us (2%)
    ppermute x41, waiting for transfers between devices, swap(): lax.ppermute(value, ('dp', 'fsdp'), [(i, i ^ mask) for i in range(count)])  87.3 us
    pallas_call x1, Pallas kernels, feed(): pl.pallas_call(functools.partial(feed_kernel, rels, (line, orders, core))...  79.2 us
    ppermute x41, starting transfers between devices, swap(): lax.ppermute(value, ('dp', 'fsdp'), [(i, i ^ mask) for i in range(count)])  57.4 us
    pallas_call x2, Pallas kernels, attend_back(): pl.pallas_call(kernel, grid_spec=pltpu.PrefetchScalarGridSpec(num_scalar_...  36.6 us
    pallas_call x2, Pallas kernels, attend(): pl.pallas_call(kernel, grid_spec=pltpu.PrefetchScalarGridSpec(num_scalar_...  22.8 us
    unnamed x115, local copies, waits for them, and re-layouts  20.1 us
    pallas_call x2, Pallas kernels, weight_grad(): pl.pallas_call(functools.partial(weight_kernel, where, left, count), grid...  19.7 us
    pallas_call x1, Pallas kernels, last_step(): pl.pallas_call(last_kernel, grid=(parts,), in_specs=[pl.BlockSpec((1, row...  19.1 us
  transfers between devices with their start and end apart: 43, of which 17 were waited for; matrix products, arithmetic and copies ran while one was open for 17% of the time, Pallas kernels for 26%

profile of v3, /device:TPU:1, one launch (start us, length us, event | category | flops | bytes accessed | tf_op | source)
XLA Modules:
  0.0 483.8 jit_solution(10796226014465852941)
XLA Ops:
  14.5 4.2 collective-permute-start.4
  26.5 5.5 %shard_map.380 = (bf16[1040,1024]{1,0:T(8,128)(2,1)}, bf16[1040,1024]{1,0:T(8,128)(2,1)}, f32[1,1024]{1,0:T(1,128)}) custom-call(bf16[1032,1024]{1,0:T(8,128)(2,1)} %x_ref.1, bf16[1032,1024]{1,0:T(8,128)(2,1)} %g_ref.1), custom_call_target="tpu_custom_call" | custom-call | flops 1000000000 | tf_op jit(solution)/shard_map/pallas_call | solution.py:939
  33.9 3.9 collective-permute-done.3
  41.2 7.7 %collective-permute-done.5 = bf16[2,32,3328]{2,1,0:T(8,128)(2,1)S(1)} collective-permute-done((bf16[2,32,3328]{2,1,0:T(8,128)(2,1)S(1)}, bf16[2,32,3328]{2,1,0:T(8,128)(2,1)S(1)}, u32[]{:S(2)}, u32[]{:S(2)}) %collective-permute-start.5) | collective-permute-done | bytes 426016 | tf_op jit(solution)/shard_map/ppermute | solution.py:41
  53.8 4.3 collective-permute-start.9
  58.1 15.6 %collective-permute-done.6.refs_3_ = bf16[4,32,3328]{2,1,0:T(8,128)(2,1)S(1)} collective-permute-done((bf16[4,32,3328]{2,1,0:T(8,128)(2,1)S(1)}, bf16[4,32,3328]{2,1,0:T(8,128)(2,1)S(1)}, u32[]{:S(2)}, u32[]{:S(2)}) %collective-permute-start.6) | collective-permute-done | bytes 852000 | tf_op jit(solution)/shard_map/ppermute | solution.py:41
  81.9 5.8 %shard_map.381 = (bf16[1024,3072]{1,0:T(8,128)(2,1)}, bf16[1024,256]{1,0:T(8,128)(2,1)}) custom-call(s32[1]{0:T(128)} %bitcast.me_ref, bf16[4,32,3328]{2,1,0:T(8,128)(2,1)} %copy-done.19, bf16[4,32,3328]{2,1,0:T(8,128)(2,1)} %copy-done.35, bf16[4,32,3328]{2,1,0:T(8,128)(2,1)} %copy-done.33, bf16[4,32,3328]{2,1,0:T(8,128)(2,1)} %copy-done.34, ...), custom_call_target="tpu_custom_call" | custom-call | flops 1500000000 | tf_op jit(solution)/shard_map/pallas_call | solution.py:171
  99.1 14.9 %shard_map.382.q_ref.k_ref.v_ref.refs_1_.refs_2_.refs_3_ = bf16[1040,3072]{1,0:T(8,128)(2,1)} custom-call(bf16[1040,1024]{1,0:T(8,128)(2,1)} %fusion.6.x_ref, bf16[1024,3072]{1,0:T(8,128)(2,1)} %get-tuple-element.40.w_ref.refs_1_, f32[1,3072]{1,0:T(1,128)} %reshape_reshape.3.b_ref, f32[1040,128]{1,0:T(8,128)} %get-tuple-element.118.cos_ref.refs_9_, ...), custom_call_target="tpu_custom_call" | custom-call | flops 4000000000 | tf_op jit(solution)/shard_map/pallas_call | solution.py:584
  120.8 11.5 %shard_map.383 = (bf16[1040,1024]{1,0:T(8,128)(2,1)}, f32[1,8,1024]{2,1,0:T(8,128)}, f32[1,1,64]{2,1,0:T(1,128)}) custom-call(s32[4]{0:T(128)} %copy-done.43, bf16[1040,3072]{1,0:T(8,128)(2,1)} %shard_map.382.q_ref.k_ref.v_ref.refs_1_.refs_2_.refs_3_, bf16[1040,3072]{1,0:T(8,128)(2,1)} %shard_map.382.q_ref.k_ref.v_ref.refs_1_.refs_2_.refs_3_, ...), custom_call_target="tpu_custom_call" | custom-call | flops 6400000000 | tf_op jit(solution)/shard_map/pallas_call | solution.py:365
  138.5 5.1 %collective-permute-done.18.refs_0_ = bf16[2,32,4096]{2,1,0:T(8,128)(2,1)S(1)} collective-permute-done((bf16[2,32,4096]{2,1,0:T(8,128)(2,1)}, bf16[2,32,4096]{2,1,0:T(8,128)(2,1)S(1)}, u32[]{:S(2)}, u32[]{:S(2)}) %collective-permute-start.18) | collective-permute-done | bytes 524320 | tf_op jit(solution)/shard_map/ppermute | solution.py:41
  149.0 11.3 %shard_map.384 = (bf16[1040,1024]{1,0:T(8,128)(2,1)}, f32[1,8,1024]{2,1,0:T(8,128)}, f32[1,1,64]{2,1,0:T(1,128)}) custom-call(s32[4]{0:T(128)} %copy-done.43, bf16[1040,3072]{1,0:T(8,128)(2,1)} %shard_map.382.q_ref.k_ref.v_ref.refs_1_.refs_2_.refs_3_, ...), custom_call_target="tpu_custom_call", output_to_operand_aliasing={{0}: (5, {})} | custom-call | flops 6400000000 | tf_op jit(solution)/shard_map/pallas_call | solution.py:365
  160.3 7.4 %collective-permute-done.20 = bf16[2,32,4096]{2,1,0:T(8,128)(2,1)S(1)} collective-permute-done((bf16[2,32,4096]{2,1,0:T(8,128)(2,1)}, bf16[2,32,4096]{2,1,0:T(8,128)(2,1)S(1)}, u32[]{:S(2)}, u32[]{:S(2)}) %collective-permute-start.20) | collective-permute-done | bytes 524320 | tf_op jit(solution)/shard_map/ppermute | solution.py:41
  172.2 4.6 collective-permute-start.15
  176.9 4.8 fusion.34
  186.9 79.2 %shard_map.394 = (bf16[1040,1024]{1,0:T(8,128)(2,1)}, f32[1040,1024]{1,0:T(8,128)}, f32[1,4096]{1,0:T(1,128)}, bf16[16,32,8192]{2,1,0:T(8,128)(2,1)}, bf16[16,32,8192]{2,1,0:T(8,128)(2,1)}) custom-call(s32[1]{0:T(128)} %bitcast.me_ref, bf16[1040,1024]{1,0:T(8,128)(2,1)} %add_convert_fusion.x_ref, bf16[1040,1024]{1,0:T(8,128)(2,1)} %get-tuple-element.43.g_ref, ...), custom_call_target="tpu_custom_call" | custom-call | flops 20000000000 | tf_op jit(solution)/shard_map/pallas_call | solution.py:816
  266.6 5.3 %multiply_reduce_fusion = (bf16[1024]{0:T(1024)(128)(2,1)S(1)}, f32[1040]{0:T(1024)S(1)}, f32[1040]{0:T(1024)S(1)}, bf16[1024]{0:T(1024)(128)(2,1)S(1)}) fusion(f32[1040,1024]{1,0:T(8,128)} %get-tuple-element.45, f32[1040,1024]{1,0:T(8,128)} %copy-done.1, f32[1040]{0:T(1024)S(1)} %add_rsqrt_fusion, f32[1040]{0:T(1024)S(1)} %broadcast_multiply_fusion.2, ...), kind=kLoop, calls=%fused_computation.11 | loop fusion | flops 9580512 | bytes 8544512 | tf_op jit(solution)/shard_map/reduce_sum | solution.py:1172
  271.9 7.7 %collective-permute-done.22 = bf16[16,32,8192]{2,1,0:T(8,128)(2,1)S(1)} collective-permute-done((bf16[16,32,8192]{2,1,0:T(8,128)(2,1)}, bf16[16,32,8192]{2,1,0:T(8,128)(2,1)S(1)}, u32[]{:S(2)}, u32[]{:S(2)}) %collective-permute-start.22) | collective-permute-done | bytes 8388640 | tf_op jit(solution)/shard_map/ppermute | solution.py:41
  279.7 4.9 %add_convert_fusion.1 = (bf16[4,32,8192]{2,1,0:T(8,128)(2,1)}, bf16[4,32,8192]{2,1,0:T(8,128)(2,1)}, bf16[4,32,8192]{2,1,0:T(8,128)(2,1)}, bf16[4,32,8192]{2,1,0:T(8,128)(2,1)}) fusion(bf16[16,32,8192]{2,1,0:T(8,128)(2,1)S(1)} %collective-permute-done.22, bf16[16,32,8192]{2,1,0:T(8,128)(2,1)S(1)} %copy-done.13), kind=kLoop, calls=%fused_computation.17 | loop fusion | flops 16777216 | bytes 25165824 | tf_op jit(solution)/shard_map/convert_element_type | solution.py:98
  288.2 4.8 convert_reduce_fusion.1
  293.0 6.7 %shard_map.395 = (bf16[16,32,4096]{2,1,0:T(8,128)(2,1)}, bf16[16,32,4096]{2,1,0:T(8,128)(2,1)}) custom-call(s32[1]{0:T(128)} %bitcast.me_ref, bf16[1040,1024]{1,0:T(8,128)(2,1)} %get-tuple-element.42.refs_1_.x_ref.o_ref.refs_4_, bf16[1040,1024]{1,0:T(8,128)(2,1)} %get-tuple-element.73.g_ref), custom_call_target="tpu_custom_call" | custom-call | flops 1000000000 | tf_op jit(solution)/shard_map/pallas_call | solution.py:904
  299.7 6.0 %convolution_convert_fusion.refs_0_ = bf16[1040,1024]{1,0:T(8,128)(2,1)} fusion(bf16[1040,1024]{1,0:T(8,128)(2,1)} %get-tuple-element.73.g_ref, bf16[1024,1024]{1,0:T(8,128)(2,1)} %all-gather.3.cloned.1.call-done), kind=kOutput, calls=%fused_computation.22 | convolution fusion | flops 2182103040 | bytes 6356992 | tf_op jit(solution)/shard_map/dot_general | solution.py:234
  305.6 18.1 %shard_map.397.refs_12_ = bf16[3,1040,1024]{2,1,0:T(8,128)(2,1)} custom-call(s32[4]{0:T(128)} %copy-done.43, bf16[1040,3072]{1,0:T(8,128)(2,1)} %shard_map.382.q_ref.k_ref.v_ref.refs_1_.refs_2_.refs_3_, bf16[1040,3072]{1,0:T(8,128)(2,1)} %shard_map.382.q_ref.k_ref.v_ref.refs_1_.refs_2_.refs_3_, ...), custom_call_target="tpu_custom_call" | custom-call | flops 7600000000 | tf_op jit(solution)/shard_map/pallas_call | solution.py:513
  323.8 18.5 %shard_map.398.refs_1_.refs_0_ = bf16[3,1040,1024]{2,1,0:T(8,128)(2,1)} custom-call(s32[4]{0:T(128)} %copy-done.43, bf16[1040,3072]{1,0:T(8,128)(2,1)} %shard_map.382.q_ref.k_ref.v_ref.refs_1_.refs_2_.refs_3_, bf16[1040,3072]{1,0:T(8,128)(2,1)} %shard_map.382.q_ref.k_ref.v_ref.refs_1_.refs_2_.refs_3_, ...), custom_call_target="tpu_custom_call", output_to_operand_aliasing={{}: (12, {})} | custom-call | flops 7600000000 | tf_op jit(solution)/shard_map/pallas_call | solution.py:513
  348.4 3.8 add_convert_fusion.11
  352.8 13.1 %shard_map.404 = (bf16[16,32,4096]{2,1,0:T(8,128)(2,1)}, bf16[16,32,4096]{2,1,0:T(8,128)(2,1)}) custom-call(s32[1]{0:T(128)} %bitcast.me_ref, bf16[1040,1024]{1,0:T(8,128)(2,1)} %fusion.6.x_ref, bf16[3,1040,1024]{2,1,0:T(8,128)(2,1)} %shard_map.403.g_ref.refs_0_, ...), custom_call_target="tpu_custom_call", output_to_operand_aliasing={{0}: (3, {}), {1}: (4, {})} | custom-call | flops 3000000000 | tf_op jit(solution)/shard_map/pallas_call | solution.py:904
  365.9 4.3 collective-permute-start.27
  379.3 7.0 %collective-permute-start.40 = (bf16[32,8192]{1,0:T(8,128)(2,1)}, bf16[32,8192]{1,0:T(8,128)(2,1)}, u32[]{:S(2)}, u32[]{:S(2)}) collective-permute-start(bf16[32,8192]{1,0:T(8,128)(2,1)} %get-tuple-element.93.refs_3_), channel_id=1, source_target_pairs={{0,6},{1,7},{2,4},{3,5},{4,2},{5,3},{6,0},{7,1},{8,14},{9,15},{10,... | collective-permute-start | bytes 1572872 | tf_op jit(solution)/shard_map/ppermute | solution.py:41
  389.0 5.2 %add_convert_fusion.5 = (bf16[4,32,4096]{2,1,0:T(8,128)(2,1)S(1)}, bf16[4,32,4096]{2,1,0:T(8,128)(2,1)}, bf16[4,32,4096]{2,1,0:T(8,128)(2,1)S(1)}, bf16[4,32,4096]{2,1,0:T(8,128)(2,1)}) fusion(bf16[16,32,4096]{2,1,0:T(8,128)(2,1)} %collective-permute-done.27, bf16[16,32,4096]{2,1,0:T(8,128)(2,1)} %shard_map.407), kind=kLoop, calls=%fused_computation.26 | loop fusion | flops 8388608 | bytes 12582912 | tf_op jit(solution)/shard_map/convert_element_type | solution.py:98
  395.6 19.1 %shard_map.409 = (f32[1032,1024]{1,0:T(8,128)}, f32[1,1024]{1,0:T(1,128)}, f32[1,1024]{1,0:T(1,128)}, f32[3,1,1024]{2,1,0:T(1,128)}) custom-call(bf16[3,1040,1024]{2,1,0:T(8,128)(2,1)} %shard_map.408.g_ref, bf16[1024,3072]{1,0:T(8,128)(2,1)} %get-tuple-element.40.w_ref.refs_1_, bf16[1040,1024]{1,0:T(8,128)(2,1)} %get-tuple-element.38.x_ref, ...), custom_call_target="tpu_custom_call" | custom-call | flops 5000000000 | tf_op jit(solution)/shard_map/pallas_call | solution.py:1022
  429.1 10.3 %collective-permute-done.33 = bf16[2,32,4352]{2,1,0:T(8,128)(2,1)S(1)} collective-permute-done((bf16[2,32,4352]{2,1,0:T(8,128)(2,1)S(1)}, bf16[2,32,4352]{2,1,0:T(8,128)(2,1)S(1)}, u32[]{:S(2)}, u32[]{:S(2)}) %collective-permute-start.33) | collective-permute-done | bytes 557088 | tf_op jit(solution)/shard_map/ppermute | solution.py:41
  447.6 20.1 %collective-permute-done.35 = bf16[32,4352]{1,0:T(8,128)(2,1)S(1)} collective-permute-done((bf16[32,4352]{1,0:T(8,128)(2,1)S(1)}, bf16[32,4352]{1,0:T(8,128)(2,1)S(1)}, u32[]{:S(2)}, u32[]{:S(2)}) %collective-permute-start.35) | collective-permute-done | bytes 278560 | tf_op jit(solution)/shard_map/ppermute | solution.py:41
  468.5 3.6 shard_map.411
  (317 shorter events, 124.9 us)
Async XLA Ops:
  7.2 169.7 %all-gather.3.cloned.1.call-start = ((), (), s32[]{:S(2)}) async-start(), calls=%async_computation | async-start | bytes 2162688 | tf_op jit(solution)/shard_map/all_gather | solution.py:1109
  8.0 178.9 %all-gather.5.cloned.1.call-start = ((), (), s32[]{:S(2)}) async-start(), calls=%async_computation.1 | async-start | bytes 8650752 | tf_op jit(solution)/shard_map/all_gather | solution.py:1110
  14.5 19.4 %collective-permute-start.4 = (bf16[1,32,3328]{2,1,0:T(8,128)(2,1)S(1)}, bf16[1,32,3328]{2,1,0:T(8,128)(2,1)S(1)}, u32[]{:S(2)}, u32[]{:S(2)}) collective-permute-start(bf16[1,32,3328]{2,1,0:T(8,128)(2,1)S(1)} %fusion.19), channel_id=1, source_target_pairs={{0,6},{1,7},{2,4},{3,5},{4,2},{5,3},{6,0},{7,1},{8,14},{9,15},{10,... | collective-permute-start | bytes 638984 | tf_op jit(solution)/shard_map/ppermute | solution.py:41
  18.7 19.1 %collective-permute-start.3 = (bf16[1,32,3328]{2,1,0:T(8,128)(2,1)S(1)}, bf16[1,32,3328]{2,1,0:T(8,128)(2,1)S(1)}, u32[]{:S(2)}, u32[]{:S(2)}) collective-permute-start(bf16[1,32,3328]{2,1,0:T(8,128)(2,1)S(1)} %fusion.19), channel_id=1, source_target_pairs={{0,4},{1,5},{2,6},{3,7},{4,0},{5,1},{6,2},{7,3},{8,12},{9,13},{10,... | collective-permute-start | bytes 638984 | tf_op jit(solution)/shard_map/ppermute | solution.py:41
  18.7 20.4 %collective-permute-start = (bf16[1,32,3328]{2,1,0:T(8,128)(2,1)S(1)}, bf16[1,32,3328]{2,1,0:T(8,128)(2,1)S(1)}, u32[]{:S(2)}, u32[]{:S(2)}) collective-permute-start(bf16[1,32,3328]{2,1,0:T(8,128)(2,1)S(1)} %fusion.19), channel_id=1, source_target_pairs={{0,2},{1,3},{2,0},{3,1},{4,6},{5,7},{6,4},{7,5},{8,10},{9,11},{10,... | collective-permute-start | bytes 638984 | tf_op jit(solution)/shard_map/ppermute | solution.py:41
  48.9 24.8 %collective-permute-start.6 = (bf16[4,32,3328]{2,1,0:T(8,128)(2,1)S(1)}, bf16[4,32,3328]{2,1,0:T(8,128)(2,1)S(1)}, u32[]{:S(2)}, u32[]{:S(2)}) collective-permute-start(bf16[4,32,3328]{2,1,0:T(8,128)(2,1)S(1)} %constant_dynamic-update-slice_fusion.refs_2_), channel_id=1, source_target_pairs={{0,1},{1,0},{2,3},{3,2},{4,5},{5,4},{6,7},{7,6},{8,9},{9,8},{10,11... | collective-permute-start | bytes 2555912 | tf_op jit(solution)/shard_map/ppermute | solution.py:41
  52.5 23.4 %collective-permute-start.2 = (bf16[4,32,3328]{2,1,0:T(8,128)(2,1)S(1)}, bf16[4,32,3328]{2,1,0:T(8,128)(2,1)S(1)}, u32[]{:S(2)}, u32[]{:S(2)}) collective-permute-start(bf16[4,32,3328]{2,1,0:T(8,128)(2,1)S(1)} %pad_maximum_fusion.2.refs_0_), channel_id=1, source_target_pairs={{0,16},{1,17},{2,18},{3,19},{4,20},{5,21},{6,22},{7,23},{8,24},{9,... | collective-permute-start | bytes 2555912 | tf_op jit(solution)/shard_map/ppermute | solution.py:41
  53.8 25.7 %collective-permute-start.9 = (bf16[4,32,3328]{2,1,0:T(8,128)(2,1)S(1)}, bf16[4,32,3328]{2,1,0:T(8,128)(2,1)S(1)}, u32[]{:S(2)}, u32[]{:S(2)}) collective-permute-start(bf16[4,32,3328]{2,1,0:T(8,128)(2,1)S(1)} %constant_dynamic-update-slice_fusion.refs_2_), channel_id=1, source_target_pairs={{0,8},{1,9},{2,10},{3,11},{4,12},{5,13},{6,14},{7,15},{8,0},{9,1},... | collective-permute-start | bytes 2555912 | tf_op jit(solution)/shard_map/ppermute | solution.py:41
  58.0 21.4 %collective-permute-start.7 = (bf16[4,32,3328]{2,1,0:T(8,128)(2,1)S(1)}, bf16[4,32,3328]{2,1,0:T(8,128)(2,1)S(1)}, u32[]{:S(2)}, u32[]{:S(2)}) collective-permute-start(bf16[4,32,3328]{2,1,0:T(8,128)(2,1)S(1)} %pad_maximum_fusion.2.refs_0_), channel_id=1, source_target_pairs={{0,8},{1,9},{2,10},{3,11},{4,12},{5,13},{6,14},{7,15},{8,0},{9,1},... | collective-permute-start | bytes 2555912 | tf_op jit(solution)/shard_map/ppermute | solution.py:41
  87.7 29.9 %collective-permute-start.17 = (bf16[1,32,4096]{2,1,0:T(8,128)(2,1)}, bf16[1,32,4096]{2,1,0:T(8,128)(2,1)S(1)}, u32[]{:S(2)}, u32[]{:S(2)}) collective-permute-start(bf16[1,32,4096]{2,1,0:T(8,128)(2,1)} %bitcast.91), channel_id=1, source_target_pairs={{0,6},{1,7},{2,4},{3,5},{4,2},{5,3},{6,0},{7,1},{8,14},{9,15},{10,... | collective-permute-start | bytes 786440 | tf_op jit(solution)/shard_map/ppermute | solution.py:41
  89.6 28.0 %collective-permute-start.16 = (bf16[1,32,4096]{2,1,0:T(8,128)(2,1)}, bf16[1,32,4096]{2,1,0:T(8,128)(2,1)}, u32[]{:S(2)}, u32[]{:S(2)}) collective-permute-start(bf16[1,32,4096]{2,1,0:T(8,128)(2,1)} %bitcast.92), channel_id=1, source_target_pairs={{0,4},{1,5},{2,6},{3,7},{4,0},{5,1},{6,2},{7,3},{8,12},{9,13},{10,... | collective-permute-start | bytes 786440 | tf_op jit(solution)/shard_map/ppermute | solution.py:41
  89.6 24.3 %collective-permute-start.11 = (bf16[1,32,4096]{2,1,0:T(8,128)(2,1)}, bf16[1,32,4096]{2,1,0:T(8,128)(2,1)}, u32[]{:S(2)}, u32[]{:S(2)}) collective-permute-start(bf16[1,32,4096]{2,1,0:T(8,128)(2,1)} %bitcast.93), channel_id=1, source_target_pairs={{0,2},{1,3},{2,0},{3,1},{4,6},{5,7},{6,4},{7,5},{8,10},{9,11},{10,... | collective-permute-start | bytes 786440 | tf_op jit(solution)/shard_map/ppermute | solution.py:41
  115.7 32.5 %collective-permute-start.13 = (bf16[2,32,4096]{2,1,0:T(8,128)(2,1)}, bf16[2,32,4096]{2,1,0:T(8,128)(2,1)S(1)}, u32[]{:S(2)}, u32[]{:S(2)}) collective-permute-start(bf16[2,32,4096]{2,1,0:T(8,128)(2,1)} %shard_map.386), channel_id=1, source_target_pairs={{0,16},{1,17},{2,18},{3,19},{4,20},{5,21},{6,22},{7,23},{8,24},{9,... | collective-permute-start | bytes 1572872 | tf_op jit(solution)/shard_map/ppermute | solution.py:41
  116.1 19.6 %collective-permute-start.12 = (bf16[2,32,4096]{2,1,0:T(8,128)(2,1)}, bf16[2,32,4096]{2,1,0:T(8,128)(2,1)S(1)}, u32[]{:S(2)}, u32[]{:S(2)}) collective-permute-start(bf16[2,32,4096]{2,1,0:T(8,128)(2,1)} %shard_map.386), channel_id=1, source_target_pairs={{0,1},{1,0},{2,3},{3,2},{4,5},{5,4},{6,7},{7,6},{8,9},{9,8},{10,11... | collective-permute-start | bytes 1572872 | tf_op jit(solution)/shard_map/ppermute | solution.py:41
  119.4 28.0 %collective-permute-start.19 = (bf16[2,32,4096]{2,1,0:T(8,128)(2,1)}, bf16[2,32,4096]{2,1,0:T(8,128)(2,1)S(1)}, u32[]{:S(2)}, u32[]{:S(2)}) collective-permute-start(bf16[2,32,4096]{2,1,0:T(8,128)(2,1)} %shard_map.390), channel_id=1, source_target_pairs={{0,1},{1,0},{2,3},{3,2},{4,5},{5,4},{6,7},{7,6},{8,9},{9,8},{10,11... | collective-permute-start | bytes 1572872 | tf_op jit(solution)/shard_map/ppermute | solution.py:41
  120.3 23.3 %collective-permute-start.18 = (bf16[2,32,4096]{2,1,0:T(8,128)(2,1)}, bf16[2,32,4096]{2,1,0:T(8,128)(2,1)S(1)}, u32[]{:S(2)}, u32[]{:S(2)}) collective-permute-start(bf16[2,32,4096]{2,1,0:T(8,128)(2,1)} %shard_map.390), channel_id=1, source_target_pairs={{0,16},{1,17},{2,18},{3,19},{4,20},{5,21},{6,22},{7,23},{8,24},{9,... | collective-permute-start | bytes 1572872 | tf_op jit(solution)/shard_map/ppermute | solution.py:41
  136.5 32.8 %collective-permute-start.14 = (bf16[2,32,4096]{2,1,0:T(8,128)(2,1)}, bf16[2,32,4096]{2,1,0:T(8,128)(2,1)S(1)}, u32[]{:S(2)}, u32[]{:S(2)}) collective-permute-start(bf16[2,32,4096]{2,1,0:T(8,128)(2,1)} %shard_map.387), channel_id=1, source_target_pairs={{0,16},{1,17},{2,18},{3,19},{4,20},{5,21},{6,22},{7,23},{8,24},{9,... | collective-permute-start | bytes 1572872 | tf_op jit(solution)/shard_map/ppermute | solution.py:41
  144.4 23.3 %collective-permute-start.20 = (bf16[2,32,4096]{2,1,0:T(8,128)(2,1)}, bf16[2,32,4096]{2,1,0:T(8,128)(2,1)S(1)}, u32[]{:S(2)}, u32[]{:S(2)}) collective-permute-start(bf16[2,32,4096]{2,1,0:T(8,128)(2,1)} %shard_map.391), channel_id=1, source_target_pairs={{0,1},{1,0},{2,3},{3,2},{4,5},{5,4},{6,7},{7,6},{8,9},{9,8},{10,11... | collective-permute-start | bytes 1572872 | tf_op jit(solution)/shard_map/ppermute | solution.py:41
  266.1 13.6 %collective-permute-start.22 = (bf16[16,32,8192]{2,1,0:T(8,128)(2,1)}, bf16[16,32,8192]{2,1,0:T(8,128)(2,1)S(1)}, u32[]{:S(2)}, u32[]{:S(2)}) collective-permute-start(bf16[16,32,8192]{2,1,0:T(8,128)(2,1)} %get-tuple-element.48), channel_id=1, source_target_pairs={{0,8},{1,9},{2,10},{3,11},{4,12},{5,13},{6,14},{7,15},{8,0},{9,1},... | collective-permute-start | bytes 25165832 | tf_op jit(solution)/shard_map/ppermute | solution.py:41
  284.6 57.7 %collective-permute-start.24 = (bf16[4,32,8192]{2,1,0:T(8,128)(2,1)}, bf16[4,32,8192]{2,1,0:T(8,128)(2,1)S(1)}, u32[]{:S(2)}, u32[]{:S(2)}) collective-permute-start(bf16[4,32,8192]{2,1,0:T(8,128)(2,1)} %get-tuple-element.75.refs_5_), channel_id=1, source_target_pairs={{0,1},{1,0},{2,3},{3,2},{4,5},{5,4},{6,7},{7,6},{8,9},{9,8},{10,11... | collective-permute-start | bytes 6291464 | tf_op jit(solution)/shard_map/ppermute | solution.py:41
  286.6 55.7 %collective-permute-start.23 = (bf16[4,32,8192]{2,1,0:T(8,128)(2,1)}, bf16[4,32,8192]{2,1,0:T(8,128)(2,1)}, u32[]{:S(2)}, u32[]{:S(2)}) collective-permute-start(bf16[4,32,8192]{2,1,0:T(8,128)(2,1)} %get-tuple-element.77.refs_3_), channel_id=1, source_target_pairs={{0,16},{1,17},{2,18},{3,19},{4,20},{5,21},{6,22},{7,23},{8,24},{9,... | collective-permute-start | bytes 6291464 | tf_op jit(solution)/shard_map/ppermute | solution.py:41
  352.2 21.4 %collective-permute-start.25 = (bf16[2,32,8192]{2,1,0:T(8,128)(2,1)}, bf16[2,32,8192]{2,1,0:T(8,128)(2,1)S(1)}, u32[]{:S(2)}, u32[]{:S(2)}) collective-permute-start(bf16[2,32,8192]{2,1,0:T(8,128)(2,1)} %get-tuple-element.85.refs_2_), channel_id=1, source_target_pairs={{0,1},{1,0},{2,3},{3,2},{4,5},{5,4},{6,7},{7,6},{8,9},{9,8},{10,11... | collective-permute-start | bytes 3145736 | tf_op jit(solution)/shard_map/ppermute | solution.py:41
  352.2 21.4 %collective-permute-start.26 = (bf16[2,32,8192]{2,1,0:T(8,128)(2,1)S(1)}, bf16[2,32,8192]{2,1,0:T(8,128)(2,1)S(1)}, u32[]{:S(2)}, u32[]{:S(2)}) collective-permute-start(bf16[2,32,8192]{2,1,0:T(8,128)(2,1)S(1)} %get-tuple-element.83.refs_4_), channel_id=1, source_target_pairs={{0,16},{1,17},{2,18},{3,19},{4,20},{5,21},{6,22},{7,23},{8,24},{9,... | collective-permute-start | bytes 3145736 | tf_op jit(solution)/shard_map/ppermute | solution.py:41
  365.9 23.1 %collective-permute-start.27 = (bf16[16,32,4096]{2,1,0:T(8,128)(2,1)}, bf16[16,32,4096]{2,1,0:T(8,128)(2,1)}, u32[]{:S(2)}, u32[]{:S(2)}) collective-permute-start(bf16[16,32,4096]{2,1,0:T(8,128)(2,1)} %get-tuple-element.55), channel_id=1, source_target_pairs={{0,8},{1,9},{2,10},{3,11},{4,12},{5,13},{6,14},{7,15},{8,0},{9,1},... | collective-permute-start | bytes 12582920 | tf_op jit(solution)/shard_map/ppermute | solution.py:41
  379.3 64.2 %collective-permute-start.40 = (bf16[32,8192]{1,0:T(8,128)(2,1)}, bf16[32,8192]{1,0:T(8,128)(2,1)}, u32[]{:S(2)}, u32[]{:S(2)}) collective-permute-start(bf16[32,8192]{1,0:T(8,128)(2,1)} %get-tuple-element.93.refs_3_), channel_id=1, source_target_pairs={{0,6},{1,7},{2,4},{3,5},{4,2},{5,3},{6,0},{7,1},{8,14},{9,15},{10,... | collective-permute-start | bytes 1572872 | tf_op jit(solution)/shard_map/ppermute | solution.py:41
  386.4 58.5 %collective-permute-start.39 = (bf16[32,8192]{1,0:T(8,128)(2,1)}, bf16[32,8192]{1,0:T(8,128)(2,1)}, u32[]{:S(2)}, u32[]{:S(2)}) collective-permute-start(bf16[32,8192]{1,0:T(8,128)(2,1)} %get-tuple-element.94.refs_2_), channel_id=1, source_target_pairs={{0,4},{1,5},{2,6},{3,7},{4,0},{5,1},{6,2},{7,3},{8,12},{9,13},{10,... | collective-permute-start | bytes 1572872 | tf_op jit(solution)/shard_map/ppermute | solution.py:41
  389.0 55.9 %collective-permute-start.38 = (bf16[32,8192]{1,0:T(8,128)(2,1)}, bf16[32,8192]{1,0:T(8,128)(2,1)}, u32[]{:S(2)}, u32[]{:S(2)}) collective-permute-start(bf16[32,8192]{1,0:T(8,128)(2,1)} %get-tuple-element.92.refs_1_), channel_id=1, source_target_pairs={{0,2},{1,3},{2,0},{3,1},{4,6},{5,7},{6,4},{7,5},{8,10},{9,11},{10,... | collective-permute-start | bytes 1572872 | tf_op jit(solution)/shard_map/ppermute | solution.py:41
  394.2 27.0 %collective-permute-start.31 = (bf16[4,32,4096]{2,1,0:T(8,128)(2,1)S(1)}, bf16[4,32,4096]{2,1,0:T(8,128)(2,1)}, u32[]{:S(2)}, u32[]{:S(2)}) collective-permute-start(bf16[4,32,4096]{2,1,0:T(8,128)(2,1)S(1)} %get-tuple-element.79.refs_4_), channel_id=1, source_target_pairs={{0,1},{1,0},{2,3},{3,2},{4,5},{5,4},{6,7},{7,6},{8,9},{9,8},{10,11... | collective-permute-start | bytes 3145736 | tf_op jit(solution)/shard_map/ppermute | solution.py:41
  394.7 31.0 %collective-permute-start.28 = (bf16[4,32,4096]{2,1,0:T(8,128)(2,1)S(1)}, bf16[4,32,4096]{2,1,0:T(8,128)(2,1)}, u32[]{:S(2)}, u32[]{:S(2)}) collective-permute-start(bf16[4,32,4096]{2,1,0:T(8,128)(2,1)S(1)} %get-tuple-element.81.refs_2_), channel_id=1, source_target_pairs={{0,16},{1,17},{2,18},{3,19},{4,20},{5,21},{6,22},{7,23},{8,24},{9,... | collective-permute-start | bytes 3145736 | tf_op jit(solution)/shard_map/ppermute | solution.py:41
  425.7 13.7 %collective-permute-start.33 = (bf16[2,32,4352]{2,1,0:T(8,128)(2,1)S(1)}, bf16[2,32,4352]{2,1,0:T(8,128)(2,1)S(1)}, u32[]{:S(2)}, u32[]{:S(2)}) collective-permute-start(bf16[2,32,4352]{2,1,0:T(8,128)(2,1)S(1)} %get-tuple-element.88), channel_id=1, source_target_pairs={{0,16},{1,17},{2,18},{3,19},{4,20},{5,21},{6,22},{7,23},{8,24},{9,... | collective-permute-start | bytes 1671176 | tf_op jit(solution)/shard_map/ppermute | solution.py:41
  441.0 26.7 %collective-permute-start.35 = (bf16[32,4352]{1,0:T(8,128)(2,1)S(1)}, bf16[32,4352]{1,0:T(8,128)(2,1)S(1)}, u32[]{:S(2)}, u32[]{:S(2)}) collective-permute-start(bf16[32,4352]{1,0:T(8,128)(2,1)S(1)} %get-tuple-element.96.refs_2_), channel_id=1, source_target_pairs={{0,4},{1,5},{2,6},{3,7},{4,0},{5,1},{6,2},{7,3},{8,12},{9,13},{10,... | collective-permute-start | bytes 835592 | tf_op jit(solution)/shard_map/ppermute | solution.py:41
  444.5 23.2 %collective-permute-start.34 = (bf16[32,4352]{1,0:T(8,128)(2,1)S(1)}, bf16[32,4352]{1,0:T(8,128)(2,1)S(1)}, u32[]{:S(2)}, u32[]{:S(2)}) collective-permute-start(bf16[32,4352]{1,0:T(8,128)(2,1)S(1)} %copy-done.22), channel_id=1, source_target_pairs={{0,2},{1,3},{2,0},{3,1},{4,6},{5,7},{6,4},{7,5},{8,10},{9,11},{10,... | collective-permute-start | bytes 835592 | tf_op jit(solution)/shard_map/ppermute | solution.py:41
  (65 other events, 496.4 us)
Sparse Core Ops, SparseCore 0:
  11.0 68.8 all-gather.2
  82.9 103.9 all-gather.4

commit v4 on v3

--- a/solution.py
+++ b/solution.py
@@ -106,10 +106,9 @@
     ]
 
 
-def together(groups):
-    (kept, came), (other_kept, other_came) = groups
-    came = after(came, other_came)
-    return [(kept, came), (other_kept, after(other_came, came))]
+def together(groups, *others):
+    came = [group[1] for group in groups]
+    return [(after(kept, *came, *others), taken) for kept, taken in groups]
 
 
 def after_pieces(pieces, *others):
@@ -181,26 +180,32 @@
 
 def pack_small(parts, rows):
     def fill(blocks):
-        blocks = [jnp.pad(v, ((0, 0), (0, 128 - v.shape[1]))) for v in blocks]
-        used = sum(v.shape[0] for v in blocks)
-        return jnp.concatenate(blocks + [jnp.zeros((rows - used, 128), bf16)], axis=0)
-
-    flat = fill([v[None] for v in parts if v.ndim == 1])
+        size = max(v.shape[1] for v in blocks)
+        same = [v for v in blocks if v.shape[1] < size]
+        rest = [v for v in blocks if v.shape[1] == size]
+        if same:
+            joined = jnp.concatenate(same, axis=0)
+            rest = [jnp.pad(joined, ((0, 0), (0, size - joined.shape[1])))] + rest
+        block = jnp.concatenate(rest, axis=0)
+        return jnp.pad(block, ((0, rows - block.shape[0]), (0, 128 - size)))
+
+    flat = sorted((v for v in parts if v.ndim == 1), key=lambda v: v.shape[0])
+    flat = fill([v[None] for v in flat])
     return jnp.concatenate([flat] + [fill([v]) for v in parts if v.ndim == 2], axis=1)
 
 
 def unpack_small(whole, rows, parts):
     whole = whole.reshape(-1, rows, whole.shape[1]).astype(f32)
-    found, at, left = [], 0, 128
-    for v in parts:
+    found, left = [], 128
+    flat = sorted((i for i, v in enumerate(parts) if v.ndim == 1), key=lambda i: parts[i].shape[0])
+    for i, v in enumerate(parts):
         size = v.shape[-1]
         if v.ndim == 2:
             block = whole[:, : v.shape[0], left : left + size].swapaxes(0, 1)
             found.append(block.reshape(v.shape[0], -1))
             left += 128
         else:
-            found.append(whole[:, at, :size].reshape(-1))
-            at += 1
+            found.append(whole[:, flat.index(i), :size].reshape(-1))
     return found
 
 
@@ -1122,17 +1127,15 @@
     qkv_matrix, whole_small = assemble(
         first, me, [(0, rows, 0, third), (0, rows, third, first_unit.shape[1] - third)]
     )
-    gain_one, bias_one, qkv_rows, out_bias, gain_two, bias_two, up_bias, down_bias = unpack_small(
-        whole_small, rows, smalls
-    )
+    gain_one, bias_one, qkv_rows, *_ = unpack_small(whole_small, rows, smalls)
     stacked = [w_down[at : at + rows] for at in range(0, w_down.shape[0], rows)]
-    second_unit = after(jnp.concatenate(stacked, axis=1), qkv_matrix)
+    second_unit = after(jnp.concatenate(stacked, axis=1), first[0][0], first[2][0])
     seconds = gather_line(second_unit, line, sizes)
     normed_one, unit_one, inv_one = normalize(values_in, gain_one, bias_one)
     normed_one = normed_one.astype(bf16)
     qkv = project(normed_one, qkv_matrix, qkv_rows.reshape(1, 3 * width), cosine, sine, partner)
     pairs = width // (2 * HEAD)
-    seconds = [after_pieces(pieces, qkv) for pieces in seconds]
+    seconds = [after_pieces(pieces, qkv_matrix) for pieces in seconds]
     seconds = [
         [pieces, moved(pieces, order[0], sizes) + moved(pieces, order[1], sizes)]
         for pieces, order in zip(seconds, orders)
@@ -1151,6 +1154,8 @@
         arrays, rels = zip(*pieces)
         pieces = [(after(jnp.concatenate(arrays, axis=0), attended), sum(rels, []))]
         second += pieces + moved(pieces, core, sizes)
+    whole_small = after(whole_small, attended)
+    *_, out_bias, gain_two, bias_two, up_bias, down_bias = unpack_small(whole_small, rows, smalls)
     hidden = w_up.shape[1]
     middle = values_in + jnp.dot(attended, out_matrix, preferred_element_type=f32) + out_bias
     normed_two, unit_two, inv_two = normalize(middle, gain_two, bias_two)
@@ -1176,6 +1181,7 @@
     grad_b_out_local = jnp.sum(grad_branch.astype(f32), axis=0)
     grads = weight_grad(attended, grad_branch, where, third, third + width, me)
     grad_attended = dot_t(grad_branch, out_matrix).astype(bf16)
+    feed_own = after(feed_own, feed_taken, grads[0])
     feed_sums = reduce_start(feed_own, feed_taken, orders, sizes)
     grad_attended = after(grad_attended, grads[0], *[v for group in feed_sums for v in group[:1] + group[2:]])
     feed_sums = [group[:2] for group in feed_sums]
@@ -1188,7 +1194,7 @@
     )
     steps = len(orders[0])
     for step in range(1, steps):
-        feed_sums = [(kept, after(came, grad_mixed)) for kept, came in together(feed_sums)]
+        feed_sums = together(feed_sums, grad_mixed)
         feed_sums = reduce_next(feed_sums, orders, step, sizes)
         grad_mixed = after(grad_mixed, *[v for group in feed_sums for v in group[:1] + group[2:]])
         feed_sums = [group[:2] for group in feed_sums]
@@ -1230,10 +1236,10 @@
     parts = line_parts(sums)
     parts = parts[:1] + [v.astype(bf16) for v in parts[1:]]
     feed_parts[0] = after(feed_parts[0], *parts[1:])
-    result = after(result, *parts[1:])
+    output = unsort_rows(after(result, *parts[1:]))
+    parts[0] = after(parts[0], output)
     feed_sum = reduce_line(feed_parts, line, sizes)
     sum_one = reduce_line(parts, line, sizes)
-    output = unsort_rows(result)
     small = sum_one[:, third + width :]
     small = small[:, :128] + swap(small[:, 128:], 1 << core, sizes)
     small = small_parts(small, vectors, count)

time: 491 us -> 463 us (0.943)
  waiting for transfers between devices: 89.7 us -> 72.4 us
  other arithmetic: 62 us -> 73.7 us
  local copies, waits for them, and re-layouts: 41.8 us -> 31.6 us
  Pallas kernels: 207 us -> 198 us
    ppermute x41, waiting for transfers between devices: 87.3 us -> 62 us  [swap(): lax.ppermute(value, ('dp', 'fsdp'), [(i, i ^ mask) for i in range(count)])]
    all_gather x1, waiting for transfers between devices: 1.02 us -> 9 us  [body(): up_matrix = lax.all_gather(w_up, ('dp', 'fsdp'), axis=0, tiled=True)]
    convert_element_type x4, other arithmetic: 17.1 us -> 23.3 us  [reduce_step(): sent = (kept[half:].astype(f32) + taken[half:].astype(f32)).astype(kind)]
    unnamed x115 -> x81, local copies, waits for them, and re-layouts: 20.1 us -> 14.1 us
    pallas_call x2, Pallas kernels: 36.6 us -> 30.8 us  [attend_back(): pl.pallas_call(kernel, grid_spec=pltpu.PrefetchScalarGridSpec(num_scalar_...]
  transfers between devices with their start and end apart: 43 -> 43, of which waited for: 17 -> 17; matrix products, arithmetic and copies ran while one was open for 17% -> 20% of each run, Pallas kernels for 26% -> 26%
where the time goes in v4:
time: 463 us; the launch traced here: 456 us
  Pallas kernels  198 us (43%)
  other arithmetic  73.7 us (16%)
  waiting for transfers between devices  72.4 us (16%)
  starting transfers between devices  57.1 us (12%)
  local copies, waits for them, and re-layouts  31.6 us (7%)
  between operations  14.9 us (3%)
  matrix products  8.56 us (2%)
    pallas_call x1, Pallas kernels, feed(): pl.pallas_call(functools.partial(feed_kernel, rels, (line, orders, core))...  79.3 us
    ppermute x41, waiting for transfers between devices, swap(): lax.ppermute(value, ('dp', 'fsdp'), [(i, i ^ mask) for i in range(count)])  62 us
    ppermute x41, starting transfers between devices, swap(): lax.ppermute(value, ('dp', 'fsdp'), [(i, i ^ mask) for i in range(count)])  57 us
    pallas_call x2, Pallas kernels, attend_back(): pl.pallas_call(kernel, grid_spec=pltpu.PrefetchScalarGridSpec(num_scalar_...  30.8 us
    convert_element_type x4, other arithmetic, reduce_step(): sent = (kept[half:].astype(f32) + taken[half:].astype(f32)).astype(kind)  23.3 us
    pallas_call x2, Pallas kernels, weight_grad(): pl.pallas_call(functools.partial(weight_kernel, where, left, count), grid...  19.7 us
    pallas_call x1, Pallas kernels, last_step(): pl.pallas_call(last_kernel, grid=(parts,), in_specs=[pl.BlockSpec((1, row...  19.1 us
    pallas_call x2, Pallas kernels, attend(): pl.pallas_call(kernel, grid_spec=pltpu.PrefetchScalarGridSpec(num_scalar_...  18.7 us
  transfers between devices with their start and end apart: 43, of which 17 were waited for; matrix products, arithmetic and copies ran while one was open for 20% of the time, Pallas kernels for 26%

profile of v4, /device:TPU:1, one launch (start us, length us, event | category | flops | bytes accessed | tf_op | source)
XLA Modules:
  0.0 455.9 jit_solution(3576333313303970719)
XLA Ops:
  11.1 4.2 collective-permute-start.4
  22.7 5.5 %shard_map.380 = (bf16[1040,1024]{1,0:T(8,128)(2,1)}, bf16[1040,1024]{1,0:T(8,128)(2,1)}, f32[1,1024]{1,0:T(1,128)}) custom-call(bf16[1032,1024]{1,0:T(8,128)(2,1)} %x_ref.1, bf16[1032,1024]{1,0:T(8,128)(2,1)} %g_ref.1), custom_call_target="tpu_custom_call" | custom-call | flops 1000000000 | tf_op jit(solution)/shard_map/pallas_call | solution.py:944
  31.3 3.2 collective-permute-done.3
  42.4 4.2 collective-permute-done.5
  60.3 10.2 %collective-permute-start.9 = (bf16[4,32,3328]{2,1,0:T(8,128)(2,1)}, bf16[4,32,3328]{2,1,0:T(8,128)(2,1)S(1)}, u32[]{:S(2)}, u32[]{:S(2)}) collective-permute-start(bf16[4,32,3328]{2,1,0:T(8,128)(2,1)} %constant_dynamic-update-slice_fusion.refs_2_), channel_id=1, source_target_pairs={{0,8},{1,9},{2,10},{3,11},{4,12},{5,13},{6,14},{7,15},{8,0},{9,1},... | collective-permute-start | bytes 2555912 | tf_op jit(solution)/shard_map/ppermute | solution.py:41
  70.5 5.5 %collective-permute-done.11 = bf16[1,32,4096]{2,1,0:T(8,128)(2,1)S(1)} collective-permute-done((bf16[1,32,4096]{2,1,0:T(8,128)(2,1)}, bf16[1,32,4096]{2,1,0:T(8,128)(2,1)S(1)}, u32[]{:S(2)}, u32[]{:S(2)}) %collective-permute-start.11) | collective-permute-done | bytes 262176 | tf_op jit(solution)/shard_map/ppermute | solution.py:41
  81.9 5.8 %shard_map.381 = (bf16[1024,3072]{1,0:T(8,128)(2,1)}, bf16[1024,256]{1,0:T(8,128)(2,1)}) custom-call(s32[1]{0:T(128)} %bitcast.me_ref, bf16[4,32,3328]{2,1,0:T(8,128)(2,1)} %pad_maximum_fusion.2.refs_0_.refs_1_, bf16[4,32,3328]{2,1,0:T(8,128)(2,1)} %collective-permute-done.2.refs_1_, bf16[4,32,3328]{2,1,0:T(8,128)(2,1)} %constant_dynamic-update-slice_fusion.refs_2_, ...), custom_call_target="tpu_custom_call" | custom-call | flops 1500000000 | tf_op jit(solution)/shard_map/pallas_call | solution.py:170
  96.7 15.3 %shard_map.382.q_ref.k_ref.v_ref.refs_1_.refs_2_.refs_3_ = bf16[1040,3072]{1,0:T(8,128)(2,1)} custom-call(bf16[1040,1024]{1,0:T(8,128)(2,1)} %fusion.6.x_ref, bf16[1024,3072]{1,0:T(8,128)(2,1)} %get-tuple-element.40.w_ref.refs_1_, f32[1,3072]{1,0:T(1,128)} %reshape_reshape.3.b_ref, f32[1040,128]{1,0:T(8,128)} %get-tuple-element.120.cos_ref.refs_9_, ...), custom_call_target="tpu_custom_call" | custom-call | flops 4000000000 | tf_op jit(solution)/shard_map/pallas_call | solution.py:589
  112.0 9.3 %shard_map.383 = (bf16[1040,1024]{1,0:T(8,128)(2,1)}, f32[1,8,1024]{2,1,0:T(8,128)}, f32[1,1,64]{2,1,0:T(1,128)}) custom-call(s32[4]{0:T(128)} %copy-done.28, bf16[1040,3072]{1,0:T(8,128)(2,1)} %shard_map.382.q_ref.k_ref.v_ref.refs_1_.refs_2_.refs_3_, bf16[1040,3072]{1,0:T(8,128)(2,1)} %shard_map.382.q_ref.k_ref.v_ref.refs_1_.refs_2_.refs_3_, ...), custom_call_target="tpu_custom_call" | custom-call | flops 6400000000 | tf_op jit(solution)/shard_map/pallas_call | solution.py:370
  121.5 3.7 collective-permute-start.20
  126.0 9.4 %shard_map.384 = (bf16[1040,1024]{1,0:T(8,128)(2,1)}, f32[1,8,1024]{2,1,0:T(8,128)}, f32[1,1,64]{2,1,0:T(1,128)}) custom-call(s32[4]{0:T(128)} %copy-done.28, bf16[1040,3072]{1,0:T(8,128)(2,1)} %shard_map.382.q_ref.k_ref.v_ref.refs_1_.refs_2_.refs_3_, ...), custom_call_target="tpu_custom_call", output_to_operand_aliasing={{0}: (5, {})} | custom-call | flops 6400000000 | tf_op jit(solution)/shard_map/pallas_call | solution.py:370
  145.0 4.8 %collective-permute-start.15 = (bf16[8,32,4096]{2,1,0:T(8,128)(2,1)}, bf16[8,32,4096]{2,1,0:T(8,128)(2,1)}, u32[]{:S(2)}, u32[]{:S(2)}) collective-permute-start(bf16[8,32,4096]{2,1,0:T(8,128)(2,1)} %shard_map.390.refs_0_), channel_id=1, source_target_pairs={{0,8},{1,9},{2,10},{3,11},{4,12},{5,13},{6,14},{7,15},{8,0},{9,1},... | collective-permute-start | bytes 6291464 | tf_op jit(solution)/shard_map/ppermute | solution.py:41
  149.8 4.8 %fusion.38 = (f32[1040]{0:T(1024)S(1)}, f32[1040,1024]{1,0:T(8,128)S(1)}) fusion(f32[1024]{0:T(1024)S(1)} %add.197, bf16[1040,1024]{1,0:T(8,128)(2,1)S(1)} %copy-done, bf16[1024,1024]{1,0:T(8,128)(2,1)} %all-gather.3.cloned.1.call-done, bf16[1040,1024]{1,0:T(8,128)(2,1)} %get-tuple-element.38.x_ref), kind=kOutput, calls=%fused_computation.150 | convolution fusion | flops 2185296896 | bytes 10625088 | tf_op jit(solution)/shard_map/dot_general | solution.py:1160
  158.7 9.0 %all-gather.5.cloned.1.call-done.up_ref = bf16[1024,4096]{1,0:T(8,128)(2,1)} async-done(((bf16[32,4096]{1,0:T(8,128)(2,1)}), bf16[1024,4096]{1,0:T(8,128)(2,1)}) %all-gather.5.cloned.1.call-update) | async-done | bytes 8388624 | tf_op jit(solution)/shard_map/all_gather | solution.py:1115
  167.7 79.3 %shard_map.395 = (bf16[1040,1024]{1,0:T(8,128)(2,1)}, f32[1040,1024]{1,0:T(8,128)}, f32[1,4096]{1,0:T(1,128)}, bf16[16,32,8192]{2,1,0:T(8,128)(2,1)}, bf16[16,32,8192]{2,1,0:T(8,128)(2,1)}) custom-call(s32[1]{0:T(128)} %bitcast.me_ref, bf16[1040,1024]{1,0:T(8,128)(2,1)} %add_convert_fusion.x_ref, bf16[1040,1024]{1,0:T(8,128)(2,1)} %get-tuple-element.43.g_ref, ...), custom_call_target="tpu_custom_call" | custom-call | flops 20000000000 | tf_op jit(solution)/shard_map/pallas_call | solution.py:821
  247.2 5.3 %multiply_reduce_fusion = (bf16[1024]{0:T(1024)(128)(2,1)S(1)}, f32[1040]{0:T(1024)S(1)}, f32[1040]{0:T(1024)S(1)}, bf16[1024]{0:T(1024)(128)(2,1)S(1)}) fusion(f32[1040,1024]{1,0:T(8,128)} %get-tuple-element.45, f32[1040,1024]{1,0:T(8,128)} %copy-done.1, f32[1040]{0:T(1024)S(1)} %add_rsqrt_fusion, f32[1040]{0:T(1024)S(1)} %broadcast_multiply_fusion.2, ...), kind=kLoop, calls=%fused_computation.11 | loop fusion | flops 9580512 | bytes 8544512 | tf_op jit(solution)/shard_map/reduce_sum | solution.py:1177
  253.2 3.6 convert_reduce_fusion.1
  256.8 6.7 %shard_map.396 = (bf16[16,32,4096]{2,1,0:T(8,128)(2,1)}, bf16[16,32,4096]{2,1,0:T(8,128)(2,1)}) custom-call(s32[1]{0:T(128)} %bitcast.me_ref, bf16[1040,1024]{1,0:T(8,128)(2,1)} %get-tuple-element.42.refs_1_.x_ref.o_ref.refs_4_, bf16[1040,1024]{1,0:T(8,128)(2,1)} %get-tuple-element.72.g_ref), custom_call_target="tpu_custom_call" | custom-call | flops 1000000000 | tf_op jit(solution)/shard_map/pallas_call | solution.py:909
  263.5 10.4 %add_convert_fusion.1 = (bf16[4,32,8192]{2,1,0:T(8,128)(2,1)}, bf16[4,32,8192]{2,1,0:T(8,128)(2,1)}, bf16[4,32,8192]{2,1,0:T(8,128)(2,1)}, bf16[4,32,8192]{2,1,0:T(8,128)(2,1)}) fusion(bf16[16,32,8192]{2,1,0:T(8,128)(2,1)} %collective-permute-done.22.refs_1_, bf16[16,32,8192]{2,1,0:T(8,128)(2,1)} %shard_map.397), kind=kLoop, calls=%fused_computation.17 | loop fusion | flops 16777216 | bytes 25165824 | tf_op jit(solution)/shard_map/convert_element_type | solution.py:98
  276.1 3.7 convolution_convert_fusion.refs_0_
  279.9 15.2 %shard_map.399.refs_12_ = bf16[3,1040,1024]{2,1,0:T(8,128)(2,1)} custom-call(s32[4]{0:T(128)} %copy-done.28, bf16[1040,3072]{1,0:T(8,128)(2,1)} %shard_map.382.q_ref.k_ref.v_ref.refs_1_.refs_2_.refs_3_, bf16[1040,3072]{1,0:T(8,128)(2,1)} %shard_map.382.q_ref.k_ref.v_ref.refs_1_.refs_2_.refs_3_, ...), custom_call_target="tpu_custom_call" | custom-call | flops 7600000000 | tf_op jit(solution)/shard_map/pallas_call | solution.py:518
  295.0 15.6 %shard_map.400.refs_3_.refs_0_ = bf16[3,1040,1024]{2,1,0:T(8,128)(2,1)} custom-call(s32[4]{0:T(128)} %copy-done.28, bf16[1040,3072]{1,0:T(8,128)(2,1)} %shard_map.382.q_ref.k_ref.v_ref.refs_1_.refs_2_.refs_3_, bf16[1040,3072]{1,0:T(8,128)(2,1)} %shard_map.382.q_ref.k_ref.v_ref.refs_1_.refs_2_.refs_3_, ...), custom_call_target="tpu_custom_call", output_to_operand_aliasing={{}: (12, {})} | custom-call | flops 7600000000 | tf_op jit(solution)/shard_map/pallas_call | solution.py:518
  310.7 10.6 %collective-permute-done.24.refs_2_ = bf16[4,32,8192]{2,1,0:T(8,128)(2,1)S(1)} collective-permute-done((bf16[4,32,8192]{2,1,0:T(8,128)(2,1)}, bf16[4,32,8192]{2,1,0:T(8,128)(2,1)S(1)}, u32[]{:S(2)}, u32[]{:S(2)}) %collective-permute-start.24) | collective-permute-done | bytes 2097184 | tf_op jit(solution)/shard_map/ppermute | solution.py:41
  322.6 3.7 add_convert_fusion.9
  327.3 4.0 add_convert_fusion.11
  332.8 13.1 %shard_map.404 = (bf16[16,32,4096]{2,1,0:T(8,128)(2,1)}, bf16[16,32,4096]{2,1,0:T(8,128)(2,1)}) custom-call(s32[1]{0:T(128)} %bitcast.me_ref, bf16[1040,1024]{1,0:T(8,128)(2,1)} %fusion.6.x_ref, bf16[3,1040,1024]{2,1,0:T(8,128)(2,1)} %shard_map.403.g_ref.refs_0_, ...), custom_call_target="tpu_custom_call", output_to_operand_aliasing={{0}: (3, {}), {1}: (4, {})} | custom-call | flops 3000000000 | tf_op jit(solution)/shard_map/pallas_call | solution.py:909
  349.7 5.2 %collective-permute-done.25.refs_1_ = bf16[2,32,8192]{2,1,0:T(8,128)(2,1)S(1)} collective-permute-done((bf16[2,32,8192]{2,1,0:T(8,128)(2,1)}, bf16[2,32,8192]{2,1,0:T(8,128)(2,1)S(1)}, u32[]{:S(2)}, u32[]{:S(2)}) %collective-permute-start.25) | collective-permute-done | bytes 1048608 | tf_op jit(solution)/shard_map/ppermute | solution.py:41
  364.7 5.2 %add_convert_fusion.5 = (bf16[4,32,4096]{2,1,0:T(8,128)(2,1)S(1)}, bf16[4,32,4096]{2,1,0:T(8,128)(2,1)}, bf16[4,32,4096]{2,1,0:T(8,128)(2,1)S(1)}, bf16[4,32,4096]{2,1,0:T(8,128)(2,1)}) fusion(bf16[16,32,4096]{2,1,0:T(8,128)(2,1)} %collective-permute-done.27, bf16[16,32,4096]{2,1,0:T(8,128)(2,1)} %shard_map.407), kind=kLoop, calls=%fused_computation.26 | loop fusion | flops 8388608 | bytes 12582912 | tf_op jit(solution)/shard_map/convert_element_type | solution.py:98
  373.3 19.1 %shard_map.409 = (f32[1032,1024]{1,0:T(8,128)}, f32[1,1024]{1,0:T(1,128)}, f32[1,1024]{1,0:T(1,128)}, f32[3,1,1024]{2,1,0:T(1,128)}) custom-call(bf16[3,1040,1024]{2,1,0:T(8,128)(2,1)} %shard_map.408.g_ref, bf16[1024,3072]{1,0:T(8,128)(2,1)} %get-tuple-element.40.w_ref.refs_1_, bf16[1040,1024]{1,0:T(8,128)(2,1)} %get-tuple-element.38.x_ref, ...), custom_call_target="tpu_custom_call" | custom-call | flops 5000000000 | tf_op jit(solution)/shard_map/pallas_call | solution.py:1027
  406.4 8.4 %collective-permute-done.33 = bf16[2,32,4352]{2,1,0:T(8,128)(2,1)S(1)} collective-permute-done((bf16[2,32,4352]{2,1,0:T(8,128)(2,1)S(1)}, bf16[2,32,4352]{2,1,0:T(8,128)(2,1)S(1)}, u32[]{:S(2)}, u32[]{:S(2)}) %collective-permute-start.33) | collective-permute-done | bytes 557088 | tf_op jit(solution)/shard_map/ppermute | solution.py:41
  422.4 3.6 shard_map.411.refs_1_
  426.0 13.8 %collective-permute-done.35 = bf16[32,4352]{1,0:T(8,128)(2,1)S(1)} collective-permute-done((bf16[32,4352]{1,0:T(8,128)(2,1)S(1)}, bf16[32,4352]{1,0:T(8,128)(2,1)S(1)}, u32[]{:S(2)}, u32[]{:S(2)}) %collective-permute-start.35) | collective-permute-done | bytes 278560 | tf_op jit(solution)/shard_map/ppermute | solution.py:41
  (279 shorter events, 119.7 us)
Async XLA Ops:
  7.2 142.6 %all-gather.3.cloned.1.call-start = ((), (), s32[]{:S(2)}) async-start(), calls=%async_computation | async-start | bytes 2162688 | tf_op jit(solution)/shard_map/all_gather | solution.py:1114
  8.0 159.7 %all-gather.5.cloned.1.call-start = ((), (), s32[]{:S(2)}) async-start(), calls=%async_computation.1 | async-start | bytes 8650752 | tf_op jit(solution)/shard_map/all_gather | solution.py:1115
  11.1 20.2 %collective-permute-start.4 = (bf16[1,32,3328]{2,1,0:T(8,128)(2,1)S(1)}, bf16[1,32,3328]{2,1,0:T(8,128)(2,1)}, u32[]{:S(2)}, u32[]{:S(2)}) collective-permute-start(bf16[1,32,3328]{2,1,0:T(8,128)(2,1)S(1)} %fusion.20), channel_id=1, source_target_pairs={{0,6},{1,7},{2,4},{3,5},{4,2},{5,3},{6,0},{7,1},{8,14},{9,15},{10,... | collective-permute-start | bytes 638984 | tf_op jit(solution)/shard_map/ppermute | solution.py:41
  15.3 19.2 %collective-permute-start.3 = (bf16[1,32,3328]{2,1,0:T(8,128)(2,1)S(1)}, bf16[1,32,3328]{2,1,0:T(8,128)(2,1)}, u32[]{:S(2)}, u32[]{:S(2)}) collective-permute-start(bf16[1,32,3328]{2,1,0:T(8,128)(2,1)S(1)} %fusion.20), channel_id=1, source_target_pairs={{0,4},{1,5},{2,6},{3,7},{4,0},{5,1},{6,2},{7,3},{8,12},{9,13},{10,... | collective-permute-start | bytes 638984 | tf_op jit(solution)/shard_map/ppermute | solution.py:41
  15.3 21.5 %collective-permute-start = (bf16[1,32,3328]{2,1,0:T(8,128)(2,1)S(1)}, bf16[1,32,3328]{2,1,0:T(8,128)(2,1)}, u32[]{:S(2)}, u32[]{:S(2)}) collective-permute-start(bf16[1,32,3328]{2,1,0:T(8,128)(2,1)S(1)} %fusion.20), channel_id=1, source_target_pairs={{0,2},{1,3},{2,0},{3,1},{4,6},{5,7},{6,4},{7,5},{8,10},{9,11},{10,... | collective-permute-start | bytes 638984 | tf_op jit(solution)/shard_map/ppermute | solution.py:41
  37.8 12.4 %collective-permute-start.1 = (bf16[2,32,3328]{2,1,0:T(8,128)(2,1)S(1)}, bf16[2,32,3328]{2,1,0:T(8,128)(2,1)S(1)}, u32[]{:S(2)}, u32[]{:S(2)}) collective-permute-start(bf16[2,32,3328]{2,1,0:T(8,128)(2,1)S(1)} %pad_maximum_fusion.9), channel_id=1, source_target_pairs={{0,1},{1,0},{2,3},{3,2},{4,5},{5,4},{6,7},{7,6},{8,9},{9,8},{10,11... | collective-permute-start | bytes 1277960 | tf_op jit(solution)/shard_map/ppermute | solution.py:41
  47.4 29.8 %collective-permute-start.6 = (bf16[4,32,3328]{2,1,0:T(8,128)(2,1)}, bf16[4,32,3328]{2,1,0:T(8,128)(2,1)}, u32[]{:S(2)}, u32[]{:S(2)}) collective-permute-start(bf16[4,32,3328]{2,1,0:T(8,128)(2,1)} %constant_dynamic-update-slice_fusion.refs_2_), channel_id=1, source_target_pairs={{0,1},{1,0},{2,3},{3,2},{4,5},{5,4},{6,7},{7,6},{8,9},{9,8},{10,11... | collective-permute-start | bytes 2555912 | tf_op jit(solution)/shard_map/ppermute | solution.py:41
  52.2 25.0 %collective-permute-start.2 = (bf16[4,32,3328]{2,1,0:T(8,128)(2,1)}, bf16[4,32,3328]{2,1,0:T(8,128)(2,1)}, u32[]{:S(2)}, u32[]{:S(2)}) collective-permute-start(bf16[4,32,3328]{2,1,0:T(8,128)(2,1)} %pad_maximum_fusion.2.refs_0_.refs_1_), channel_id=1, source_target_pairs={{0,16},{1,17},{2,18},{3,19},{4,20},{5,21},{6,22},{7,23},{8,24},{9,... | collective-permute-start | bytes 2555912 | tf_op jit(solution)/shard_map/ppermute | solution.py:41
  54.4 21.7 %collective-permute-start.11 = (bf16[1,32,4096]{2,1,0:T(8,128)(2,1)}, bf16[1,32,4096]{2,1,0:T(8,128)(2,1)S(1)}, u32[]{:S(2)}, u32[]{:S(2)}) collective-permute-start(bf16[1,32,4096]{2,1,0:T(8,128)(2,1)} %bitcast.89), channel_id=1, source_target_pairs={{0,2},{1,3},{2,0},{3,1},{4,6},{5,7},{6,4},{7,5},{8,10},{9,11},{10,... | collective-permute-start | bytes 786440 | tf_op jit(solution)/shard_map/ppermute | solution.py:41
  55.4 23.1 %collective-permute-start.16 = (bf16[1,32,4096]{2,1,0:T(8,128)(2,1)S(1)}, bf16[1,32,4096]{2,1,0:T(8,128)(2,1)S(1)}, u32[]{:S(2)}, u32[]{:S(2)}) collective-permute-start(bf16[1,32,4096]{2,1,0:T(8,128)(2,1)S(1)} %bitcast.90), channel_id=1, source_target_pairs={{0,4},{1,5},{2,6},{3,7},{4,0},{5,1},{6,2},{7,3},{8,12},{9,13},{10,... | collective-permute-start | bytes 786440 | tf_op jit(solution)/shard_map/ppermute | solution.py:41
  60.3 19.1 %collective-permute-start.9 = (bf16[4,32,3328]{2,1,0:T(8,128)(2,1)}, bf16[4,32,3328]{2,1,0:T(8,128)(2,1)S(1)}, u32[]{:S(2)}, u32[]{:S(2)}) collective-permute-start(bf16[4,32,3328]{2,1,0:T(8,128)(2,1)} %constant_dynamic-update-slice_fusion.refs_2_), channel_id=1, source_target_pairs={{0,8},{1,9},{2,10},{3,11},{4,12},{5,13},{6,14},{7,15},{8,0},{9,1},... | collective-permute-start | bytes 2555912 | tf_op jit(solution)/shard_map/ppermute | solution.py:41
  87.7 37.5 %collective-permute-start.13 = (bf16[2,32,4096]{2,1,0:T(8,128)(2,1)}, bf16[2,32,4096]{2,1,0:T(8,128)(2,1)S(1)}, u32[]{:S(2)}, u32[]{:S(2)}) collective-permute-start(bf16[2,32,4096]{2,1,0:T(8,128)(2,1)} %shard_map.387), channel_id=1, source_target_pairs={{0,16},{1,17},{2,18},{3,19},{4,20},{5,21},{6,22},{7,23},{8,24},{9,... | collective-permute-start | bytes 1572872 | tf_op jit(solution)/shard_map/ppermute | solution.py:41
  88.7 32.6 %collective-permute-start.12 = (bf16[2,32,4096]{2,1,0:T(8,128)(2,1)}, bf16[2,32,4096]{2,1,0:T(8,128)(2,1)}, u32[]{:S(2)}, u32[]{:S(2)}) collective-permute-start(bf16[2,32,4096]{2,1,0:T(8,128)(2,1)} %shard_map.387), channel_id=1, source_target_pairs={{0,1},{1,0},{2,3},{3,2},{4,5},{5,4},{6,7},{7,6},{8,9},{9,8},{10,11... | collective-permute-start | bytes 1572872 | tf_op jit(solution)/shard_map/ppermute | solution.py:41
  91.4 33.8 %collective-permute-start.19 = (bf16[2,32,4096]{2,1,0:T(8,128)(2,1)}, bf16[2,32,4096]{2,1,0:T(8,128)(2,1)}, u32[]{:S(2)}, u32[]{:S(2)}) collective-permute-start(bf16[2,32,4096]{2,1,0:T(8,128)(2,1)} %shard_map.391), channel_id=1, source_target_pairs={{0,1},{1,0},{2,3},{3,2},{4,5},{5,4},{6,7},{7,6},{8,9},{9,8},{10,11... | collective-permute-start | bytes 1572872 | tf_op jit(solution)/shard_map/ppermute | solution.py:41
  91.4 30.1 %collective-permute-start.18 = (bf16[2,32,4096]{2,1,0:T(8,128)(2,1)}, bf16[2,32,4096]{2,1,0:T(8,128)(2,1)}, u32[]{:S(2)}, u32[]{:S(2)}) collective-permute-start(bf16[2,32,4096]{2,1,0:T(8,128)(2,1)} %shard_map.391), channel_id=1, source_target_pairs={{0,16},{1,17},{2,18},{3,19},{4,20},{5,21},{6,22},{7,23},{8,24},{9,... | collective-permute-start | bytes 1572872 | tf_op jit(solution)/shard_map/ppermute | solution.py:41
  121.3 19.9 %collective-permute-start.14 = (bf16[2,32,4096]{2,1,0:T(8,128)(2,1)}, bf16[2,32,4096]{2,1,0:T(8,128)(2,1)S(1)}, u32[]{:S(2)}, u32[]{:S(2)}) collective-permute-start(bf16[2,32,4096]{2,1,0:T(8,128)(2,1)} %shard_map.388), channel_id=1, source_target_pairs={{0,16},{1,17},{2,18},{3,19},{4,20},{5,21},{6,22},{7,23},{8,24},{9,... | collective-permute-start | bytes 1572872 | tf_op jit(solution)/shard_map/ppermute | solution.py:41
  121.5 16.8 %collective-permute-start.20 = (bf16[2,32,4096]{2,1,0:T(8,128)(2,1)}, bf16[2,32,4096]{2,1,0:T(8,128)(2,1)S(1)}, u32[]{:S(2)}, u32[]{:S(2)}) collective-permute-start(bf16[2,32,4096]{2,1,0:T(8,128)(2,1)} %shard_map.392), channel_id=1, source_target_pairs={{0,1},{1,0},{2,3},{3,2},{4,5},{5,4},{6,7},{7,6},{8,9},{9,8},{10,11... | collective-permute-start | bytes 1572872 | tf_op jit(solution)/shard_map/ppermute | solution.py:41
  145.0 13.7 %collective-permute-start.15 = (bf16[8,32,4096]{2,1,0:T(8,128)(2,1)}, bf16[8,32,4096]{2,1,0:T(8,128)(2,1)}, u32[]{:S(2)}, u32[]{:S(2)}) collective-permute-start(bf16[8,32,4096]{2,1,0:T(8,128)(2,1)} %shard_map.390.refs_0_), channel_id=1, source_target_pairs={{0,8},{1,9},{2,10},{3,11},{4,12},{5,13},{6,14},{7,15},{8,0},{9,1},... | collective-permute-start | bytes 6291464 | tf_op jit(solution)/shard_map/ppermute | solution.py:41
  246.9 16.6 %collective-permute-start.22 = (bf16[16,32,8192]{2,1,0:T(8,128)(2,1)}, bf16[16,32,8192]{2,1,0:T(8,128)(2,1)}, u32[]{:S(2)}, u32[]{:S(2)}) collective-permute-start(bf16[16,32,8192]{2,1,0:T(8,128)(2,1)} %get-tuple-element.48), channel_id=1, source_target_pairs={{0,8},{1,9},{2,10},{3,11},{4,12},{5,13},{6,14},{7,15},{8,0},{9,1},... | collective-permute-start | bytes 25165832 | tf_op jit(solution)/shard_map/ppermute | solution.py:41
  273.9 47.3 %collective-permute-start.24 = (bf16[4,32,8192]{2,1,0:T(8,128)(2,1)}, bf16[4,32,8192]{2,1,0:T(8,128)(2,1)S(1)}, u32[]{:S(2)}, u32[]{:S(2)}) collective-permute-start(bf16[4,32,8192]{2,1,0:T(8,128)(2,1)} %get-tuple-element.74.refs_5_), channel_id=1, source_target_pairs={{0,1},{1,0},{2,3},{3,2},{4,5},{5,4},{6,7},{7,6},{8,9},{9,8},{10,11... | collective-permute-start | bytes 6291464 | tf_op jit(solution)/shard_map/ppermute | solution.py:41
  275.5 46.9 %collective-permute-start.23 = (bf16[4,32,8192]{2,1,0:T(8,128)(2,1)}, bf16[4,32,8192]{2,1,0:T(8,128)(2,1)}, u32[]{:S(2)}, u32[]{:S(2)}) collective-permute-start(bf16[4,32,8192]{2,1,0:T(8,128)(2,1)} %get-tuple-element.76.refs_3_), channel_id=1, source_target_pairs={{0,16},{1,17},{2,18},{3,19},{4,20},{5,21},{6,22},{7,23},{8,24},{9,... | collective-permute-start | bytes 6291464 | tf_op jit(solution)/shard_map/ppermute | solution.py:41
  326.3 23.4 %collective-permute-start.26 = (bf16[2,32,8192]{2,1,0:T(8,128)(2,1)S(1)}, bf16[2,32,8192]{2,1,0:T(8,128)(2,1)S(1)}, u32[]{:S(2)}, u32[]{:S(2)}) collective-permute-start(bf16[2,32,8192]{2,1,0:T(8,128)(2,1)S(1)} %get-tuple-element.82.refs_4_), channel_id=1, source_target_pairs={{0,16},{1,17},{2,18},{3,19},{4,20},{5,21},{6,22},{7,23},{8,24},{9,... | collective-permute-start | bytes 3145736 | tf_op jit(solution)/shard_map/ppermute | solution.py:41
  331.3 23.6 %collective-permute-start.25 = (bf16[2,32,8192]{2,1,0:T(8,128)(2,1)}, bf16[2,32,8192]{2,1,0:T(8,128)(2,1)S(1)}, u32[]{:S(2)}, u32[]{:S(2)}) collective-permute-start(bf16[2,32,8192]{2,1,0:T(8,128)(2,1)} %get-tuple-element.84.refs_2_), channel_id=1, source_target_pairs={{0,1},{1,0},{2,3},{3,2},{4,5},{5,4},{6,7},{7,6},{8,9},{9,8},{10,11... | collective-permute-start | bytes 3145736 | tf_op jit(solution)/shard_map/ppermute | solution.py:41
  345.8 18.9 %collective-permute-start.27 = (bf16[16,32,4096]{2,1,0:T(8,128)(2,1)}, bf16[16,32,4096]{2,1,0:T(8,128)(2,1)}, u32[]{:S(2)}, u32[]{:S(2)}) collective-permute-start(bf16[16,32,4096]{2,1,0:T(8,128)(2,1)} %get-tuple-element.55), channel_id=1, source_target_pairs={{0,8},{1,9},{2,10},{3,11},{4,12},{5,13},{6,14},{7,15},{8,0},{9,1},... | collective-permute-start | bytes 12582920 | tf_op jit(solution)/shard_map/ppermute | solution.py:41
  358.6 59.6 %collective-permute-start.40 = (bf16[32,8192]{1,0:T(8,128)(2,1)}, bf16[32,8192]{1,0:T(8,128)(2,1)}, u32[]{:S(2)}, u32[]{:S(2)}) collective-permute-start(bf16[32,8192]{1,0:T(8,128)(2,1)} %get-tuple-element.92.refs_3_), channel_id=1, source_target_pairs={{0,6},{1,7},{2,4},{3,5},{4,2},{5,3},{6,0},{7,1},{8,14},{9,15},{10,... | collective-permute-start | bytes 1572872 | tf_op jit(solution)/shard_map/ppermute | solution.py:41
  359.5 61.0 %collective-permute-start.39 = (bf16[32,8192]{1,0:T(8,128)(2,1)}, bf16[32,8192]{1,0:T(8,128)(2,1)}, u32[]{:S(2)}, u32[]{:S(2)}) collective-permute-start(bf16[32,8192]{1,0:T(8,128)(2,1)} %get-tuple-element.93.refs_2_), channel_id=1, source_target_pairs={{0,4},{1,5},{2,6},{3,7},{4,0},{5,1},{6,2},{7,3},{8,12},{9,13},{10,... | collective-permute-start | bytes 1572872 | tf_op jit(solution)/shard_map/ppermute | solution.py:41
  364.3 56.2 %collective-permute-start.38 = (bf16[32,8192]{1,0:T(8,128)(2,1)}, bf16[32,8192]{1,0:T(8,128)(2,1)}, u32[]{:S(2)}, u32[]{:S(2)}) collective-permute-start(bf16[32,8192]{1,0:T(8,128)(2,1)} %get-tuple-element.91.refs_1_), channel_id=1, source_target_pairs={{0,2},{1,3},{2,0},{3,1},{4,6},{5,7},{6,4},{7,5},{8,10},{9,11},{10,... | collective-permute-start | bytes 1572872 | tf_op jit(solution)/shard_map/ppermute | solution.py:41
  369.9 28.9 %collective-permute-start.31 = (bf16[4,32,4096]{2,1,0:T(8,128)(2,1)S(1)}, bf16[4,32,4096]{2,1,0:T(8,128)(2,1)}, u32[]{:S(2)}, u32[]{:S(2)}) collective-permute-start(bf16[4,32,4096]{2,1,0:T(8,128)(2,1)S(1)} %get-tuple-element.78.refs_4_), channel_id=1, source_target_pairs={{0,1},{1,0},{2,3},{3,2},{4,5},{5,4},{6,7},{7,6},{8,9},{9,8},{10,11... | collective-permute-start | bytes 3145736 | tf_op jit(solution)/shard_map/ppermute | solution.py:41
  372.0 31.0 %collective-permute-start.28 = (bf16[4,32,4096]{2,1,0:T(8,128)(2,1)S(1)}, bf16[4,32,4096]{2,1,0:T(8,128)(2,1)}, u32[]{:S(2)}, u32[]{:S(2)}) collective-permute-start(bf16[4,32,4096]{2,1,0:T(8,128)(2,1)S(1)} %get-tuple-element.80.refs_2_), channel_id=1, source_target_pairs={{0,16},{1,17},{2,18},{3,19},{4,20},{5,21},{6,22},{7,23},{8,24},{9,... | collective-permute-start | bytes 3145736 | tf_op jit(solution)/shard_map/ppermute | solution.py:41
  403.0 11.8 %collective-permute-start.33 = (bf16[2,32,4352]{2,1,0:T(8,128)(2,1)S(1)}, bf16[2,32,4352]{2,1,0:T(8,128)(2,1)S(1)}, u32[]{:S(2)}, u32[]{:S(2)}) collective-permute-start(bf16[2,32,4352]{2,1,0:T(8,128)(2,1)S(1)} %get-tuple-element.87), channel_id=1, source_target_pairs={{0,16},{1,17},{2,18},{3,19},{4,20},{5,21},{6,22},{7,23},{8,24},{9,... | collective-permute-start | bytes 1671176 | tf_op jit(solution)/shard_map/ppermute | solution.py:41
  417.2 22.7 %collective-permute-start.35 = (bf16[32,4352]{1,0:T(8,128)(2,1)S(1)}, bf16[32,4352]{1,0:T(8,128)(2,1)S(1)}, u32[]{:S(2)}, u32[]{:S(2)}) collective-permute-start(bf16[32,4352]{1,0:T(8,128)(2,1)S(1)} %get-tuple-element.97.refs_2_), channel_id=1, source_target_pairs={{0,4},{1,5},{2,6},{3,7},{4,0},{5,1},{6,2},{7,3},{8,12},{9,13},{10,... | collective-permute-start | bytes 835592 | tf_op jit(solution)/shard_map/ppermute | solution.py:41
  419.1 20.7 %collective-permute-start.34 = (bf16[32,4352]{1,0:T(8,128)(2,1)S(1)}, bf16[32,4352]{1,0:T(8,128)(2,1)S(1)}, u32[]{:S(2)}, u32[]{:S(2)}) collective-permute-start(bf16[32,4352]{1,0:T(8,128)(2,1)S(1)} %copy-done.19), channel_id=1, source_target_pairs={{0,2},{1,3},{2,0},{3,1},{4,6},{5,7},{6,4},{7,5},{8,10},{9,11},{10,... | collective-permute-start | bytes 835592 | tf_op jit(solution)/shard_map/ppermute | solution.py:41
  (48 other events, 376.8 us)
Sparse Core Ops, SparseCore 0:
  11.0 66.1 all-gather.2
  80.2 87.3 all-gather.4

commit v5 on v4

--- a/solution.py
+++ b/solution.py
@@ -1179,11 +1179,10 @@
     grad_middle = cot.astype(f32) + norm_back(grad_normed_two, unit_two, inv_two, gain_two)
     grad_branch = grad_middle.astype(bf16)
     grad_b_out_local = jnp.sum(grad_branch.astype(f32), axis=0)
-    grads = weight_grad(attended, grad_branch, where, third, third + width, me)
     grad_attended = dot_t(grad_branch, out_matrix).astype(bf16)
-    feed_own = after(feed_own, feed_taken, grads[0])
+    feed_own = after(feed_own, feed_taken, grad_attended)
     feed_sums = reduce_start(feed_own, feed_taken, orders, sizes)
-    grad_attended = after(grad_attended, grads[0], *[v for group in feed_sums for v in group[:1] + group[2:]])
+    grad_attended = after(grad_attended, *[v for group in feed_sums for v in group[:1] + group[2:]])
     feed_sums = [group[:2] for group in feed_sums]
     back = (hide, cosine, sine, partner)
     grad_mixed = attend_back(
@@ -1198,7 +1197,8 @@
         feed_sums = reduce_next(feed_sums, orders, step, sizes)
         grad_mixed = after(grad_mixed, *[v for group in feed_sums for v in group[:1] + group[2:]])
         feed_sums = [group[:2] for group in feed_sums]
-    own, other = weight_grad(normed_one, grad_mixed, where, 0, third + width, me, grads)
+    grads = weight_grad(normed_one, grad_mixed, where, 0, third + width, me)
+    own, other = weight_grad(attended, grad_branch, where, third, third + width, me, grads)
     taken = swap(other, 1 << core, sizes)
     feed_parts = line_parts(together(feed_sums))
     feed_parts = feed_parts[:1] + [v.astype(bf16) for v in feed_parts[1:]]

time: 463 us -> 459 us (level)
  waiting for transfers between devices: 72.4 us -> 57.3 us
  Pallas kernels: 198 us -> 211 us
    ppermute x41, waiting for transfers between devices: 62 us -> 49.3 us  [swap(): lax.ppermute(value, ('dp', 'fsdp'), [(i, i ^ mask) for i in range(count)])]
    pallas_call x2, Pallas kernels: 30.8 us -> 39.2 us  [attend_back(): pl.pallas_call(kernel, grid_spec=pltpu.PrefetchScalarGridSpec(num_scalar_...]
    pallas_call x2, Pallas kernels: 18.7 us -> 23.5 us  [attend(): pl.pallas_call(kernel, grid_spec=pltpu.PrefetchScalarGridSpec(num_scalar_...]
  transfers between devices with their start and end apart: 43 -> 43, of which waited for: 17 -> 16; matrix products, arithmetic and copies ran while one was open for 20% -> 20% of each run, Pallas kernels for 26% -> 29%
where the time goes in v5:
time: 459 us; the launch traced here: 451 us
  Pallas kernels  211 us (46%)
  other arithmetic  73.1 us (16%)
  waiting for transfers between devices  57.3 us (12%)
  starting transfers between devices  53.1 us (12%)
  local copies, waits for them, and re-layouts  33.8 us (7%)
  between operations  14.9 us (3%)
  matrix products  8.54 us (2%)
    pallas_call x1, Pallas kernels, feed(): pl.pallas_call(functools.partial(feed_kernel, rels, (line, orders, core))...  79.3 us
    ppermute x41, starting transfers between devices, swap(): lax.ppermute(value, ('dp', 'fsdp'), [(i, i ^ mask) for i in range(count)])  53 us
    ppermute x41, waiting for transfers between devices, swap(): lax.ppermute(value, ('dp', 'fsdp'), [(i, i ^ mask) for i in range(count)])  49.3 us
    pallas_call x2, Pallas kernels, attend_back(): pl.pallas_call(kernel, grid_spec=pltpu.PrefetchScalarGridSpec(num_scalar_...  39.2 us
    pallas_call x2, Pallas kernels, attend(): pl.pallas_call(kernel, grid_spec=pltpu.PrefetchScalarGridSpec(num_scalar_...  23.5 us
    convert_element_type x4, other arithmetic, reduce_step(): sent = (kept[half:].astype(f32) + taken[half:].astype(f32)).astype(kind)  23.1 us
    pallas_call x2, Pallas kernels, weight_grad(): pl.pallas_call(functools.partial(weight_kernel, where, left, count), grid...  19.8 us
    pallas_call x1, Pallas kernels, last_step(): pl.pallas_call(last_kernel, grid=(parts,), in_specs=[pl.BlockSpec((1, row...  18.9 us
  transfers between devices with their start and end apart: 43, of which 16 were waited for; matrix products, arithmetic and copies ran while one was open for 20% of the time, Pallas kernels for 29%

profile of v5, /device:TPU:1, one launch (start us, length us, event | category | flops | bytes accessed | tf_op | source)
XLA Modules:
  0.0 451.4 jit_solution(10224752766171178255)
XLA Ops:
  11.1 4.2 collective-permute-start.4
  22.7 5.5 %shard_map.380 = (bf16[1040,1024]{1,0:T(8,128)(2,1)}, bf16[1040,1024]{1,0:T(8,128)(2,1)}, f32[1,1024]{1,0:T(1,128)}) custom-call(bf16[1032,1024]{1,0:T(8,128)(2,1)} %x_ref.1, bf16[1032,1024]{1,0:T(8,128)(2,1)} %g_ref.1), custom_call_target="tpu_custom_call" | custom-call | flops 1000000000 | tf_op jit(solution)/shard_map/pallas_call | solution.py:944
  31.3 3.2 collective-permute-done.3
  42.4 4.2 collective-permute-done.5
  57.5 2.8 collective-permute-done.17
  60.3 10.2 %collective-permute-start.9 = (bf16[4,32,3328]{2,1,0:T(8,128)(2,1)}, bf16[4,32,3328]{2,1,0:T(8,128)(2,1)S(1)}, u32[]{:S(2)}, u32[]{:S(2)}) collective-permute-start(bf16[4,32,3328]{2,1,0:T(8,128)(2,1)} %constant_dynamic-update-slice_fusion.refs_2_), channel_id=1, source_target_pairs={{0,8},{1,9},{2,10},{3,11},{4,12},{5,13},{6,14},{7,15},{8,0},{9,1},... | collective-permute-start | bytes 2555912 | tf_op jit(solution)/shard_map/ppermute | solution.py:41
  70.5 5.5 %collective-permute-done.11 = bf16[1,32,4096]{2,1,0:T(8,128)(2,1)S(1)} collective-permute-done((bf16[1,32,4096]{2,1,0:T(8,128)(2,1)}, bf16[1,32,4096]{2,1,0:T(8,128)(2,1)S(1)}, u32[]{:S(2)}, u32[]{:S(2)}) %collective-permute-start.11) | collective-permute-done | bytes 262176 | tf_op jit(solution)/shard_map/ppermute | solution.py:41
  81.9 5.8 %shard_map.381 = (bf16[1024,3072]{1,0:T(8,128)(2,1)}, bf16[1024,256]{1,0:T(8,128)(2,1)}) custom-call(s32[1]{0:T(128)} %bitcast.me_ref, bf16[4,32,3328]{2,1,0:T(8,128)(2,1)} %pad_maximum_fusion.2.refs_0_.refs_1_, bf16[4,32,3328]{2,1,0:T(8,128)(2,1)} %collective-permute-done.2.refs_1_, bf16[4,32,3328]{2,1,0:T(8,128)(2,1)} %constant_dynamic-update-slice_fusion.refs_2_, ...), custom_call_target="tpu_custom_call" | custom-call | flops 1500000000 | tf_op jit(solution)/shard_map/pallas_call | solution.py:170
  96.7 15.2 %shard_map.382.q_ref.k_ref.v_ref.refs_1_.refs_2_.refs_3_ = bf16[1040,3072]{1,0:T(8,128)(2,1)} custom-call(bf16[1040,1024]{1,0:T(8,128)(2,1)} %fusion.6.x_ref, bf16[1024,3072]{1,0:T(8,128)(2,1)} %get-tuple-element.40.w_ref.refs_1_, f32[1,3072]{1,0:T(1,128)} %reshape_reshape.3.b_ref, f32[1040,128]{1,0:T(8,128)} %get-tuple-element.120.cos_ref.refs_9_, ...), custom_call_target="tpu_custom_call" | custom-call | flops 4000000000 | tf_op jit(solution)/shard_map/pallas_call | solution.py:589
  111.9 11.7 %shard_map.383 = (bf16[1040,1024]{1,0:T(8,128)(2,1)}, f32[1,8,1024]{2,1,0:T(8,128)}, f32[1,1,64]{2,1,0:T(1,128)}) custom-call(s32[4]{0:T(128)} %copy-done.28, bf16[1040,3072]{1,0:T(8,128)(2,1)} %shard_map.382.q_ref.k_ref.v_ref.refs_1_.refs_2_.refs_3_, bf16[1040,3072]{1,0:T(8,128)(2,1)} %shard_map.382.q_ref.k_ref.v_ref.refs_1_.refs_2_.refs_3_, ...), custom_call_target="tpu_custom_call" | custom-call | flops 6400000000 | tf_op jit(solution)/shard_map/pallas_call | solution.py:370
  127.2 11.8 %shard_map.384 = (bf16[1040,1024]{1,0:T(8,128)(2,1)}, f32[1,8,1024]{2,1,0:T(8,128)}, f32[1,1,64]{2,1,0:T(1,128)}) custom-call(s32[4]{0:T(128)} %copy-done.28, bf16[1040,3072]{1,0:T(8,128)(2,1)} %shard_map.382.q_ref.k_ref.v_ref.refs_1_.refs_2_.refs_3_, ...), custom_call_target="tpu_custom_call", output_to_operand_aliasing={{0}: (5, {})} | custom-call | flops 6400000000 | tf_op jit(solution)/shard_map/pallas_call | solution.py:370
  148.5 3.0 collective-permute-start.15
  151.5 4.8 %fusion.38 = (f32[1040]{0:T(1024)S(1)}, f32[1040,1024]{1,0:T(8,128)S(1)}) fusion(f32[1024]{0:T(1024)S(1)} %add.197, bf16[1040,1024]{1,0:T(8,128)(2,1)S(1)} %copy-done, bf16[1024,1024]{1,0:T(8,128)(2,1)} %all-gather.3.cloned.1.call-done, bf16[1040,1024]{1,0:T(8,128)(2,1)} %get-tuple-element.38.x_ref), kind=kOutput, calls=%fused_computation.150 | convolution fusion | flops 2185296896 | bytes 10625088 | tf_op jit(solution)/shard_map/dot_general | solution.py:1160
  160.4 6.6 %all-gather.5.cloned.1.call-done.up_ref = bf16[1024,4096]{1,0:T(8,128)(2,1)} async-done(((bf16[32,4096]{1,0:T(8,128)(2,1)}), bf16[1024,4096]{1,0:T(8,128)(2,1)}) %all-gather.5.cloned.1.call-update) | async-done | bytes 8388624 | tf_op jit(solution)/shard_map/all_gather | solution.py:1115
  167.0 79.3 %shard_map.395 = (bf16[1040,1024]{1,0:T(8,128)(2,1)}, f32[1040,1024]{1,0:T(8,128)}, f32[1,4096]{1,0:T(1,128)}, bf16[16,32,8192]{2,1,0:T(8,128)(2,1)}, bf16[16,32,8192]{2,1,0:T(8,128)(2,1)}) custom-call(s32[1]{0:T(128)} %bitcast.me_ref, bf16[1040,1024]{1,0:T(8,128)(2,1)} %add_convert_fusion.x_ref, bf16[1040,1024]{1,0:T(8,128)(2,1)} %get-tuple-element.43.g_ref, ...), custom_call_target="tpu_custom_call" | custom-call | flops 20000000000 | tf_op jit(solution)/shard_map/pallas_call | solution.py:821
  246.6 5.3 %multiply_reduce_fusion = (bf16[1024]{0:T(1024)(128)(2,1)S(1)}, f32[1040]{0:T(1024)S(1)}, f32[1040]{0:T(1024)S(1)}, bf16[1024]{0:T(1024)(128)(2,1)S(1)}) fusion(f32[1040,1024]{1,0:T(8,128)} %get-tuple-element.45, f32[1040,1024]{1,0:T(8,128)} %copy-done.1, f32[1040]{0:T(1024)S(1)} %add_rsqrt_fusion, f32[1040]{0:T(1024)S(1)} %broadcast_multiply_fusion.2, ...), kind=kLoop, calls=%fused_computation.11 | loop fusion | flops 9580512 | bytes 8544512 | tf_op jit(solution)/shard_map/reduce_sum | solution.py:1177
  252.6 3.3 convert_reduce_fusion.1
  255.8 3.7 convolution_convert_fusion.refs_2_.refs_0_
  259.8 10.3 %add_convert_fusion.1 = (bf16[4,32,8192]{2,1,0:T(8,128)(2,1)}, bf16[4,32,8192]{2,1,0:T(8,128)(2,1)}, bf16[4,32,8192]{2,1,0:T(8,128)(2,1)}, bf16[4,32,8192]{2,1,0:T(8,128)(2,1)}) fusion(bf16[16,32,8192]{2,1,0:T(8,128)(2,1)} %collective-permute-done.22.refs_1_, bf16[16,32,8192]{2,1,0:T(8,128)(2,1)} %shard_map.396), kind=kLoop, calls=%fused_computation.17 | loop fusion | flops 16777216 | bytes 25165824 | tf_op jit(solution)/shard_map/convert_element_type | solution.py:98
  271.8 19.4 %shard_map.398.refs_12_ = bf16[3,1040,1024]{2,1,0:T(8,128)(2,1)} custom-call(s32[4]{0:T(128)} %copy-done.28, bf16[1040,3072]{1,0:T(8,128)(2,1)} %shard_map.382.q_ref.k_ref.v_ref.refs_1_.refs_2_.refs_3_, bf16[1040,3072]{1,0:T(8,128)(2,1)} %shard_map.382.q_ref.k_ref.v_ref.refs_1_.refs_2_.refs_3_, ...), custom_call_target="tpu_custom_call" | custom-call | flops 7600000000 | tf_op jit(solution)/shard_map/pallas_call | solution.py:518
  291.2 19.8 %shard_map.399.refs_3_.refs_0_ = bf16[3,1040,1024]{2,1,0:T(8,128)(2,1)} custom-call(s32[4]{0:T(128)} %copy-done.28, bf16[1040,3072]{1,0:T(8,128)(2,1)} %shard_map.382.q_ref.k_ref.v_ref.refs_1_.refs_2_.refs_3_, bf16[1040,3072]{1,0:T(8,128)(2,1)} %shard_map.382.q_ref.k_ref.v_ref.refs_1_.refs_2_.refs_3_, ...), custom_call_target="tpu_custom_call", output_to_operand_aliasing={{}: (12, {})} | custom-call | flops 7600000000 | tf_op jit(solution)/shard_map/pallas_call | solution.py:518
  311.0 6.4 %collective-permute-done.24.refs_2_ = bf16[4,32,8192]{2,1,0:T(8,128)(2,1)S(1)} collective-permute-done((bf16[4,32,8192]{2,1,0:T(8,128)(2,1)}, bf16[4,32,8192]{2,1,0:T(8,128)(2,1)S(1)}, u32[]{:S(2)}, u32[]{:S(2)}) %collective-permute-start.24) | collective-permute-done | bytes 2097184 | tf_op jit(solution)/shard_map/ppermute | solution.py:41
  318.8 3.6 add_convert_fusion.9
  323.4 4.0 add_convert_fusion.11
  328.2 13.1 %shard_map.403 = (bf16[16,32,4096]{2,1,0:T(8,128)(2,1)}, bf16[16,32,4096]{2,1,0:T(8,128)(2,1)}) custom-call(s32[1]{0:T(128)} %bitcast.me_ref, bf16[1040,1024]{1,0:T(8,128)(2,1)} %fusion.6.x_ref, bf16[3,1040,1024]{2,1,0:T(8,128)(2,1)} %shard_map.402.g_ref.refs_0_), custom_call_target="tpu_custom_call" | custom-call | flops 3000000000 | tf_op jit(solution)/shard_map/pallas_call | solution.py:909
  341.3 6.7 %shard_map.404 = (bf16[16,32,4096]{2,1,0:T(8,128)(2,1)}, bf16[16,32,4096]{2,1,0:T(8,128)(2,1)}) custom-call(s32[1]{0:T(128)} %bitcast.me_ref, bf16[1040,1024]{1,0:T(8,128)(2,1)} %get-tuple-element.42.refs_1_.o_ref.refs_4_.x_ref, bf16[1040,1024]{1,0:T(8,128)(2,1)} %copy-done.10, ...), custom_call_target="tpu_custom_call", output_to_operand_aliasing={{0}: (3, {}), {1}: (4, {})} | custom-call | flops 1000000000 | tf_op jit(solution)/shard_map/pallas_call | solution.py:909
  362.5 5.2 %add_convert_fusion.5 = (bf16[4,32,4096]{2,1,0:T(8,128)(2,1)S(1)}, bf16[4,32,4096]{2,1,0:T(8,128)(2,1)}, bf16[4,32,4096]{2,1,0:T(8,128)(2,1)S(1)}, bf16[4,32,4096]{2,1,0:T(8,128)(2,1)}) fusion(bf16[16,32,4096]{2,1,0:T(8,128)(2,1)} %collective-permute-done.27, bf16[16,32,4096]{2,1,0:T(8,128)(2,1)} %shard_map.407), kind=kLoop, calls=%fused_computation.26 | loop fusion | flops 8388608 | bytes 12582912 | tf_op jit(solution)/shard_map/convert_element_type | solution.py:98
  369.0 18.9 %shard_map.409 = (f32[1032,1024]{1,0:T(8,128)}, f32[1,1024]{1,0:T(1,128)}, f32[1,1024]{1,0:T(1,128)}, f32[3,1,1024]{2,1,0:T(1,128)}) custom-call(bf16[3,1040,1024]{2,1,0:T(8,128)(2,1)} %shard_map.408.g_ref, bf16[1024,3072]{1,0:T(8,128)(2,1)} %get-tuple-element.40.w_ref.refs_1_, bf16[1040,1024]{1,0:T(8,128)(2,1)} %get-tuple-element.38.x_ref, ...), custom_call_target="tpu_custom_call" | custom-call | flops 5000000000 | tf_op jit(solution)/shard_map/pallas_call | solution.py:1027
  402.8 8.4 %collective-permute-done.33 = bf16[2,32,4352]{2,1,0:T(8,128)(2,1)S(1)} collective-permute-done((bf16[2,32,4352]{2,1,0:T(8,128)(2,1)S(1)}, bf16[2,32,4352]{2,1,0:T(8,128)(2,1)S(1)}, u32[]{:S(2)}, u32[]{:S(2)}) %collective-permute-start.33) | collective-permute-done | bytes 557088 | tf_op jit(solution)/shard_map/ppermute | solution.py:41
  418.9 3.6 shard_map.411.refs_1_
  422.4 12.0 %collective-permute-done.35 = bf16[32,4352]{1,0:T(8,128)(2,1)S(1)} collective-permute-done((bf16[32,4352]{1,0:T(8,128)(2,1)S(1)}, bf16[32,4352]{1,0:T(8,128)(2,1)S(1)}, u32[]{:S(2)}, u32[]{:S(2)}) %collective-permute-start.35) | collective-permute-done | bytes 278560 | tf_op jit(solution)/shard_map/ppermute | solution.py:41
  435.6 3.2 collective-permute-start.37
  (279 shorter events, 115.9 us)
Async XLA Ops:
  7.2 144.3 %all-gather.3.cloned.1.call-start = ((), (), s32[]{:S(2)}) async-start(), calls=%async_computation | async-start | bytes 2162688 | tf_op jit(solution)/shard_map/all_gather | solution.py:1114
  8.0 159.0 %all-gather.5.cloned.1.call-start = ((), (), s32[]{:S(2)}) async-start(), calls=%async_computation.1 | async-start | bytes 8650752 | tf_op jit(solution)/shard_map/all_gather | solution.py:1115
  11.1 20.2 %collective-permute-start.4 = (bf16[1,32,3328]{2,1,0:T(8,128)(2,1)S(1)}, bf16[1,32,3328]{2,1,0:T(8,128)(2,1)}, u32[]{:S(2)}, u32[]{:S(2)}) collective-permute-start(bf16[1,32,3328]{2,1,0:T(8,128)(2,1)S(1)} %fusion.20), channel_id=1, source_target_pairs={{0,6},{1,7},{2,4},{3,5},{4,2},{5,3},{6,0},{7,1},{8,14},{9,15},{10,... | collective-permute-start | bytes 638984 | tf_op jit(solution)/shard_map/ppermute | solution.py:41
  15.3 19.2 %collective-permute-start.3 = (bf16[1,32,3328]{2,1,0:T(8,128)(2,1)S(1)}, bf16[1,32,3328]{2,1,0:T(8,128)(2,1)}, u32[]{:S(2)}, u32[]{:S(2)}) collective-permute-start(bf16[1,32,3328]{2,1,0:T(8,128)(2,1)S(1)} %fusion.20), channel_id=1, source_target_pairs={{0,4},{1,5},{2,6},{3,7},{4,0},{5,1},{6,2},{7,3},{8,12},{9,13},{10,... | collective-permute-start | bytes 638984 | tf_op jit(solution)/shard_map/ppermute | solution.py:41
  15.3 21.5 %collective-permute-start = (bf16[1,32,3328]{2,1,0:T(8,128)(2,1)S(1)}, bf16[1,32,3328]{2,1,0:T(8,128)(2,1)}, u32[]{:S(2)}, u32[]{:S(2)}) collective-permute-start(bf16[1,32,3328]{2,1,0:T(8,128)(2,1)S(1)} %fusion.20), channel_id=1, source_target_pairs={{0,2},{1,3},{2,0},{3,1},{4,6},{5,7},{6,4},{7,5},{8,10},{9,11},{10,... | collective-permute-start | bytes 638984 | tf_op jit(solution)/shard_map/ppermute | solution.py:41
  37.8 12.4 %collective-permute-start.1 = (bf16[2,32,3328]{2,1,0:T(8,128)(2,1)S(1)}, bf16[2,32,3328]{2,1,0:T(8,128)(2,1)S(1)}, u32[]{:S(2)}, u32[]{:S(2)}) collective-permute-start(bf16[2,32,3328]{2,1,0:T(8,128)(2,1)S(1)} %pad_maximum_fusion.9), channel_id=1, source_target_pairs={{0,1},{1,0},{2,3},{3,2},{4,5},{5,4},{6,7},{7,6},{8,9},{9,8},{10,11... | collective-permute-start | bytes 1277960 | tf_op jit(solution)/shard_map/ppermute | solution.py:41
  47.4 29.8 %collective-permute-start.6 = (bf16[4,32,3328]{2,1,0:T(8,128)(2,1)}, bf16[4,32,3328]{2,1,0:T(8,128)(2,1)}, u32[]{:S(2)}, u32[]{:S(2)}) collective-permute-start(bf16[4,32,3328]{2,1,0:T(8,128)(2,1)} %constant_dynamic-update-slice_fusion.refs_2_), channel_id=1, source_target_pairs={{0,1},{1,0},{2,3},{3,2},{4,5},{5,4},{6,7},{7,6},{8,9},{9,8},{10,11... | collective-permute-start | bytes 2555912 | tf_op jit(solution)/shard_map/ppermute | solution.py:41
  52.2 25.0 %collective-permute-start.2 = (bf16[4,32,3328]{2,1,0:T(8,128)(2,1)}, bf16[4,32,3328]{2,1,0:T(8,128)(2,1)}, u32[]{:S(2)}, u32[]{:S(2)}) collective-permute-start(bf16[4,32,3328]{2,1,0:T(8,128)(2,1)} %pad_maximum_fusion.2.refs_0_.refs_1_), channel_id=1, source_target_pairs={{0,16},{1,17},{2,18},{3,19},{4,20},{5,21},{6,22},{7,23},{8,24},{9,... | collective-permute-start | bytes 2555912 | tf_op jit(solution)/shard_map/ppermute | solution.py:41
  54.4 21.7 %collective-permute-start.11 = (bf16[1,32,4096]{2,1,0:T(8,128)(2,1)}, bf16[1,32,4096]{2,1,0:T(8,128)(2,1)S(1)}, u32[]{:S(2)}, u32[]{:S(2)}) collective-permute-start(bf16[1,32,4096]{2,1,0:T(8,128)(2,1)} %bitcast.89), channel_id=1, source_target_pairs={{0,2},{1,3},{2,0},{3,1},{4,6},{5,7},{6,4},{7,5},{8,10},{9,11},{10,... | collective-permute-start | bytes 786440 | tf_op jit(solution)/shard_map/ppermute | solution.py:41
  55.4 23.1 %collective-permute-start.16 = (bf16[1,32,4096]{2,1,0:T(8,128)(2,1)S(1)}, bf16[1,32,4096]{2,1,0:T(8,128)(2,1)S(1)}, u32[]{:S(2)}, u32[]{:S(2)}) collective-permute-start(bf16[1,32,4096]{2,1,0:T(8,128)(2,1)S(1)} %bitcast.90), channel_id=1, source_target_pairs={{0,4},{1,5},{2,6},{3,7},{4,0},{5,1},{6,2},{7,3},{8,12},{9,13},{10,... | collective-permute-start | bytes 786440 | tf_op jit(solution)/shard_map/ppermute | solution.py:41
  60.3 19.1 %collective-permute-start.9 = (bf16[4,32,3328]{2,1,0:T(8,128)(2,1)}, bf16[4,32,3328]{2,1,0:T(8,128)(2,1)S(1)}, u32[]{:S(2)}, u32[]{:S(2)}) collective-permute-start(bf16[4,32,3328]{2,1,0:T(8,128)(2,1)} %constant_dynamic-update-slice_fusion.refs_2_), channel_id=1, source_target_pairs={{0,8},{1,9},{2,10},{3,11},{4,12},{5,13},{6,14},{7,15},{8,0},{9,1},... | collective-permute-start | bytes 2555912 | tf_op jit(solution)/shard_map/ppermute | solution.py:41
  87.7 38.7 %collective-permute-start.13 = (bf16[2,32,4096]{2,1,0:T(8,128)(2,1)}, bf16[2,32,4096]{2,1,0:T(8,128)(2,1)S(1)}, u32[]{:S(2)}, u32[]{:S(2)}) collective-permute-start(bf16[2,32,4096]{2,1,0:T(8,128)(2,1)} %shard_map.387), channel_id=1, source_target_pairs={{0,16},{1,17},{2,18},{3,19},{4,20},{5,21},{6,22},{7,23},{8,24},{9,... | collective-permute-start | bytes 1572872 | tf_op jit(solution)/shard_map/ppermute | solution.py:41
  88.7 34.9 %collective-permute-start.12 = (bf16[2,32,4096]{2,1,0:T(8,128)(2,1)}, bf16[2,32,4096]{2,1,0:T(8,128)(2,1)}, u32[]{:S(2)}, u32[]{:S(2)}) collective-permute-start(bf16[2,32,4096]{2,1,0:T(8,128)(2,1)} %shard_map.387), channel_id=1, source_target_pairs={{0,1},{1,0},{2,3},{3,2},{4,5},{5,4},{6,7},{7,6},{8,9},{9,8},{10,11... | collective-permute-start | bytes 1572872 | tf_op jit(solution)/shard_map/ppermute | solution.py:41
  91.4 35.0 %collective-permute-start.19 = (bf16[2,32,4096]{2,1,0:T(8,128)(2,1)}, bf16[2,32,4096]{2,1,0:T(8,128)(2,1)}, u32[]{:S(2)}, u32[]{:S(2)}) collective-permute-start(bf16[2,32,4096]{2,1,0:T(8,128)(2,1)} %shard_map.391), channel_id=1, source_target_pairs={{0,1},{1,0},{2,3},{3,2},{4,5},{5,4},{6,7},{7,6},{8,9},{9,8},{10,11... | collective-permute-start | bytes 1572872 | tf_op jit(solution)/shard_map/ppermute | solution.py:41
  91.4 32.4 %collective-permute-start.18 = (bf16[2,32,4096]{2,1,0:T(8,128)(2,1)}, bf16[2,32,4096]{2,1,0:T(8,128)(2,1)}, u32[]{:S(2)}, u32[]{:S(2)}) collective-permute-start(bf16[2,32,4096]{2,1,0:T(8,128)(2,1)} %shard_map.391), channel_id=1, source_target_pairs={{0,16},{1,17},{2,18},{3,19},{4,20},{5,21},{6,22},{7,23},{8,24},{9,... | collective-permute-start | bytes 1572872 | tf_op jit(solution)/shard_map/ppermute | solution.py:41
  123.6 21.1 %collective-permute-start.14 = (bf16[2,32,4096]{2,1,0:T(8,128)(2,1)}, bf16[2,32,4096]{2,1,0:T(8,128)(2,1)S(1)}, u32[]{:S(2)}, u32[]{:S(2)}) collective-permute-start(bf16[2,32,4096]{2,1,0:T(8,128)(2,1)} %shard_map.388), channel_id=1, source_target_pairs={{0,16},{1,17},{2,18},{3,19},{4,20},{5,21},{6,22},{7,23},{8,24},{9,... | collective-permute-start | bytes 1572872 | tf_op jit(solution)/shard_map/ppermute | solution.py:41
  123.8 18.1 %collective-permute-start.20 = (bf16[2,32,4096]{2,1,0:T(8,128)(2,1)}, bf16[2,32,4096]{2,1,0:T(8,128)(2,1)S(1)}, u32[]{:S(2)}, u32[]{:S(2)}) collective-permute-start(bf16[2,32,4096]{2,1,0:T(8,128)(2,1)} %shard_map.392), channel_id=1, source_target_pairs={{0,1},{1,0},{2,3},{3,2},{4,5},{5,4},{6,7},{7,6},{8,9},{9,8},{10,11... | collective-permute-start | bytes 1572872 | tf_op jit(solution)/shard_map/ppermute | solution.py:41
  148.5 11.8 %collective-permute-start.15 = (bf16[8,32,4096]{2,1,0:T(8,128)(2,1)}, bf16[8,32,4096]{2,1,0:T(8,128)(2,1)}, u32[]{:S(2)}, u32[]{:S(2)}) collective-permute-start(bf16[8,32,4096]{2,1,0:T(8,128)(2,1)} %shard_map.390.refs_0_), channel_id=1, source_target_pairs={{0,8},{1,9},{2,10},{3,11},{4,12},{5,13},{6,14},{7,15},{8,0},{9,1},... | collective-permute-start | bytes 6291464 | tf_op jit(solution)/shard_map/ppermute | solution.py:41
  246.2 13.6 %collective-permute-start.22 = (bf16[16,32,8192]{2,1,0:T(8,128)(2,1)}, bf16[16,32,8192]{2,1,0:T(8,128)(2,1)}, u32[]{:S(2)}, u32[]{:S(2)}) collective-permute-start(bf16[16,32,8192]{2,1,0:T(8,128)(2,1)} %get-tuple-element.47), channel_id=1, source_target_pairs={{0,8},{1,9},{2,10},{3,11},{4,12},{5,13},{6,14},{7,15},{8,0},{9,1},... | collective-permute-start | bytes 25165832 | tf_op jit(solution)/shard_map/ppermute | solution.py:41
  270.1 47.4 %collective-permute-start.24 = (bf16[4,32,8192]{2,1,0:T(8,128)(2,1)}, bf16[4,32,8192]{2,1,0:T(8,128)(2,1)S(1)}, u32[]{:S(2)}, u32[]{:S(2)}) collective-permute-start(bf16[4,32,8192]{2,1,0:T(8,128)(2,1)} %get-tuple-element.74.refs_4_), channel_id=1, source_target_pairs={{0,1},{1,0},{2,3},{3,2},{4,5},{5,4},{6,7},{7,6},{8,9},{9,8},{10,11... | collective-permute-start | bytes 6291464 | tf_op jit(solution)/shard_map/ppermute | solution.py:41
  271.0 47.0 %collective-permute-start.23 = (bf16[4,32,8192]{2,1,0:T(8,128)(2,1)}, bf16[4,32,8192]{2,1,0:T(8,128)(2,1)}, u32[]{:S(2)}, u32[]{:S(2)}) collective-permute-start(bf16[4,32,8192]{2,1,0:T(8,128)(2,1)} %get-tuple-element.76.refs_2_), channel_id=1, source_target_pairs={{0,16},{1,17},{2,18},{3,19},{4,20},{5,21},{6,22},{7,23},{8,24},{9,... | collective-permute-start | bytes 6291464 | tf_op jit(solution)/shard_map/ppermute | solution.py:41
  322.4 29.2 %collective-permute-start.26 = (bf16[2,32,8192]{2,1,0:T(8,128)(2,1)S(1)}, bf16[2,32,8192]{2,1,0:T(8,128)(2,1)S(1)}, u32[]{:S(2)}, u32[]{:S(2)}) collective-permute-start(bf16[2,32,8192]{2,1,0:T(8,128)(2,1)S(1)} %get-tuple-element.82.refs_4_), channel_id=1, source_target_pairs={{0,16},{1,17},{2,18},{3,19},{4,20},{5,21},{6,22},{7,23},{8,24},{9,... | collective-permute-start | bytes 3145736 | tf_op jit(solution)/shard_map/ppermute | solution.py:41
  327.4 24.3 %collective-permute-start.25 = (bf16[2,32,8192]{2,1,0:T(8,128)(2,1)}, bf16[2,32,8192]{2,1,0:T(8,128)(2,1)S(1)}, u32[]{:S(2)}, u32[]{:S(2)}) collective-permute-start(bf16[2,32,8192]{2,1,0:T(8,128)(2,1)} %get-tuple-element.84.refs_2_), channel_id=1, source_target_pairs={{0,1},{1,0},{2,3},{3,2},{4,5},{5,4},{6,7},{7,6},{8,9},{9,8},{10,11... | collective-permute-start | bytes 3145736 | tf_op jit(solution)/shard_map/ppermute | solution.py:41
  348.0 14.5 %collective-permute-start.27 = (bf16[16,32,4096]{2,1,0:T(8,128)(2,1)}, bf16[16,32,4096]{2,1,0:T(8,128)(2,1)}, u32[]{:S(2)}, u32[]{:S(2)}) collective-permute-start(bf16[16,32,4096]{2,1,0:T(8,128)(2,1)} %get-tuple-element.55), channel_id=1, source_target_pairs={{0,8},{1,9},{2,10},{3,11},{4,12},{5,13},{6,14},{7,15},{8,0},{9,1},... | collective-permute-start | bytes 12582920 | tf_op jit(solution)/shard_map/ppermute | solution.py:41
  356.4 58.3 %collective-permute-start.40 = (bf16[32,8192]{1,0:T(8,128)(2,1)}, bf16[32,8192]{1,0:T(8,128)(2,1)}, u32[]{:S(2)}, u32[]{:S(2)}) collective-permute-start(bf16[32,8192]{1,0:T(8,128)(2,1)} %get-tuple-element.92.refs_3_), channel_id=1, source_target_pairs={{0,6},{1,7},{2,4},{3,5},{4,2},{5,3},{6,0},{7,1},{8,14},{9,15},{10,... | collective-permute-start | bytes 1572872 | tf_op jit(solution)/shard_map/ppermute | solution.py:41
  357.1 59.8 %collective-permute-start.39 = (bf16[32,8192]{1,0:T(8,128)(2,1)}, bf16[32,8192]{1,0:T(8,128)(2,1)}, u32[]{:S(2)}, u32[]{:S(2)}) collective-permute-start(bf16[32,8192]{1,0:T(8,128)(2,1)} %get-tuple-element.93.refs_2_), channel_id=1, source_target_pairs={{0,4},{1,5},{2,6},{3,7},{4,0},{5,1},{6,2},{7,3},{8,12},{9,13},{10,... | collective-permute-start | bytes 1572872 | tf_op jit(solution)/shard_map/ppermute | solution.py:41
  360.6 56.3 %collective-permute-start.38 = (bf16[32,8192]{1,0:T(8,128)(2,1)}, bf16[32,8192]{1,0:T(8,128)(2,1)}, u32[]{:S(2)}, u32[]{:S(2)}) collective-permute-start(bf16[32,8192]{1,0:T(8,128)(2,1)} %get-tuple-element.91.refs_1_), channel_id=1, source_target_pairs={{0,2},{1,3},{2,0},{3,1},{4,6},{5,7},{6,4},{7,5},{8,10},{9,11},{10,... | collective-permute-start | bytes 1572872 | tf_op jit(solution)/shard_map/ppermute | solution.py:41
  367.7 26.7 %collective-permute-start.31 = (bf16[4,32,4096]{2,1,0:T(8,128)(2,1)S(1)}, bf16[4,32,4096]{2,1,0:T(8,128)(2,1)}, u32[]{:S(2)}, u32[]{:S(2)}) collective-permute-start(bf16[4,32,4096]{2,1,0:T(8,128)(2,1)S(1)} %get-tuple-element.78.refs_4_), channel_id=1, source_target_pairs={{0,1},{1,0},{2,3},{3,2},{4,5},{5,4},{6,7},{7,6},{8,9},{9,8},{10,11... | collective-permute-start | bytes 3145736 | tf_op jit(solution)/shard_map/ppermute | solution.py:41
  368.2 30.8 %collective-permute-start.28 = (bf16[4,32,4096]{2,1,0:T(8,128)(2,1)S(1)}, bf16[4,32,4096]{2,1,0:T(8,128)(2,1)}, u32[]{:S(2)}, u32[]{:S(2)}) collective-permute-start(bf16[4,32,4096]{2,1,0:T(8,128)(2,1)S(1)} %get-tuple-element.80.refs_2_), channel_id=1, source_target_pairs={{0,16},{1,17},{2,18},{3,19},{4,20},{5,21},{6,22},{7,23},{8,24},{9,... | collective-permute-start | bytes 3145736 | tf_op jit(solution)/shard_map/ppermute | solution.py:41
  399.0 12.2 %collective-permute-start.33 = (bf16[2,32,4352]{2,1,0:T(8,128)(2,1)S(1)}, bf16[2,32,4352]{2,1,0:T(8,128)(2,1)S(1)}, u32[]{:S(2)}, u32[]{:S(2)}) collective-permute-start(bf16[2,32,4352]{2,1,0:T(8,128)(2,1)S(1)} %get-tuple-element.87), channel_id=1, source_target_pairs={{0,16},{1,17},{2,18},{3,19},{4,20},{5,21},{6,22},{7,23},{8,24},{9,... | collective-permute-start | bytes 1671176 | tf_op jit(solution)/shard_map/ppermute | solution.py:41
  413.6 20.8 %collective-permute-start.35 = (bf16[32,4352]{1,0:T(8,128)(2,1)S(1)}, bf16[32,4352]{1,0:T(8,128)(2,1)S(1)}, u32[]{:S(2)}, u32[]{:S(2)}) collective-permute-start(bf16[32,4352]{1,0:T(8,128)(2,1)S(1)} %get-tuple-element.97.refs_2_), channel_id=1, source_target_pairs={{0,4},{1,5},{2,6},{3,7},{4,0},{5,1},{6,2},{7,3},{8,12},{9,13},{10,... | collective-permute-start | bytes 835592 | tf_op jit(solution)/shard_map/ppermute | solution.py:41
  415.6 18.8 %collective-permute-start.34 = (bf16[32,4352]{1,0:T(8,128)(2,1)S(1)}, bf16[32,4352]{1,0:T(8,128)(2,1)S(1)}, u32[]{:S(2)}, u32[]{:S(2)}) collective-permute-start(bf16[32,4352]{1,0:T(8,128)(2,1)S(1)} %copy-done.19), channel_id=1, source_target_pairs={{0,2},{1,3},{2,0},{3,1},{4,6},{5,7},{6,4},{7,5},{8,10},{9,11},{10,... | collective-permute-start | bytes 835592 | tf_op jit(solution)/shard_map/ppermute | solution.py:41
  (48 other events, 336.3 us)
Sparse Core Ops, SparseCore 0:
  11.0 66.1 all-gather.2
  80.2 86.6 all-gather.4

commit v6 on v5

--- a/solution.py
+++ b/solution.py
@@ -758,16 +758,14 @@
     def _():
         middle.wait()
 
-    sd[slot, low, :] = dot_tl(act[:, low], g_ref[...]).astype(bf16)
-    su[slot, :, low] = dot_n(xt[...], gup[:, low]).astype(bf16)
     a, g, total = curves(u1, g1)
     act[:, high] = a
     gup[:, high] = g
     gb_ref[:, high] = total
+    sd[slot] = dot_tl(act[...], g_ref[...]).astype(bf16)
+    su[slot] = dot_n(xt[...], gup[...]).astype(bf16)
     acc[...] += dot_n(act[...], wd[slot])
     gx_ref[...] += dot_t(gup[...], wu[slot])
-    sd[slot, high, :] = dot_tl(act[:, high], g_ref[...]).astype(bf16)
-    su[slot, :, high] = dot_n(xt[...], gup[:, high]).astype(bf16)
     at = pl.multiple_of(group(i) * cols, cols)
     for p in range(count):
         c, n = place(p, *where)
@@ -974,8 +972,20 @@
     )(x)
 
 
-def last_kernel(g_ref, w_ref, x_ref, mid_ref, gain_ref, out_ref, gain_out, bias_out, sum_ref, acc):
+def last_kernel(
+    g_ref, w_ref, x_any, mid_any, gain_ref, out_ref, sum_ref, acc, x_ref, mid_ref, sems
+):
     i = pl.program_id(0)
+    copies = [
+        pltpu.make_async_copy(x_any, x_ref, sems.at[0]),
+        pltpu.make_async_copy(mid_any, mid_ref, sems.at[1]),
+    ]
+
+    @pl.when(i == 0)
+    def _():
+        for copy in copies:
+            copy.start()
+
     g = g_ref[0]
     more = dot_t(g, w_ref[...])
 
@@ -987,10 +997,12 @@
     def _():
         acc[...] += more
 
-    sum_ref[0] = jnp.sum(g.astype(f32), axis=0, keepdims=True)
+    sum_ref[pl.ds(2 + i, 1), :] = jnp.sum(g.astype(f32), axis=0, keepdims=True)
 
     @pl.when(i == pl.num_programs(0) - 1)
     def _():
+        for copy in copies:
+            copy.wait()
         gain = gain_ref[...]
         gain_sum, bias_sum = 0.0, 0.0
         spans = [(f * PATCH, PATCH) for f in range(FRAMES)] + [(BODY, EXTRA)]
@@ -1013,8 +1025,8 @@
             else:
                 for f in range(FRAMES):
                     out_ref[f * FRAME_ROWS : f * FRAME_ROWS + 2, :] = found[2 * f : 2 * f + 2]
-        gain_out[...] = gain_sum
-        bias_out[...] = bias_sum
+        sum_ref[0:1, :] = gain_sum
+        sum_ref[1:2, :] = bias_sum
 
 
 def last_step(grad_mixed, w, x, middle, gain):
@@ -1030,23 +1042,24 @@
         in_specs=[
             pl.BlockSpec((1, rows, width), lambda i: (i, 0, 0)),
             pl.BlockSpec((width, width), lambda i: (0, i)),
-            pl.BlockSpec((rows, width), whole, pipeline_mode=once),
-            pl.BlockSpec((rows, width), whole, pipeline_mode=once),
+            pl.BlockSpec(memory_space=pl.ANY),
+            pl.BlockSpec(memory_space=pl.ANY),
             pl.BlockSpec((1, width), whole),
         ],
         out_specs=[
             pl.BlockSpec((FRAMES * FRAME_ROWS, width), whole, pipeline_mode=once),
-            pl.BlockSpec((1, width), whole),
-            pl.BlockSpec((1, width), whole),
-            pl.BlockSpec((1, 1, width), lambda i: (i, 0, 0)),
+            pl.BlockSpec((8, width), whole),
         ],
         out_shape=[
             jax.ShapeDtypeStruct((FRAMES * FRAME_ROWS, width), f32),
-            jax.ShapeDtypeStruct((1, width), f32),
-            jax.ShapeDtypeStruct((1, width), f32),
-            jax.ShapeDtypeStruct((parts, 1, width), f32),
+            jax.ShapeDtypeStruct((8, width), f32),
         ],
-        scratch_shapes=[pltpu.VMEM((rows, width), f32)],
+        scratch_shapes=[
+            pltpu.VMEM((rows, width), f32),
+            pltpu.VMEM((rows, width), bf16),
+            pltpu.VMEM((rows, width), f32),
+            pltpu.SemaphoreType.DMA((2,)),
+        ],
         compiler_params=pltpu.CompilerParams(vmem_limit_bytes=vmem_most),
         cost_estimate=cost(5),
     )(grad_mixed, w, x, middle, gain)
@@ -1180,7 +1193,7 @@
     grad_branch = grad_middle.astype(bf16)
     grad_b_out_local = jnp.sum(grad_branch.astype(f32), axis=0)
     grad_attended = dot_t(grad_branch, out_matrix).astype(bf16)
-    feed_own = after(feed_own, feed_taken, grad_attended)
+    feed_own = after(feed_own, grad_attended)
     feed_sums = reduce_start(feed_own, feed_taken, orders, sizes)
     grad_attended = after(grad_attended, *[v for group in feed_sums for v in group[:1] + group[2:]])
     feed_sums = [group[:2] for group in feed_sums]
@@ -1207,18 +1220,13 @@
     going = [v for group in sums for v in group[:1] + group[2:]]
     sums = [group[:2] for group in sums]
     grad_mixed = after(grad_mixed, *going)
-    grad_tokens, grad_gain_one, grad_bias_one, grad_b_qkv_local = last_step(
+    grad_tokens, late_sums = last_step(
         grad_mixed, qkv_matrix, tokens_in, grad_middle, gain_one[None]
     )
     vectors = [
-        grad_gain_one[0],
-        grad_bias_one[0],
-        grad_b_qkv_local[:, 0],
-        grad_b_out_local,
-        grad_gain_two,
-        grad_bias_two,
+        late_sums[:5],
+        jnp.stack([grad_b_out_local, grad_gain_two, grad_bias_two, grad_b_down_local[0]]),
         grad_b_up_local[0],
-        grad_b_down_local[0],
     ]
     small_own, small_other = small_units(vectors, rows, where, me)
     small = jnp.concatenate([small_own, small_other], axis=2).astype(bf16)
@@ -1247,18 +1255,18 @@
     return (
         output,
         grad_tokens,
-        small[0],
-        small[1],
+        small[0][0],
+        small[0][1],
         sum_one[:, :third],
+        small[0][2:],
+        sum_one[:, third : third + width],
+        small[1][0],
+        small[1][1],
+        small[1][2],
+        feed_sum[:, :hidden],
         small[2],
-        sum_one[:, third : third + width],
-        small[3],
-        small[4],
-        small[5],
-        feed_sum[:, :hidden],
-        small[6],
         sum_down,
-        small[7],
+        small[1][3],
     )
 
 

time: 459 us -> 458 us (level)
  Pallas kernels: 211 us -> 181 us
  waiting for transfers between devices: 57.3 us -> 80.9 us
  starting transfers between devices: 53.1 us -> 61.8 us
    ppermute x41, waiting for transfers between devices: 49.3 us -> 67.7 us  [swap(): lax.ppermute(value, ('dp', 'fsdp'), [(i, i ^ mask) for i in range(count)])]
    pallas_call x2, Pallas kernels: 39.2 us -> 24 us  [attend_back(): pl.pallas_call(kernel, grid_spec=pltpu.PrefetchScalarGridSpec(num_scalar_...]
    pallas_call x2, Pallas kernels: 23.5 us -> 12.9 us  [attend(): pl.pallas_call(kernel, grid_spec=pltpu.PrefetchScalarGridSpec(num_scalar_...]
    ppermute x41, starting transfers between devices: 53 us -> 61.7 us  [swap(): lax.ppermute(value, ('dp', 'fsdp'), [(i, i ^ mask) for i in range(count)])]
    all_gather x1, waiting for transfers between devices: 6.63 us -> 11.9 us  [body(): up_matrix = lax.all_gather(w_up, ('dp', 'fsdp'), axis=0, tiled=True)]
    unnamed x81 -> x78, local copies, waits for them, and re-layouts: 16.2 us -> 14.9 us
  transfers between devices with their start and end apart: 43 -> 43, of which waited for: 16 -> 12; matrix products, arithmetic and copies ran while one was open for 20% -> 19% of each run, Pallas kernels for 29% -> 23%
where the time goes in v6:
time: 458 us; the launch traced here: 450 us
  Pallas kernels  181 us (40%)
  waiting for transfers between devices  80.9 us (18%)
  other arithmetic  69.5 us (15%)
  starting transfers between devices  61.8 us (13%)
  local copies, waits for them, and re-layouts  32.3 us (7%)
  between operations  15 us (3%)
  matrix products  8.6 us (2%)
    pallas_call x1, Pallas kernels, feed(): pl.pallas_call(functools.partial(feed_kernel, rels, (line, orders, core))...  77.8 us
    ppermute x41, waiting for transfers between devices, swap(): lax.ppermute(value, ('dp', 'fsdp'), [(i, i ^ mask) for i in range(count)])  67.7 us
    ppermute x41, starting transfers between devices, swap(): lax.ppermute(value, ('dp', 'fsdp'), [(i, i ^ mask) for i in range(count)])  61.7 us
    pallas_call x2, Pallas kernels, attend_back(): pl.pallas_call(kernel, grid_spec=pltpu.PrefetchScalarGridSpec(num_scalar_...  24 us
    convert_element_type x4, other arithmetic, reduce_step(): sent = (kept[half:].astype(f32) + taken[half:].astype(f32)).astype(kind)  22.8 us
    pallas_call x2, Pallas kernels, weight_grad(): pl.pallas_call(functools.partial(weight_kernel, where, left, count), grid...  19.7 us
    pallas_call x1, Pallas kernels, last_step(): pl.pallas_call(last_kernel, grid=(parts,), in_specs=[pl.BlockSpec((1, row...  16.9 us
    pallas_call x1, Pallas kernels, project(): pl.pallas_call(functools.partial(project_kernel, 1.0 / math.sqrt(HEAD)),...  15.3 us
  transfers between devices with their start and end apart: 43, of which 12 were waited for; matrix products, arithmetic and copies ran while one was open for 19% of the time, Pallas kernels for 23%

profile of v6, /device:TPU:1, one launch (start us, length us, event | category | flops | bytes accessed | tf_op | source)
XLA Modules:
  0.0 449.5 jit_solution(9944989775251764937)
XLA Ops:
  11.1 3.2 collective-permute-start.3
  22.7 5.5 %shard_map.380 = (bf16[1040,1024]{1,0:T(8,128)(2,1)}, bf16[1040,1024]{1,0:T(8,128)(2,1)}, f32[1,1024]{1,0:T(1,128)}) custom-call(bf16[1032,1024]{1,0:T(8,128)(2,1)} %x_ref.1, bf16[1032,1024]{1,0:T(8,128)(2,1)} %g_ref.1), custom_call_target="tpu_custom_call" | custom-call | flops 1000000000 | tf_op jit(solution)/shard_map/pallas_call | solution.py:942
  39.1 3.3 collective-permute-done.5
  48.3 8.1 %collective-permute-start.16 = (bf16[1,32,4096]{2,1,0:T(8,128)(2,1)}, bf16[1,32,4096]{2,1,0:T(8,128)(2,1)S(1)}, u32[]{:S(2)}, u32[]{:S(2)}) collective-permute-start(bf16[1,32,4096]{2,1,0:T(8,128)(2,1)} %bitcast.89), channel_id=1, source_target_pairs={{0,4},{1,5},{2,6},{3,7},{4,0},{5,1},{6,2},{7,3},{8,12},{9,13},{10,... | collective-permute-start | bytes 786440 | tf_op jit(solution)/shard_map/ppermute | solution.py:41
  59.6 12.8 %collective-permute-done.16 = bf16[1,32,4096]{2,1,0:T(8,128)(2,1)S(1)} collective-permute-done((bf16[1,32,4096]{2,1,0:T(8,128)(2,1)}, bf16[1,32,4096]{2,1,0:T(8,128)(2,1)S(1)}, u32[]{:S(2)}, u32[]{:S(2)}) %collective-permute-start.16) | collective-permute-done | bytes 262176 | tf_op jit(solution)/shard_map/ppermute | solution.py:41
  76.8 3.4 collective-permute-done.17
  82.0 5.8 %shard_map.381 = (bf16[1024,3072]{1,0:T(8,128)(2,1)}, bf16[1024,256]{1,0:T(8,128)(2,1)}) custom-call(s32[1]{0:T(128)} %bitcast.me_ref, bf16[4,32,3328]{2,1,0:T(8,128)(2,1)} %pad_maximum_fusion.2.refs_0_.refs_1_, bf16[4,32,3328]{2,1,0:T(8,128)(2,1)} %collective-permute-done.2.refs_1_, bf16[4,32,3328]{2,1,0:T(8,128)(2,1)} %constant_dynamic-update-slice_fusion.refs_2_, ...), custom_call_target="tpu_custom_call" | custom-call | flops 1500000000 | tf_op jit(solution)/shard_map/pallas_call | solution.py:170
  94.0 15.3 %shard_map.382.q_ref.k_ref.v_ref.refs_1_.refs_2_.refs_3_ = bf16[1040,3072]{1,0:T(8,128)(2,1)} custom-call(bf16[1040,1024]{1,0:T(8,128)(2,1)} %fusion.6.x_ref, bf16[1024,3072]{1,0:T(8,128)(2,1)} %get-tuple-element.38.w_ref.refs_1_, f32[1,3072]{1,0:T(1,128)} %reshape_reshape.3.b_ref, f32[1040,128]{1,0:T(8,128)} %get-tuple-element.116.cos_ref.refs_9_, ...), custom_call_target="tpu_custom_call" | custom-call | flops 4000000000 | tf_op jit(solution)/shard_map/pallas_call | solution.py:589
  109.3 6.4 %shard_map.383 = (bf16[1040,1024]{1,0:T(8,128)(2,1)}, f32[1,8,1024]{2,1,0:T(8,128)}, f32[1,1,64]{2,1,0:T(1,128)}) custom-call(s32[4]{0:T(128)} %copy-done.27, bf16[1040,3072]{1,0:T(8,128)(2,1)} %shard_map.382.q_ref.k_ref.v_ref.refs_1_.refs_2_.refs_3_, bf16[1040,3072]{1,0:T(8,128)(2,1)} %shard_map.382.q_ref.k_ref.v_ref.refs_1_.refs_2_.refs_3_, ...), custom_call_target="tpu_custom_call" | custom-call | flops 6400000000 | tf_op jit(solution)/shard_map/pallas_call | solution.py:370
  115.7 2.9 collective-permute-start.20
  118.6 3.6 collective-permute-start.14
  123.0 6.5 %shard_map.384 = (bf16[1040,1024]{1,0:T(8,128)(2,1)}, f32[1,8,1024]{2,1,0:T(8,128)}, f32[1,1,64]{2,1,0:T(1,128)}) custom-call(s32[4]{0:T(128)} %copy-done.27, bf16[1040,3072]{1,0:T(8,128)(2,1)} %shard_map.382.q_ref.k_ref.v_ref.refs_1_.refs_2_.refs_3_, ...), custom_call_target="tpu_custom_call", output_to_operand_aliasing={{0}: (5, {})} | custom-call | flops 6400000000 | tf_op jit(solution)/shard_map/pallas_call | solution.py:370
  135.1 10.1 %collective-permute-start.21 = (bf16[8,32,4096]{2,1,0:T(8,128)(2,1)}, bf16[8,32,4096]{2,1,0:T(8,128)(2,1)}, u32[]{:S(2)}, u32[]{:S(2)}) collective-permute-start(bf16[8,32,4096]{2,1,0:T(8,128)(2,1)} %shard_map.394.refs_2_), channel_id=1, source_target_pairs={{0,8},{1,9},{2,10},{3,11},{4,12},{5,13},{6,14},{7,15},{8,0},{9,1},... | collective-permute-start | bytes 6291464 | tf_op jit(solution)/shard_map/ppermute | solution.py:41
  149.7 4.9 %fusion.39 = (f32[1040]{0:T(1024)S(1)}, f32[1040,1024]{1,0:T(8,128)S(1)}) fusion(f32[1024]{0:T(1024)S(1)} %add.197, bf16[1040,1024]{1,0:T(8,128)(2,1)S(1)} %copy-done, bf16[1024,1024]{1,0:T(8,128)(2,1)} %all-gather.3.cloned.1.call-done, bf16[1040,1024]{1,0:T(8,128)(2,1)} %get-tuple-element.36.x_any), kind=kOutput, calls=%fused_computation.152 | convolution fusion | flops 2185296896 | bytes 10625088 | tf_op jit(solution)/shard_map/dot_general | solution.py:1173
  158.5 11.9 %all-gather.5.cloned.1.call-done.up_ref = bf16[1024,4096]{1,0:T(8,128)(2,1)} async-done(((bf16[32,4096]{1,0:T(8,128)(2,1)}), bf16[1024,4096]{1,0:T(8,128)(2,1)}) %all-gather.5.cloned.1.call-update) | async-done | bytes 8388624 | tf_op jit(solution)/shard_map/all_gather | solution.py:1128
  170.4 77.8 %shard_map.395 = (bf16[1040,1024]{1,0:T(8,128)(2,1)}, f32[1040,1024]{1,0:T(8,128)}, f32[1,4096]{1,0:T(1,128)}, bf16[16,32,8192]{2,1,0:T(8,128)(2,1)}, bf16[16,32,8192]{2,1,0:T(8,128)(2,1)}) custom-call(s32[1]{0:T(128)} %bitcast.me_ref, bf16[1040,1024]{1,0:T(8,128)(2,1)} %add_convert_fusion.x_ref, bf16[1040,1024]{1,0:T(8,128)(2,1)} %get-tuple-element.41.g_ref, ...), custom_call_target="tpu_custom_call" | custom-call | flops 20000000000 | tf_op jit(solution)/shard_map/pallas_call | solution.py:819
  248.5 5.3 %multiply_reduce_fusion = (bf16[1024]{0:T(1024)(128)(2,1)S(1)}, f32[1040]{0:T(1024)S(1)}, f32[1040]{0:T(1024)S(1)}, bf16[1024]{0:T(1024)(128)(2,1)S(1)}) fusion(f32[1040,1024]{1,0:T(8,128)} %get-tuple-element.43, f32[1040,1024]{1,0:T(8,128)} %copy-done.1, f32[1040]{0:T(1024)S(1)} %add_rsqrt_fusion, f32[1040]{0:T(1024)S(1)} %broadcast_multiply_fusion.2, ...), kind=kLoop, calls=%fused_computation.11 | loop fusion | flops 9580512 | bytes 8544512 | tf_op jit(solution)/shard_map/reduce_sum | solution.py:1190
  254.5 3.2 convert_reduce_fusion.1
  257.7 3.7 convolution_convert_fusion.refs_1_.refs_0_
  261.8 10.3 %add_convert_fusion.1 = (bf16[4,32,8192]{2,1,0:T(8,128)(2,1)}, bf16[4,32,8192]{2,1,0:T(8,128)(2,1)}, bf16[4,32,8192]{2,1,0:T(8,128)(2,1)}, bf16[4,32,8192]{2,1,0:T(8,128)(2,1)}) fusion(bf16[16,32,8192]{2,1,0:T(8,128)(2,1)} %collective-permute-done.22, bf16[16,32,8192]{2,1,0:T(8,128)(2,1)} %shard_map.396), kind=kLoop, calls=%fused_computation.17 | loop fusion | flops 16777216 | bytes 25165824 | tf_op jit(solution)/shard_map/convert_element_type | solution.py:98
  273.5 10.6 %shard_map.398.refs_12_ = bf16[3,1040,1024]{2,1,0:T(8,128)(2,1)} custom-call(s32[4]{0:T(128)} %copy-done.27, bf16[1040,3072]{1,0:T(8,128)(2,1)} %shard_map.382.q_ref.k_ref.v_ref.refs_1_.refs_2_.refs_3_, bf16[1040,3072]{1,0:T(8,128)(2,1)} %shard_map.382.q_ref.k_ref.v_ref.refs_1_.refs_2_.refs_3_, ...), custom_call_target="tpu_custom_call" | custom-call | flops 7600000000 | tf_op jit(solution)/shard_map/pallas_call | solution.py:518
  284.1 13.4 %shard_map.399.refs_3_.refs_0_ = bf16[3,1040,1024]{2,1,0:T(8,128)(2,1)} custom-call(s32[4]{0:T(128)} %copy-done.27, bf16[1040,3072]{1,0:T(8,128)(2,1)} %shard_map.382.q_ref.k_ref.v_ref.refs_1_.refs_2_.refs_3_, bf16[1040,3072]{1,0:T(8,128)(2,1)} %shard_map.382.q_ref.k_ref.v_ref.refs_1_.refs_2_.refs_3_, ...), custom_call_target="tpu_custom_call", output_to_operand_aliasing={{}: (12, {})} | custom-call | flops 7600000000 | tf_op jit(solution)/shard_map/pallas_call | solution.py:518
  297.6 21.9 %collective-permute-done.23.refs_1_ = bf16[4,32,8192]{2,1,0:T(8,128)(2,1)S(1)} collective-permute-done((bf16[4,32,8192]{2,1,0:T(8,128)(2,1)}, bf16[4,32,8192]{2,1,0:T(8,128)(2,1)S(1)}, u32[]{:S(2)}, u32[]{:S(2)}) %collective-permute-start.23) | collective-permute-done | bytes 2097184 | tf_op jit(solution)/shard_map/ppermute | solution.py:41
  320.7 4.0 add_convert_fusion.9
  326.4 3.4 add_convert_fusion.11
  330.9 13.0 %shard_map.403 = (bf16[16,32,4096]{2,1,0:T(8,128)(2,1)}, bf16[16,32,4096]{2,1,0:T(8,128)(2,1)}) custom-call(s32[1]{0:T(128)} %bitcast.me_ref, bf16[1040,1024]{1,0:T(8,128)(2,1)} %fusion.6.x_ref, bf16[3,1040,1024]{2,1,0:T(8,128)(2,1)} %shard_map.402.g_ref.refs_0_), custom_call_target="tpu_custom_call" | custom-call | flops 3000000000 | tf_op jit(solution)/shard_map/pallas_call | solution.py:907
  344.0 6.7 %shard_map.404 = (bf16[16,32,4096]{2,1,0:T(8,128)(2,1)}, bf16[16,32,4096]{2,1,0:T(8,128)(2,1)}) custom-call(s32[1]{0:T(128)} %bitcast.me_ref, bf16[1040,1024]{1,0:T(8,128)(2,1)} %get-tuple-element.40.refs_1_.o_ref.refs_4_.x_ref, bf16[1040,1024]{1,0:T(8,128)(2,1)} %copy-done.11, ...), custom_call_target="tpu_custom_call", output_to_operand_aliasing={{0}: (3, {}), {1}: (4, {})} | custom-call | flops 1000000000 | tf_op jit(solution)/shard_map/pallas_call | solution.py:907
  364.9 5.2 %add_convert_fusion.5 = (bf16[4,32,4096]{2,1,0:T(8,128)(2,1)S(1)}, bf16[4,32,4096]{2,1,0:T(8,128)(2,1)}, bf16[4,32,4096]{2,1,0:T(8,128)(2,1)S(1)}, bf16[4,32,4096]{2,1,0:T(8,128)(2,1)}) fusion(bf16[16,32,4096]{2,1,0:T(8,128)(2,1)} %collective-permute-done.27, bf16[16,32,4096]{2,1,0:T(8,128)(2,1)} %shard_map.407), kind=kLoop, calls=%fused_computation.26 | loop fusion | flops 8388608 | bytes 12582912 | tf_op jit(solution)/shard_map/convert_element_type | solution.py:98
  371.6 16.9 %shard_map.409 = (f32[1032,1024]{1,0:T(8,128)}, f32[8,1024]{1,0:T(8,128)}) custom-call(bf16[3,1040,1024]{2,1,0:T(8,128)(2,1)} %shard_map.408.g_ref, bf16[1024,3072]{1,0:T(8,128)(2,1)} %get-tuple-element.38.w_ref.refs_1_, bf16[1040,1024]{1,0:T(8,128)(2,1)} %get-tuple-element.36.x_any, f32[1040,1024]{1,0:T(8,128)} %get-tuple-element.69.mid_any, ...), custom_call_target="tpu_custom_call" | custom-call | flops 5000000000 | tf_op jit(solution)/shard_map/pallas_call | solution.py:1039
  401.3 9.3 %collective-permute-done.33 = bf16[2,32,4352]{2,1,0:T(8,128)(2,1)S(1)} collective-permute-done((bf16[2,32,4352]{2,1,0:T(8,128)(2,1)S(1)}, bf16[2,32,4352]{2,1,0:T(8,128)(2,1)S(1)}, u32[]{:S(2)}, u32[]{:S(2)}) %collective-permute-start.33) | collective-permute-done | bytes 557088 | tf_op jit(solution)/shard_map/ppermute | solution.py:41
  417.6 3.6 shard_map.411.refs_1_
  421.2 10.4 %collective-permute-done.35 = bf16[32,4352]{1,0:T(8,128)(2,1)S(1)} collective-permute-done((bf16[32,4352]{1,0:T(8,128)(2,1)S(1)}, bf16[32,4352]{1,0:T(8,128)(2,1)S(1)}, u32[]{:S(2)}, u32[]{:S(2)}) %collective-permute-start.35) | collective-permute-done | bytes 278560 | tf_op jit(solution)/shard_map/ppermute | solution.py:41
  (274 shorter events, 112.3 us)
Async XLA Ops:
  7.2 141.9 %all-gather.3.cloned.1.call-start = ((), (), s32[]{:S(2)}) async-start(), calls=%async_computation | async-start | bytes 2162688 | tf_op jit(solution)/shard_map/all_gather | solution.py:1127
  8.0 162.4 %all-gather.5.cloned.1.call-start = ((), (), s32[]{:S(2)}) async-start(), calls=%async_computation.1 | async-start | bytes 8650752 | tf_op jit(solution)/shard_map/all_gather | solution.py:1128
  11.1 20.1 %collective-permute-start.3 = (bf16[1,32,3328]{2,1,0:T(8,128)(2,1)S(1)}, bf16[1,32,3328]{2,1,0:T(8,128)(2,1)}, u32[]{:S(2)}, u32[]{:S(2)}) collective-permute-start(bf16[1,32,3328]{2,1,0:T(8,128)(2,1)S(1)} %fusion.21), channel_id=1, source_target_pairs={{0,4},{1,5},{2,6},{3,7},{4,0},{5,1},{6,2},{7,3},{8,12},{9,13},{10,... | collective-permute-start | bytes 638984 | tf_op jit(solution)/shard_map/ppermute | solution.py:41
  14.3 16.9 %collective-permute-start.4 = (bf16[1,32,3328]{2,1,0:T(8,128)(2,1)S(1)}, bf16[1,32,3328]{2,1,0:T(8,128)(2,1)}, u32[]{:S(2)}, u32[]{:S(2)}) collective-permute-start(bf16[1,32,3328]{2,1,0:T(8,128)(2,1)S(1)} %fusion.21), channel_id=1, source_target_pairs={{0,6},{1,7},{2,4},{3,5},{4,2},{5,3},{6,0},{7,1},{8,14},{9,15},{10,... | collective-permute-start | bytes 638984 | tf_op jit(solution)/shard_map/ppermute | solution.py:41
  15.4 18.2 %collective-permute-start = (bf16[1,32,3328]{2,1,0:T(8,128)(2,1)S(1)}, bf16[1,32,3328]{2,1,0:T(8,128)(2,1)}, u32[]{:S(2)}, u32[]{:S(2)}) collective-permute-start(bf16[1,32,3328]{2,1,0:T(8,128)(2,1)S(1)} %fusion.21), channel_id=1, source_target_pairs={{0,2},{1,3},{2,0},{3,1},{4,6},{5,7},{6,4},{7,5},{8,10},{9,11},{10,... | collective-permute-start | bytes 638984 | tf_op jit(solution)/shard_map/ppermute | solution.py:41
  43.2 29.8 %collective-permute-start.6 = (bf16[4,32,3328]{2,1,0:T(8,128)(2,1)}, bf16[4,32,3328]{2,1,0:T(8,128)(2,1)}, u32[]{:S(2)}, u32[]{:S(2)}) collective-permute-start(bf16[4,32,3328]{2,1,0:T(8,128)(2,1)} %constant_dynamic-update-slice_fusion.refs_2_), channel_id=1, source_target_pairs={{0,1},{1,0},{2,3},{3,2},{4,5},{5,4},{6,7},{7,6},{8,9},{9,8},{10,11... | collective-permute-start | bytes 2555912 | tf_op jit(solution)/shard_map/ppermute | solution.py:41
  46.4 29.5 %collective-permute-start.2 = (bf16[4,32,3328]{2,1,0:T(8,128)(2,1)}, bf16[4,32,3328]{2,1,0:T(8,128)(2,1)}, u32[]{:S(2)}, u32[]{:S(2)}) collective-permute-start(bf16[4,32,3328]{2,1,0:T(8,128)(2,1)} %pad_maximum_fusion.2.refs_0_.refs_1_), channel_id=1, source_target_pairs={{0,16},{1,17},{2,18},{3,19},{4,20},{5,21},{6,22},{7,23},{8,24},{9,... | collective-permute-start | bytes 2555912 | tf_op jit(solution)/shard_map/ppermute | solution.py:41
  48.3 24.0 %collective-permute-start.16 = (bf16[1,32,4096]{2,1,0:T(8,128)(2,1)}, bf16[1,32,4096]{2,1,0:T(8,128)(2,1)S(1)}, u32[]{:S(2)}, u32[]{:S(2)}) collective-permute-start(bf16[1,32,4096]{2,1,0:T(8,128)(2,1)} %bitcast.89), channel_id=1, source_target_pairs={{0,4},{1,5},{2,6},{3,7},{4,0},{5,1},{6,2},{7,3},{8,12},{9,13},{10,... | collective-permute-start | bytes 786440 | tf_op jit(solution)/shard_map/ppermute | solution.py:41
  56.5 16.6 %collective-permute-start.11 = (bf16[1,32,4096]{2,1,0:T(8,128)(2,1)}, bf16[1,32,4096]{2,1,0:T(8,128)(2,1)S(1)}, u32[]{:S(2)}, u32[]{:S(2)}) collective-permute-start(bf16[1,32,4096]{2,1,0:T(8,128)(2,1)} %bitcast.90), channel_id=1, source_target_pairs={{0,2},{1,3},{2,0},{3,1},{4,6},{5,7},{6,4},{7,5},{8,10},{9,11},{10,... | collective-permute-start | bytes 786440 | tf_op jit(solution)/shard_map/ppermute | solution.py:41
  57.5 23.5 %collective-permute-start.9 = (bf16[4,32,3328]{2,1,0:T(8,128)(2,1)}, bf16[4,32,3328]{2,1,0:T(8,128)(2,1)S(1)}, u32[]{:S(2)}, u32[]{:S(2)}) collective-permute-start(bf16[4,32,3328]{2,1,0:T(8,128)(2,1)} %constant_dynamic-update-slice_fusion.refs_2_), channel_id=1, source_target_pairs={{0,8},{1,9},{2,10},{3,11},{4,12},{5,13},{6,14},{7,15},{8,0},{9,1},... | collective-permute-start | bytes 2555912 | tf_op jit(solution)/shard_map/ppermute | solution.py:41
  87.8 27.9 %collective-permute-start.18 = (bf16[2,32,4096]{2,1,0:T(8,128)(2,1)}, bf16[2,32,4096]{2,1,0:T(8,128)(2,1)}, u32[]{:S(2)}, u32[]{:S(2)}) collective-permute-start(bf16[2,32,4096]{2,1,0:T(8,128)(2,1)} %shard_map.391), channel_id=1, source_target_pairs={{0,16},{1,17},{2,18},{3,19},{4,20},{5,21},{6,22},{7,23},{8,24},{9,... | collective-permute-start | bytes 1572872 | tf_op jit(solution)/shard_map/ppermute | solution.py:41
  88.9 33.3 %collective-permute-start.19 = (bf16[2,32,4096]{2,1,0:T(8,128)(2,1)}, bf16[2,32,4096]{2,1,0:T(8,128)(2,1)S(1)}, u32[]{:S(2)}, u32[]{:S(2)}) collective-permute-start(bf16[2,32,4096]{2,1,0:T(8,128)(2,1)} %shard_map.391), channel_id=1, source_target_pairs={{0,1},{1,0},{2,3},{3,2},{4,5},{5,4},{6,7},{7,6},{8,9},{9,8},{10,11... | collective-permute-start | bytes 1572872 | tf_op jit(solution)/shard_map/ppermute | solution.py:41
  90.4 28.2 %collective-permute-start.12 = (bf16[2,32,4096]{2,1,0:T(8,128)(2,1)}, bf16[2,32,4096]{2,1,0:T(8,128)(2,1)}, u32[]{:S(2)}, u32[]{:S(2)}) collective-permute-start(bf16[2,32,4096]{2,1,0:T(8,128)(2,1)} %shard_map.387), channel_id=1, source_target_pairs={{0,1},{1,0},{2,3},{3,2},{4,5},{5,4},{6,7},{7,6},{8,9},{9,8},{10,11... | collective-permute-start | bytes 1572872 | tf_op jit(solution)/shard_map/ppermute | solution.py:41
  90.4 32.6 %collective-permute-start.13 = (bf16[2,32,4096]{2,1,0:T(8,128)(2,1)}, bf16[2,32,4096]{2,1,0:T(8,128)(2,1)}, u32[]{:S(2)}, u32[]{:S(2)}) collective-permute-start(bf16[2,32,4096]{2,1,0:T(8,128)(2,1)} %shard_map.387), channel_id=1, source_target_pairs={{0,16},{1,17},{2,18},{3,19},{4,20},{5,21},{6,22},{7,23},{8,24},{9,... | collective-permute-start | bytes 1572872 | tf_op jit(solution)/shard_map/ppermute | solution.py:41
  115.7 16.8 %collective-permute-start.20 = (bf16[2,32,4096]{2,1,0:T(8,128)(2,1)}, bf16[2,32,4096]{2,1,0:T(8,128)(2,1)S(1)}, u32[]{:S(2)}, u32[]{:S(2)}) collective-permute-start(bf16[2,32,4096]{2,1,0:T(8,128)(2,1)} %shard_map.392), channel_id=1, source_target_pairs={{0,1},{1,0},{2,3},{3,2},{4,5},{5,4},{6,7},{7,6},{8,9},{9,8},{10,11... | collective-permute-start | bytes 1572872 | tf_op jit(solution)/shard_map/ppermute | solution.py:41
  118.6 26.7 %collective-permute-start.14 = (bf16[2,32,4096]{2,1,0:T(8,128)(2,1)}, bf16[2,32,4096]{2,1,0:T(8,128)(2,1)S(1)}, u32[]{:S(2)}, u32[]{:S(2)}) collective-permute-start(bf16[2,32,4096]{2,1,0:T(8,128)(2,1)} %shard_map.388), channel_id=1, source_target_pairs={{0,16},{1,17},{2,18},{3,19},{4,20},{5,21},{6,22},{7,23},{8,24},{9,... | collective-permute-start | bytes 1572872 | tf_op jit(solution)/shard_map/ppermute | solution.py:41
  135.1 23.4 %collective-permute-start.21 = (bf16[8,32,4096]{2,1,0:T(8,128)(2,1)}, bf16[8,32,4096]{2,1,0:T(8,128)(2,1)}, u32[]{:S(2)}, u32[]{:S(2)}) collective-permute-start(bf16[8,32,4096]{2,1,0:T(8,128)(2,1)} %shard_map.394.refs_2_), channel_id=1, source_target_pairs={{0,8},{1,9},{2,10},{3,11},{4,12},{5,13},{6,14},{7,15},{8,0},{9,1},... | collective-permute-start | bytes 6291464 | tf_op jit(solution)/shard_map/ppermute | solution.py:41
  248.2 13.6 %collective-permute-start.22 = (bf16[16,32,8192]{2,1,0:T(8,128)(2,1)}, bf16[16,32,8192]{2,1,0:T(8,128)(2,1)}, u32[]{:S(2)}, u32[]{:S(2)}) collective-permute-start(bf16[16,32,8192]{2,1,0:T(8,128)(2,1)} %get-tuple-element.45), channel_id=1, source_target_pairs={{0,8},{1,9},{2,10},{3,11},{4,12},{5,13},{6,14},{7,15},{8,0},{9,1},... | collective-permute-start | bytes 25165832 | tf_op jit(solution)/shard_map/ppermute | solution.py:41
  272.0 47.4 %collective-permute-start.23 = (bf16[4,32,8192]{2,1,0:T(8,128)(2,1)}, bf16[4,32,8192]{2,1,0:T(8,128)(2,1)S(1)}, u32[]{:S(2)}, u32[]{:S(2)}) collective-permute-start(bf16[4,32,8192]{2,1,0:T(8,128)(2,1)} %get-tuple-element.72.refs_2_), channel_id=1, source_target_pairs={{0,16},{1,17},{2,18},{3,19},{4,20},{5,21},{6,22},{7,23},{8,24},{9,... | collective-permute-start | bytes 6291464 | tf_op jit(solution)/shard_map/ppermute | solution.py:41
  273.3 47.0 %collective-permute-start.24 = (bf16[4,32,8192]{2,1,0:T(8,128)(2,1)}, bf16[4,32,8192]{2,1,0:T(8,128)(2,1)}, u32[]{:S(2)}, u32[]{:S(2)}) collective-permute-start(bf16[4,32,8192]{2,1,0:T(8,128)(2,1)} %get-tuple-element.70.refs_4_), channel_id=1, source_target_pairs={{0,1},{1,0},{2,3},{3,2},{4,5},{5,4},{6,7},{7,6},{8,9},{9,8},{10,11... | collective-permute-start | bytes 6291464 | tf_op jit(solution)/shard_map/ppermute | solution.py:41
  324.8 29.5 %collective-permute-start.26 = (bf16[2,32,8192]{2,1,0:T(8,128)(2,1)}, bf16[2,32,8192]{2,1,0:T(8,128)(2,1)S(1)}, u32[]{:S(2)}, u32[]{:S(2)}) collective-permute-start(bf16[2,32,8192]{2,1,0:T(8,128)(2,1)} %get-tuple-element.78.refs_4_), channel_id=1, source_target_pairs={{0,16},{1,17},{2,18},{3,19},{4,20},{5,21},{6,22},{7,23},{8,24},{9,... | collective-permute-start | bytes 3145736 | tf_op jit(solution)/shard_map/ppermute | solution.py:41
  329.7 24.6 %collective-permute-start.25 = (bf16[2,32,8192]{2,1,0:T(8,128)(2,1)}, bf16[2,32,8192]{2,1,0:T(8,128)(2,1)S(1)}, u32[]{:S(2)}, u32[]{:S(2)}) collective-permute-start(bf16[2,32,8192]{2,1,0:T(8,128)(2,1)} %get-tuple-element.80.refs_2_), channel_id=1, source_target_pairs={{0,1},{1,0},{2,3},{3,2},{4,5},{5,4},{6,7},{7,6},{8,9},{9,8},{10,11... | collective-permute-start | bytes 3145736 | tf_op jit(solution)/shard_map/ppermute | solution.py:41
  350.6 14.2 %collective-permute-start.27 = (bf16[16,32,4096]{2,1,0:T(8,128)(2,1)}, bf16[16,32,4096]{2,1,0:T(8,128)(2,1)}, u32[]{:S(2)}, u32[]{:S(2)}) collective-permute-start(bf16[16,32,4096]{2,1,0:T(8,128)(2,1)} %get-tuple-element.53), channel_id=1, source_target_pairs={{0,8},{1,9},{2,10},{3,11},{4,12},{5,13},{6,14},{7,15},{8,0},{9,1},... | collective-permute-start | bytes 12582920 | tf_op jit(solution)/shard_map/ppermute | solution.py:41
  359.0 55.8 %collective-permute-start.39 = (bf16[32,8192]{1,0:T(8,128)(2,1)}, bf16[32,8192]{1,0:T(8,128)(2,1)}, u32[]{:S(2)}, u32[]{:S(2)}) collective-permute-start(bf16[32,8192]{1,0:T(8,128)(2,1)} %get-tuple-element.89.refs_2_), channel_id=1, source_target_pairs={{0,4},{1,5},{2,6},{3,7},{4,0},{5,1},{6,2},{7,3},{8,12},{9,13},{10,... | collective-permute-start | bytes 1572872 | tf_op jit(solution)/shard_map/ppermute | solution.py:41
  361.0 54.7 %collective-permute-start.40 = (bf16[32,8192]{1,0:T(8,128)(2,1)}, bf16[32,8192]{1,0:T(8,128)(2,1)}, u32[]{:S(2)}, u32[]{:S(2)}) collective-permute-start(bf16[32,8192]{1,0:T(8,128)(2,1)} %get-tuple-element.88.refs_3_), channel_id=1, source_target_pairs={{0,6},{1,7},{2,4},{3,5},{4,2},{5,3},{6,0},{7,1},{8,14},{9,15},{10,... | collective-permute-start | bytes 1572872 | tf_op jit(solution)/shard_map/ppermute | solution.py:41
  364.8 50.9 %collective-permute-start.38 = (bf16[32,8192]{1,0:T(8,128)(2,1)}, bf16[32,8192]{1,0:T(8,128)(2,1)}, u32[]{:S(2)}, u32[]{:S(2)}) collective-permute-start(bf16[32,8192]{1,0:T(8,128)(2,1)} %get-tuple-element.87.refs_1_), channel_id=1, source_target_pairs={{0,2},{1,3},{2,0},{3,1},{4,6},{5,7},{6,4},{7,5},{8,10},{9,11},{10,... | collective-permute-start | bytes 1572872 | tf_op jit(solution)/shard_map/ppermute | solution.py:41
  370.0 24.0 %collective-permute-start.31 = (bf16[4,32,4096]{2,1,0:T(8,128)(2,1)S(1)}, bf16[4,32,4096]{2,1,0:T(8,128)(2,1)}, u32[]{:S(2)}, u32[]{:S(2)}) collective-permute-start(bf16[4,32,4096]{2,1,0:T(8,128)(2,1)S(1)} %get-tuple-element.74.refs_4_), channel_id=1, source_target_pairs={{0,1},{1,0},{2,3},{3,2},{4,5},{5,4},{6,7},{7,6},{8,9},{9,8},{10,11... | collective-permute-start | bytes 3145736 | tf_op jit(solution)/shard_map/ppermute | solution.py:41
  370.4 27.6 %collective-permute-start.28 = (bf16[4,32,4096]{2,1,0:T(8,128)(2,1)S(1)}, bf16[4,32,4096]{2,1,0:T(8,128)(2,1)}, u32[]{:S(2)}, u32[]{:S(2)}) collective-permute-start(bf16[4,32,4096]{2,1,0:T(8,128)(2,1)S(1)} %get-tuple-element.76.refs_2_), channel_id=1, source_target_pairs={{0,16},{1,17},{2,18},{3,19},{4,20},{5,21},{6,22},{7,23},{8,24},{9,... | collective-permute-start | bytes 3145736 | tf_op jit(solution)/shard_map/ppermute | solution.py:41
  398.1 12.5 %collective-permute-start.33 = (bf16[2,32,4352]{2,1,0:T(8,128)(2,1)S(1)}, bf16[2,32,4352]{2,1,0:T(8,128)(2,1)S(1)}, u32[]{:S(2)}, u32[]{:S(2)}) collective-permute-start(bf16[2,32,4352]{2,1,0:T(8,128)(2,1)S(1)} %get-tuple-element.83), channel_id=1, source_target_pairs={{0,16},{1,17},{2,18},{3,19},{4,20},{5,21},{6,22},{7,23},{8,24},{9,... | collective-permute-start | bytes 1671176 | tf_op jit(solution)/shard_map/ppermute | solution.py:41
  410.7 20.8 %collective-permute-start.35 = (bf16[32,4352]{1,0:T(8,128)(2,1)S(1)}, bf16[32,4352]{1,0:T(8,128)(2,1)S(1)}, u32[]{:S(2)}, u32[]{:S(2)}) collective-permute-start(bf16[32,4352]{1,0:T(8,128)(2,1)S(1)} %get-tuple-element.93.refs_2_), channel_id=1, source_target_pairs={{0,4},{1,5},{2,6},{3,7},{4,0},{5,1},{6,2},{7,3},{8,12},{9,13},{10,... | collective-permute-start | bytes 835592 | tf_op jit(solution)/shard_map/ppermute | solution.py:41
  411.6 20.0 %collective-permute-start.36 = (bf16[32,4352]{1,0:T(8,128)(2,1)S(1)}, bf16[32,4352]{1,0:T(8,128)(2,1)S(1)}, u32[]{:S(2)}, u32[]{:S(2)}) collective-permute-start(bf16[32,4352]{1,0:T(8,128)(2,1)S(1)} %get-tuple-element.92.refs_3_), channel_id=1, source_target_pairs={{0,6},{1,7},{2,4},{3,5},{4,2},{5,3},{6,0},{7,1},{8,14},{9,15},{10,... | collective-permute-start | bytes 835592 | tf_op jit(solution)/shard_map/ppermute | solution.py:41
  415.7 17.4 %collective-permute-start.34 = (bf16[32,4352]{1,0:T(8,128)(2,1)S(1)}, bf16[32,4352]{1,0:T(8,128)(2,1)S(1)}, u32[]{:S(2)}, u32[]{:S(2)}) collective-permute-start(bf16[32,4352]{1,0:T(8,128)(2,1)S(1)} %copy-done.19), channel_id=1, source_target_pairs={{0,2},{1,3},{2,0},{3,1},{4,6},{5,7},{6,4},{7,5},{8,10},{9,11},{10,... | collective-permute-start | bytes 835592 | tf_op jit(solution)/shard_map/ppermute | solution.py:41
  (47 other events, 370.5 us)
Sparse Core Ops, SparseCore 0:
  11.0 68.1 all-gather.2
  82.2 88.1 all-gather.4
